TPU v7x, 256 devices: a whole 4x4x8 slice. The times are simulated.
256 devices in a mesh: batch: 8 (over y_lo, x), seq: 32 (over z, y_hi, core).
Axes of the slice: x: 4, y: 4 (y_hi: 2, y_lo: 2; y = y_hi * 2 + y_lo), z: 8, core: 2. Of those that a mesh axis runs over, the one named last changes fastest.
Arguments:
- inputs: bfloat16 [8, 65536, 512], P('batch', 'seq'), may hold values from -100 to 100
- dilated_tap_weight: bfloat16 [2, 3, 512, 256], replicated, may hold values from -0.15625 to 0.15625
- pointwise_weight: bfloat16 [2, 256, 512], replicated, may hold values from -0.375 to 0.375
- stream_norm_gain: float32 [2, 512], replicated, may hold values from 0.5 to 1.5
- stream_norm_bias: float32 [2, 512], replicated, may hold values from -3 to 3
- conv_norm_gain: float32 [2, 256], replicated, may hold values from 0.5 to 1.5
- conv_norm_bias: float32 [2, 256], replicated, may hold values from -3 to 3
Outputs:
- head_bins: float32 [8, 8, 64, 8192], P('batch', None, 'seq')
All inputs are finite; a program needn't handle non-finite values.
Results may differ from a plain program's by a relative error of at most 0.00095.
Values may be sent and summed in bfloat16 or wider, within the bound.
No kernel may reach another device: no remote copies, remote signals or barrier semaphores. Data moves between devices by JAX's collectives and lax.ppermute only.
A program may use at most 64 MiB of HBM per device.

v0:
```python
import jax
import jax.numpy as jnp
from jax import lax
from jax.sharding import PartitionSpec as P

HEADS = 8
POOL = 8


EPS = 1e-05


def padded(x, sides, width):
    for axis, dim in sides:
        peers, length = (lax.axis_size(axis), x.shape[dim])
        up = [(i, (i + 1) % peers) for i in range(peers - 1)]
        down = [(j, i) for i, j in up]
        last = lax.slice_in_dim(x, length - width, length, axis=dim)
        leading = lax.slice_in_dim(x, 0, width, axis=dim)
        before = lax.ppermute(last, axis, up)
        after = lax.ppermute(leading, axis, down)
        x = jnp.concatenate([before, x, after], axis=dim)
    return x


def moments(values, total_count):
    sums = lax.psum(jnp.sum(values, axis=(0, 1)), ("batch", "seq"))
    average = sums / total_count
    deviation = values - average
    squares = lax.psum(jnp.sum(deviation * deviation, axis=(0, 1)), ("batch", "seq"))
    variance = squares / total_count
    return (average, variance)


def norm_apply(values, average, variance, scale_gain, shift_bias):
    factor = scale_gain * lax.rsqrt(variance + EPS)
    return jax.nn.gelu((values - average) * factor + shift_bias, approximate=False).astype(
        jnp.bfloat16
    )


def conv_point(
    residual_rows, edge_padded, dilation, conv_taps, point_proj, mid_gain, mid_bias, total_count
):
    seqs_here, rows_out, channels = residual_rows.shape
    earlier = edge_padded[:, 0:rows_out]
    centre = edge_padded[:, dilation : dilation + rows_out]
    following = edge_padded[:, 2 * dilation : 2 * dilation + rows_out]
    mixture = jnp.dot(
        centre.reshape(-1, channels), conv_taps[1], preferred_element_type=jnp.float32
    )
    mixture = mixture + jnp.dot(
        earlier.reshape(-1, channels), conv_taps[0], preferred_element_type=jnp.float32
    )
    mixture = mixture + jnp.dot(
        following.reshape(-1, channels), conv_taps[2], preferred_element_type=jnp.float32
    )
    mixture = mixture.reshape(seqs_here, rows_out, -1)
    average, variance = moments(mixture, total_count)
    gated = norm_apply(mixture, average, variance, mid_gain, mid_bias)
    branch = jnp.dot(
        gated.reshape(seqs_here * rows_out, -1), point_proj, preferred_element_type=jnp.float32
    )
    return residual_rows + branch.reshape(seqs_here, rows_out, channels)


def per_device(
    inputs,
    dilated_tap_weight,
    pointwise_weight,
    stream_norm_gain,
    stream_norm_bias,
    conv_norm_gain,
    conv_norm_bias,
):
    seqs_here, position_grid, channels = inputs.shape
    total_count = seqs_here * position_grid * lax.axis_size("batch") * lax.axis_size("seq")
    near_dilation = position_grid // 8
    far_dilation = position_grid // 4
    residual_flow = inputs.astype(jnp.float32)
    average, variance = moments(residual_flow, total_count)
    gelu_activated = norm_apply(
        residual_flow, average, variance, stream_norm_gain[0], stream_norm_bias[0]
    )
    edge_padded = padded(gelu_activated, (("seq", 1),), near_dilation)
    residual_flow = conv_point(
        residual_flow,
        edge_padded,
        near_dilation,
        dilated_tap_weight[0],
        pointwise_weight[0],
        conv_norm_gain[0],
        conv_norm_bias[0],
        total_count,
    )
    average, variance = moments(residual_flow, total_count)
    gelu_activated = norm_apply(
        residual_flow, average, variance, stream_norm_gain[1], stream_norm_bias[1]
    )
    edge_padded = padded(gelu_activated, (("seq", 1),), far_dilation)
    residual_flow = conv_point(
        residual_flow,
        edge_padded,
        far_dilation,
        dilated_tap_weight[1],
        pointwise_weight[1],
        conv_norm_gain[1],
        conv_norm_bias[1],
        total_count,
    )
    pooled = residual_flow.reshape(seqs_here, position_grid // POOL, POOL, channels).mean(axis=2)
    grouped = pooled.reshape(seqs_here, position_grid // POOL, HEADS, channels // HEADS).transpose(
        0, 2, 3, 1
    )
    return lax.all_to_all(grouped, "seq", split_axis=2, concat_axis=3, tiled=True)


def solution(mesh):
    return jax.shard_map(
        per_device,
        mesh=mesh,
        in_specs=(P("batch", "seq", None), P(), P(), P(), P(), P(), P()),
        out_specs=P("batch", None, "seq", None),
        check_vma=False,
    )
```

profile of v0, /device:TPU:1, one launch (start us, length us, event | category | flops | bytes accessed | tf_op | source)
XLA Modules:
  0.0 701.7 jit_solution(14856842227652571610)
XLA Ops:
  0.0 2.1 convert_reduce_fusion
  2.1 81.4 %psum.56 = f32[512]{0:T(512)S(1)} all-reduce(f32[512]{0:T(512)S(1)} %convert_reduce_fusion), channel_id=1, replica_groups=mesh['batch'=8,'seq'=32] {'batch','seq'}, use_global_device_ids=true, to_apply=%region_1.0 | all-reduce | flops 512 | bytes 4096 | tf_op jit(solution)/shard_map/psum | solution.py:27
  83.5 0.6 fusion.2
  84.1 72.4 %psum.57 = f32[512]{0:T(512)S(1)} all-reduce(f32[512]{0:T(512)S(1)} %fusion.2), channel_id=1, replica_groups=mesh['batch'=8,'seq'=32] {'batch','seq'}, use_global_device_ids=true, to_apply=%region_3.0 | all-reduce | flops 512 | bytes 4096 | tf_op jit(solution)/shard_map/psum | solution.py:30
  156.6 9.5 %fusion.7 = bf16[1,2048,512]{2,1,0:T(8,128)(2,1)S(1)} fusion(bf16[1,2048,512]{2,1,0:T(8,128)(2,1)S(1)} %copy-done, f32[512]{0:T(512)S(1)} %bitcast.79, f32[512]{0:T(512)S(1)} %rsqrt_multiply_fusion.1, f32[512]{0:T(512)S(1)} %broadcast_multiply_fusion.2), kind=kLoop, calls=%fused_computation.12 | loop fusion | flops 72351744 | bytes 4200448 | tf_op jit(solution)/shard_map/convert_element_type | solution.py:37
  166.2 2.6 collective-permute-start.1
  168.8 4.5 collective-permute-start
  173.3 0.7 fusion.50
  174.0 2.7 collective-permute-done
  176.8 0.7 convolution_add_fusion.3
  177.5 2.0 fusion.220
  179.5 76.3 %psum.58 = f32[256]{0:T(256)S(1)} all-reduce(f32[256]{0:T(256)S(1)} %get-tuple-element.17), channel_id=1, replica_groups=mesh['batch'=8,'seq'=32] {'batch','seq'}, use_global_device_ids=true, to_apply=%region_5.0 | all-reduce | flops 256 | bytes 2048 | tf_op jit(solution)/shard_map/psum | solution.py:27
  255.9 1.9 multiply_reduce_fusion.2
  257.8 73.7 %psum.59 = f32[256]{0:T(256)S(1)} all-reduce(f32[256]{0:T(256)S(1)} %multiply_reduce_fusion.2), channel_id=1, replica_groups=mesh['batch'=8,'seq'=32] {'batch','seq'}, use_global_device_ids=true, to_apply=%region_7.0 | all-reduce | flops 256 | bytes 2048 | tf_op jit(solution)/shard_map/psum | solution.py:30
  331.5 7.7 %fusion.221 = (f32[512]{0:T(512)S(1)}, f32[1,2048,512]{2,1,0:T(8,128)}) fusion(bf16[2,256,512]{2,1,0:T(8,128)(2,1)S(1)} %copy-done.7, f32[2048,256]{1,0:T(8,128)} %get-tuple-element.18, f32[256]{0:T(256)S(1)} %bitcast.85, f32[256]{0:T(256)S(1)} %rsqrt_multiply_fusion.3, f32[256]{0:T(256)S(1)} %broadcast_multiply_fusion.4, bf16[1,2048,512]{2,1,0:T(8,128)(2,1)S(1)} %copy-done), kind=kOutput, calls=%fused_computation.277 | convolution fusion | flops 575667712 | bytes 8655872 | tf_op jit(solution)/shard_map/dot_general | solution.py:61
  339.2 73.3 %psum.60 = f32[512]{0:T(512)S(1)} all-reduce(f32[512]{0:T(512)S(1)} %get-tuple-element.19), channel_id=1, replica_groups=mesh['batch'=8,'seq'=32] {'batch','seq'}, use_global_device_ids=true, to_apply=%region_9.0 | all-reduce | flops 512 | bytes 4096 | tf_op jit(solution)/shard_map/psum | solution.py:27
  412.5 2.7 multiply_reduce_fusion
  415.2 74.2 %psum.61 = f32[512]{0:T(512)S(1)} all-reduce(f32[512]{0:T(512)S(1)} %multiply_reduce_fusion), channel_id=1, replica_groups=mesh['batch'=8,'seq'=32] {'batch','seq'}, use_global_device_ids=true, to_apply=%region_11.0 | all-reduce | flops 512 | bytes 4096 | tf_op jit(solution)/shard_map/psum | solution.py:30
  489.4 10.9 %fusion.12 = bf16[1,2048,512]{2,1,0:T(8,128)(2,1)S(1)} fusion(f32[1,2048,512]{2,1,0:T(8,128)} %get-tuple-element.20, f32[512]{0:T(512)S(1)} %bitcast.78, f32[512]{0:T(512)S(1)} %rsqrt_multiply_fusion, f32[512]{0:T(512)S(1)} %broadcast_multiply_fusion.1), kind=kLoop, calls=%fused_computation.17 | loop fusion | flops 71303168 | bytes 6297600 | tf_op jit(solution)/shard_map/convert_element_type | solution.py:37
  500.3 3.7 collective-permute-start.2
  504.1 1.9 collective-permute-start.3
  506.0 0.7 fusion.48
  506.7 3.5 collective-permute-done.2
  510.2 0.7 convolution_add_fusion.1
  510.9 5.2 collective-permute-done.3
  516.1 0.7 fusion.222
  516.8 77.0 %psum.62 = f32[256]{0:T(256)S(1)} all-reduce(f32[256]{0:T(256)S(1)} %get-tuple-element.21), channel_id=1, replica_groups=mesh['batch'=8,'seq'=32] {'batch','seq'}, use_global_device_ids=true, to_apply=%region_13.0 | all-reduce | flops 256 | bytes 2048 | tf_op jit(solution)/shard_map/psum | solution.py:27
  593.8 0.3 multiply_reduce_fusion.1
  594.1 74.6 %psum.63 = f32[256]{0:T(256)S(1)} all-reduce(f32[256]{0:T(256)S(1)} %multiply_reduce_fusion.1), channel_id=1, replica_groups=mesh['batch'=8,'seq'=32] {'batch','seq'}, use_global_device_ids=true, to_apply=%region_15.0 | all-reduce | flops 256 | bytes 2048 | tf_op jit(solution)/shard_map/psum | solution.py:30
  668.7 7.7 %bitcast_reduce_fusion = f32[256,512]{1,0:T(8,128)S(1)} fusion(f32[1,2048,512]{2,1,0:T(8,128)} %get-tuple-element.20, f32[2048,256]{1,0:T(8,128)S(1)} %get-tuple-element.22, f32[256]{0:T(256)S(1)} %bitcast.84, f32[256]{0:T(256)S(1)} %rsqrt_multiply_fusion.2, f32[256]{0:T(256)S(1)} %broadcast_multiply_fusion.3, bf16[2,256,512]{2,1,0:T(8,128)(2,1)S(1)} %copy-done.7), kind=kOutput, calls=%fused_computation.18 | convolution fusion | flops 574488576 | bytes 7080960 | tf_op jit(solution)/shard_map/dot_general | solution.py:61
  676.9 23.3 %all_to_all.18 = f32[1,8,64,256]{3,1,0,2:T(8,128)S(1)} all-to-all(f32[1,8,64,256]{3,1,0,2:T(8,128)S(1)} %copy.13), channel_id=1, replica_groups=mesh['batch'=8,'seq'=32] {'seq'}, dimensions={2} | all-to-all | bytes 1048576 | tf_op jit(solution)/shard_map/all_to_all | solution.py:115
  700.6 1.1 reshape.251
  (35 shorter events, 1.1 us)
Async XLA Ops:
  0.0 83.5 %copy-start = (bf16[1,2048,512]{2,1,0:T(8,128)(2,1)S(1)}, bf16[1,2048,512]{2,1,0:T(8,128)(2,1)}, u32[]{:S(2)}) copy-start(bf16[1,2048,512]{2,1,0:T(8,128)(2,1)} %param.7) | copy-start | bytes 6291460
  0.0 156.5 %copy-start.3 = (f32[2,512]{1,0:T(2,128)S(1)}, f32[2,512]{1,0:T(2,128)}, u32[]{:S(2)}) copy-start(f32[2,512]{1,0:T(2,128)} %param.10) | copy-start | bytes 12292
  0.0 156.5 %copy-start.4 = (f32[2,512]{1,0:T(2,128)S(1)}, f32[2,512]{1,0:T(2,128)}, u32[]{:S(2)}) copy-start(f32[2,512]{1,0:T(2,128)} %param.11) | copy-start | bytes 12292
  156.6 16.7 %copy-start.1 = (bf16[2,3,512,256]{3,2,1,0:T(8,128)(2,1)S(1)}, bf16[2,3,512,256]{3,2,1,0:T(8,128)(2,1)}, u32[]{:S(2)}) copy-start(bf16[2,3,512,256]{3,2,1,0:T(8,128)(2,1)} %param.8) | copy-start | bytes 4718596
  166.2 11.3 %collective-permute-start.1 = (bf16[1,256,512]{2,1,0:T(8,128)(2,1)S(1)}, bf16[1,256,512]{2,1,0:T(8,128)(2,1)S(1)}, u32[]{:S(2)}, u32[]{:S(2)}) collective-permute-start(bf16[1,256,512]{2,1,0:T(8,128)(2,1)S(1)} %get-tuple-element.7), channel_id=1, source_target_pairs={{1,0},{2,1},{3,2},{4,3},{5,4},{6,5},{7,6},{8,7},{9,8},{10,9},{11,1... | collective-permute-start | bytes 786440 | tf_op jit(solution)/shard_map/ppermute | solution.py:21
  168.8 5.2 copy-start.5
  168.8 5.2 copy-start.6
  168.8 8.0 %collective-permute-start = (bf16[1,256,512]{2,1,0:T(8,128)(2,1)S(1)}, bf16[1,256,512]{2,1,0:T(8,128)(2,1)S(1)}, u32[]{:S(2)}, u32[]{:S(2)}) collective-permute-start(bf16[1,256,512]{2,1,0:T(8,128)(2,1)S(1)} %get-tuple-element.8), channel_id=1, source_target_pairs={{0,1},{1,2},{2,3},{3,4},{4,5},{5,6},{6,7},{7,8},{8,9},{9,10},{10,1... | collective-permute-start | bytes 786440 | tf_op jit(solution)/shard_map/ppermute | solution.py:20
  179.5 152.0 %copy-start.7 = (bf16[2,256,512]{2,1,0:T(8,128)(2,1)S(1)}, bf16[2,256,512]{2,1,0:T(8,128)(2,1)}, u32[]{:S(2)}) copy-start(bf16[2,256,512]{2,1,0:T(8,128)(2,1)} %param.9) | copy-start | bytes 1572868
  500.3 5.7 copy-start.2
  500.3 9.8 %collective-permute-start.2 = (bf16[1,512,512]{2,1,0:T(8,128)(2,1)S(1)}, bf16[1,512,512]{2,1,0:T(8,128)(2,1)S(1)}, u32[]{:S(2)}, u32[]{:S(2)}) collective-permute-start(bf16[1,512,512]{2,1,0:T(8,128)(2,1)S(1)} %get-tuple-element.6), channel_id=1, source_target_pairs={{0,1},{1,2},{2,3},{3,4},{4,5},{5,6},{6,7},{7,8},{8,9},{9,10},{10,1... | collective-permute-start | bytes 1572872 | tf_op jit(solution)/shard_map/ppermute | solution.py:20
  504.1 12.0 %collective-permute-start.3 = (bf16[1,512,512]{2,1,0:T(8,128)(2,1)S(1)}, bf16[1,512,512]{2,1,0:T(8,128)(2,1)S(1)}, u32[]{:S(2)}, u32[]{:S(2)}) collective-permute-start(bf16[1,512,512]{2,1,0:T(8,128)(2,1)S(1)} %get-tuple-element.5), channel_id=1, source_target_pairs={{1,0},{2,1},{3,2},{4,3},{5,4},{6,5},{7,6},{8,7},{9,8},{10,9},{11,1... | collective-permute-start | bytes 1572872 | tf_op jit(solution)/shard_map/ppermute | solution.py:21
where the time goes:
time: 704 us; the launch traced here: 702 us
  blocking collectives  626 us (89%)
  other arithmetic  28.1 us (4%)
  matrix products  21 us (3%)
  starting transfers between devices  12.7 us (2%)
  waiting for transfers between devices  11.4 us (2%)
    psum x4, blocking collectives, moments(): sums = lax.psum(jnp.sum(values, axis=(0, 1)), ('batch', 'seq'))  308 us
    psum x4, blocking collectives, moments(): lax.psum(jnp.sum(deviation * deviation, axis=(0, 1)), ('batch', 'seq'))  295 us
    all_to_all x1, blocking collectives, per_device(): lax.all_to_all(grouped, 'seq', split_axis=2, concat_axis=3, tiled=True)  23.3 us
    convert_element_type x2, other arithmetic, norm_apply(): jax.nn.gelu((values - average) * factor + shift_bias, approximate=False)  20.4 us
    dot_general x2, matrix products, conv_point(): jnp.dot(gated.reshape(seqs_here * rows_out, -1), point_proj, preferred_el...  15.4 us
  transfers between devices with their start and end apart: 4, of which 3 were waited for; matrix products, arithmetic and copies ran while one was open for 0% of the time, Pallas kernels for 0%

commit v1 on v0

v1 whole, which is shorter than its diff:
```python
import jax
import jax.numpy as jnp
from jax import lax
from jax.sharding import Mesh, PartitionSpec as P

HEADS = 8
POOL = 8
EPS = 1e-05

NAMES = ("y_lo", "x", "z", "y_hi", "core")
SIZES = (2, 4, 8, 2, 2)
BATCH = ("y_lo", "x")
SEQ = ("z", "y_hi", "core")
STAGES = (("z", "core"), ("y_lo", "x", "y_hi"))


def padded(x, width):
    peers, length = (lax.axis_size(SEQ), x.shape[1])
    up = [(i, i + 1) for i in range(peers - 1)]
    down = [(j, i) for i, j in up]
    before = lax.ppermute(x[:, length - width :], SEQ, up)
    after = lax.ppermute(x[:, :width], SEQ, down)
    return jnp.concatenate([before, x, after], axis=1)


def moments(values):
    count = values.shape[0] * values.shape[1]
    mean = jnp.sum(values, axis=(0, 1)) / count
    deviation = values - mean
    stats = jnp.stack([mean, jnp.sum(deviation * deviation, axis=(0, 1))])
    for axes in STAGES:
        peers = lax.axis_size(axes)
        tiles = stats.reshape(-1, 128)
        sent = jnp.broadcast_to(tiles[None], (peers,) + tiles.shape)
        got = lax.all_to_all(sent, axes, 0, 0, tiled=True).reshape(peers, 2, -1)
        mean = jnp.mean(got[:, 0], axis=0)
        spread = got[:, 0] - mean
        stats = jnp.stack([mean, jnp.sum(got[:, 1], axis=0) + count * jnp.sum(spread * spread, axis=0)])
        count = count * peers
    return stats[0], stats[1] / count


def norm_gelu(values, gain, bias):
    average, variance = moments(values)
    factor = gain * lax.rsqrt(variance + EPS)
    return jax.nn.gelu((values - average) * factor + bias, approximate=False).astype(jnp.bfloat16)


def block(stream, taps, point, in_gain, in_bias, mid_gain, mid_bias, dilation):
    seqs, rows, channels = stream.shape
    edged = padded(norm_gelu(stream, in_gain, in_bias), dilation)

    def tap(k):
        piece = edged[:, k * dilation : k * dilation + rows].reshape(-1, channels)
        return jnp.dot(piece, taps[k], preferred_element_type=jnp.float32)

    mixture = (tap(1) + tap(0) + tap(2)).reshape(seqs, rows, -1)
    gated = norm_gelu(mixture, mid_gain, mid_bias)
    branch = jnp.dot(gated.reshape(seqs * rows, -1), point, preferred_element_type=jnp.float32)
    return stream + branch.reshape(stream.shape)


def per_device(inputs, taps, point, in_gain, in_bias, mid_gain, mid_bias):
    seqs, rows, channels = inputs.shape
    stream = inputs.astype(jnp.float32)
    for k, dilation in enumerate((256, 512)):
        stream = block(
            stream, taps[k], point[k], in_gain[k], in_bias[k], mid_gain[k], mid_bias[k], dilation
        )
    pooled = stream.reshape(seqs, rows // POOL, POOL, channels).mean(axis=2)
    grouped = pooled.reshape(seqs, rows // POOL, HEADS, channels // HEADS).transpose(0, 2, 3, 1)
    return lax.all_to_all(grouped, SEQ, split_axis=2, concat_axis=3, tiled=True)


def solution(mesh):
    fine = Mesh(mesh.devices.reshape(SIZES), NAMES)
    return jax.shard_map(
        per_device,
        mesh=fine,
        in_specs=(P(BATCH, SEQ, None), P(), P(), P(), P(), P(), P()),
        out_specs=P(BATCH, None, SEQ, None),
        check_vma=False,
    )
```

time: 704 us -> 201 us (0.29)
  blocking collectives: 626 us -> 66.2 us
  starting transfers between devices: 12.7 us -> 41.3 us
  waiting for transfers between devices: 11.4 us -> 39.5 us
  local copies, waits for them, and re-layouts: 2.12 us -> 9.16 us
    psum x8 -> x0, blocking collectives: 603 us -> none  [the longest x4 308 us: moments(): sums = lax.psum(jnp.sum(values, axis=(0, 1)), ('batch', 'seq'))]
    all_to_all x1 -> x5, blocking collectives: 23.3 us -> 66.2 us  [the longest x4 44.6 us: moments(): got = lax.all_to_all(sent, axes, 0, 0, tiled=True).reshape(peers, 2, -1)]
    all_to_all x0 -> x4, waiting for transfers between devices: none -> 28.3 us  [moments(): got = lax.all_to_all(sent, axes, 0, 0, tiled=True).reshape(peers, 2, -1)]
    all_to_all x0 -> x4, starting transfers between devices: none -> 28.1 us  [moments(): got = lax.all_to_all(sent, axes, 0, 0, tiled=True).reshape(peers, 2, -1)]
  transfers between devices with their start and end apart: 4 -> 8, of which waited for: 3 -> 7; matrix products, arithmetic and copies ran while one was open for 0% -> 1% of each run, Pallas kernels for 0% -> 0%
where the time goes in v1:
time: 201 us; the launch traced here: 200 us
  blocking collectives  66.2 us (33%)
  starting transfers between devices  41.3 us (21%)
  waiting for transfers between devices  39.5 us (20%)
  other arithmetic  25.2 us (13%)
  matrix products  18.6 us (9%)
  local copies, waits for them, and re-layouts  9.16 us (5%)
    all_to_all x4, blocking collectives, moments(): got = lax.all_to_all(sent, axes, 0, 0, tiled=True).reshape(peers, 2, -1)  44.6 us
    all_to_all x4, waiting for transfers between devices, moments(): got = lax.all_to_all(sent, axes, 0, 0, tiled=True).reshape(peers, 2, -1)  28.3 us
    all_to_all x4, starting transfers between devices, moments(): got = lax.all_to_all(sent, axes, 0, 0, tiled=True).reshape(peers, 2, -1)  28.1 us
    all_to_all x1, blocking collectives, per_device(): return lax.all_to_all(grouped, SEQ, split_axis=2, concat_axis=3, tiled=True)  21.6 us
    convert_element_type x2, other arithmetic, norm_gelu(): jax.nn.gelu((values - average) * factor + bias, approximate=False)  20.4 us
    dot_general x2, matrix products, block(): jnp.dot(gated.reshape(seqs * rows, -1), point, preferred_element_type=jnp...  14.3 us
    ppermute x2, starting transfers between devices, padded(): before = lax.ppermute(x[:, length - width:], SEQ, up)  7.71 us
    ppermute x2, waiting for transfers between devices, padded(): before = lax.ppermute(x[:, length - width:], SEQ, up)  6.02 us
  transfers between devices with their start and end apart: 8, of which 7 were waited for; matrix products, arithmetic and copies ran while one was open for 1% of the time, Pallas kernels for 0%

profile of v1, /device:TPU:1, one launch (start us, length us, event | category | flops | bytes accessed | tf_op | source)
XLA Modules:
  0.0 200.5 jit_solution(2026583481576846273)
XLA Ops:
  0.0 2.1 %convert_reduce_fusion = f32[512]{0:T(512)S(1)} fusion(bf16[1,2048,512]{2,1,0:T(8,128)(2,1)} %param.7), kind=kLoop, calls=%fused_computation.3 | loop fusion | flops 2096640 | bytes 2099200 | tf_op jit(solution)/shard_map/reduce_sum | solution.py:28
  3.5 10.0 %all-to-all-start = ((f32[16,8,128]{2,1,0:T(8,128)}), f32[16,8,128]{2,1,0:T(8,128)S(1)}, u32[]{:S(2)}, u32[]{:S(2)}) async-start(f32[16,8,128]{2,1,0:T(8,128)} %broadcast_in_dim.33), calls=%async_computation | async-start | bytes 131072 | tf_op jit(solution)/shard_map/all_to_all | solution.py:35
  13.5 7.8 %all-to-all-done = f32[16,8,128]{2,1,0:T(8,128)S(1)} async-done(((f32[16,8,128]{2,1,0:T(8,128)}), f32[16,8,128]{2,1,0:T(8,128)S(1)}, u32[]{:S(2)}, u32[]{:S(2)}) %all-to-all-start) | async-done | bytes 65568 | tf_op jit(solution)/shard_map/all_to_all | solution.py:35
  22.1 6.8 %all-to-all-start.1 = ((f32[16,8,128]{2,1,0:T(8,128)}), f32[16,8,128]{2,1,0:T(8,128)S(1)}, u32[]{:S(2)}, u32[]{:S(2)}) async-start(f32[16,8,128]{2,1,0:T(8,128)} %broadcast_in_dim.35), calls=%async_computation.1 | async-start | bytes 131072 | tf_op jit(solution)/shard_map/all_to_all | solution.py:35
  28.9 6.7 %all-to-all-done.1 = f32[16,8,128]{2,1,0:T(8,128)S(1)} async-done(((f32[16,8,128]{2,1,0:T(8,128)}), f32[16,8,128]{2,1,0:T(8,128)S(1)}, u32[]{:S(2)}, u32[]{:S(2)}) %all-to-all-start.1) | async-done | bytes 65568 | tf_op jit(solution)/shard_map/all_to_all | solution.py:35
  35.8 9.5 %fusion.2 = bf16[1,2048,512]{2,1,0:T(8,128)(2,1)S(1)} fusion(bf16[1,2048,512]{2,1,0:T(8,128)(2,1)S(1)} %copy-done, f32[512]{0:T(512)S(1)} %bitcast.152, f32[512]{0:T(512)S(1)} %rsqrt_multiply_fusion.1, f32[512]{0:T(512)S(1)} %broadcast_multiply_fusion.3), kind=kLoop, calls=%fused_computation.8 | loop fusion | flops 72351744 | bytes 4200448 | tf_op jit(solution)/shard_map/convert_element_type | solution.py:46
  45.4 3.5 %collective-permute-start.1 = (bf16[1,256,512]{2,1,0:T(8,128)(2,1)S(1)}, bf16[1,256,512]{2,1,0:T(8,128)(2,1)S(1)}, u32[]{:S(2)}, u32[]{:S(2)}) collective-permute-start(bf16[1,256,512]{2,1,0:T(8,128)(2,1)S(1)} %get-tuple-element.23), channel_id=1, source_target_pairs={{1,0},{2,1},{3,2},{4,3},{5,4},{6,5},{7,6},{8,7},{9,8},{10,9},{11,1... | collective-permute-start | bytes 786440 | tf_op jit(solution)/shard_map/ppermute | solution.py:22
  48.9 3.6 %collective-permute-start = (bf16[1,256,512]{2,1,0:T(8,128)(2,1)S(1)}, bf16[1,256,512]{2,1,0:T(8,128)(2,1)S(1)}, u32[]{:S(2)}, u32[]{:S(2)}) collective-permute-start(bf16[1,256,512]{2,1,0:T(8,128)(2,1)S(1)} %get-tuple-element.24), channel_id=1, source_target_pairs={{0,1},{1,2},{2,3},{3,4},{4,5},{5,6},{6,7},{7,8},{8,9},{9,10},{10,1... | collective-permute-start | bytes 786440 | tf_op jit(solution)/shard_map/ppermute | solution.py:21
  53.2 2.6 %collective-permute-done = bf16[1,256,512]{2,1,0:T(8,128)(2,1)S(1)} collective-permute-done((bf16[1,256,512]{2,1,0:T(8,128)(2,1)S(1)}, bf16[1,256,512]{2,1,0:T(8,128)(2,1)S(1)}, u32[]{:S(2)}, u32[]{:S(2)}) %collective-permute-start) | collective-permute-done | bytes 262176 | tf_op jit(solution)/shard_map/ppermute | solution.py:21
  56.5 0.7 fusion.236
  57.3 1.3 copy-done.2
  59.5 7.9 %all-to-all-start.2 = ((f32[16,4,128]{2,1,0:T(4,128)}), f32[16,4,128]{2,1,0:T(4,128)S(1)}, u32[]{:S(2)}, u32[]{:S(2)}) async-start(f32[16,4,128]{2,1,0:T(4,128)} %broadcast_in_dim.37), calls=%async_computation.2 | async-start | bytes 65536 | tf_op jit(solution)/shard_map/all_to_all | solution.py:35
  67.4 7.4 %all-to-all-done.2 = f32[16,4,128]{2,1,0:T(4,128)S(1)} async-done(((f32[16,4,128]{2,1,0:T(4,128)}), f32[16,4,128]{2,1,0:T(4,128)S(1)}, u32[]{:S(2)}, u32[]{:S(2)}) %all-to-all-start.2) | async-done | bytes 32800 | tf_op jit(solution)/shard_map/all_to_all | solution.py:35
  75.6 3.5 %all-to-all-start.3 = ((f32[16,4,128]{2,1,0:T(4,128)}), f32[16,4,128]{2,1,0:T(4,128)S(1)}, u32[]{:S(2)}, u32[]{:S(2)}) async-start(f32[16,4,128]{2,1,0:T(4,128)} %broadcast_in_dim.39), calls=%async_computation.3 | async-start | bytes 65536 | tf_op jit(solution)/shard_map/all_to_all | solution.py:35
  79.1 6.5 %all-to-all-done.3 = f32[16,4,128]{2,1,0:T(4,128)S(1)} async-done(((f32[16,4,128]{2,1,0:T(4,128)}), f32[16,4,128]{2,1,0:T(4,128)S(1)}, u32[]{:S(2)}, u32[]{:S(2)}) %all-to-all-start.3) | async-done | bytes 32800 | tf_op jit(solution)/shard_map/all_to_all | solution.py:35
  85.7 6.5 %fusion.237 = (f32[512]{0:T(512)S(1)}, f32[1,2048,512]{2,1,0:T(8,128)S(1)}) fusion(bf16[2,256,512]{2,1,0:T(8,128)(2,1)S(1)} %copy-done.10, f32[2048,256]{1,0:T(8,128)} %copy-done.2, f32[256]{0:T(256)S(1)} %bitcast.165, f32[256]{0:T(256)S(1)} %rsqrt_multiply_fusion.3, f32[256]{0:T(256)S(1)} %broadcast_multiply_fusion.9, bf16[1,2048,512]{2,1,0:T(8,128)(2,1)S(1)} %copy-done), kind=kOutput, calls=%fused_computation.338 | convolution fusion | flops 575667712 | bytes 8655872 | tf_op jit(solution)/shard_map/dot_general | solution.py:59
  92.7 1.4 copy-done.1
  94.2 11.8 %all_to_all.58 = f32[16,8,128]{2,1,0:T(8,128)S(1)} all-to-all(f32[16,8,128]{2,1,0:T(8,128)S(1)} %broadcast_in_dim.81), channel_id=1, replica_groups=mesh['y_lo'=2,'x'=4,'z'=8,'y_hi'=2,'core'=2] {'z','core'}, dimensions={0} | all-to-all | bytes 131072 | tf_op jit(solution)/shard_map/all_to_all | solution.py:35
  106.2 9.5 %all_to_all.59 = f32[16,8,128]{2,1,0:T(8,128)S(1)} all-to-all(f32[16,8,128]{2,1,0:T(8,128)S(1)} %broadcast_in_dim.83), channel_id=1, replica_groups=mesh['y_lo'=2,'x'=4,'z'=8,'y_hi'=2,'core'=2] {'y_lo','x','y_hi'}, dimensions={0} | all-to-all | bytes 131072 | tf_op jit(solution)/shard_map/all_to_all | solution.py:35
  115.8 10.9 %fusion.5 = bf16[1,2048,512]{2,1,0:T(8,128)(2,1)S(1)} fusion(f32[1,2048,512]{2,1,0:T(8,128)} %copy-done.1, f32[512]{0:T(512)S(1)} %bitcast.150, f32[512]{0:T(512)S(1)} %rsqrt_multiply_fusion, f32[512]{0:T(512)S(1)} %broadcast_multiply_fusion.1), kind=kLoop, calls=%fused_computation.11 | loop fusion | flops 71303168 | bytes 6297600 | tf_op jit(solution)/shard_map/convert_element_type | solution.py:46
  126.8 4.1 %collective-permute-start.2 = (bf16[1,512,512]{2,1,0:T(8,128)(2,1)S(1)}, bf16[1,512,512]{2,1,0:T(8,128)(2,1)S(1)}, u32[]{:S(2)}, u32[]{:S(2)}) collective-permute-start(bf16[1,512,512]{2,1,0:T(8,128)(2,1)S(1)} %get-tuple-element.22), channel_id=1, source_target_pairs={{0,1},{1,2},{2,3},{3,4},{4,5},{5,6},{6,7},{7,8},{8,9},{9,10},{10,1... | collective-permute-start | bytes 1572872 | tf_op jit(solution)/shard_map/ppermute | solution.py:21
  130.9 1.9 collective-permute-start.3
  133.6 3.4 %collective-permute-done.2 = bf16[1,512,512]{2,1,0:T(8,128)(2,1)S(1)} collective-permute-done((bf16[1,512,512]{2,1,0:T(8,128)(2,1)S(1)}, bf16[1,512,512]{2,1,0:T(8,128)(2,1)S(1)}, u32[]{:S(2)}, u32[]{:S(2)}) %collective-permute-start.2) | collective-permute-done | bytes 524320 | tf_op jit(solution)/shard_map/ppermute | solution.py:21
  137.0 0.7 convolution_add_fusion.1
  137.8 5.2 %collective-permute-done.3 = bf16[1,512,512]{2,1,0:T(8,128)(2,1)S(1)} collective-permute-done((bf16[1,512,512]{2,1,0:T(8,128)(2,1)S(1)}, bf16[1,512,512]{2,1,0:T(8,128)(2,1)S(1)}, u32[]{:S(2)}, u32[]{:S(2)}) %collective-permute-start.3) | collective-permute-done | bytes 524320 | tf_op jit(solution)/shard_map/ppermute | solution.py:22
  142.9 0.7 fusion.238
  143.7 1.3 copy-done.3
  145.3 14.3 %all_to_all.60 = f32[16,4,128]{2,1,0:T(4,128)S(1)} all-to-all(f32[16,4,128]{2,1,0:T(4,128)S(1)} %broadcast_in_dim.85), channel_id=1, replica_groups=mesh['y_lo'=2,'x'=4,'z'=8,'y_hi'=2,'core'=2] {'z','core'}, dimensions={0} | all-to-all | bytes 65536 | tf_op jit(solution)/shard_map/all_to_all | solution.py:35
  159.8 9.1 %all_to_all.61 = f32[16,4,128]{2,1,0:T(4,128)S(1)} all-to-all(f32[16,4,128]{2,1,0:T(4,128)S(1)} %broadcast_in_dim.87), channel_id=1, replica_groups=mesh['y_lo'=2,'x'=4,'z'=8,'y_hi'=2,'core'=2] {'y_lo','x','y_hi'}, dimensions={0} | all-to-all | bytes 65536 | tf_op jit(solution)/shard_map/all_to_all | solution.py:35
  169.0 7.9 %bitcast_reduce_fusion = f32[256,512]{1,0:T(8,128)S(1)} fusion(f32[1,2048,512]{2,1,0:T(8,128)} %copy-done.1, f32[2048,256]{1,0:T(8,128)} %copy-done.3, f32[256]{0:T(256)S(1)} %bitcast.164, f32[256]{0:T(256)S(1)} %rsqrt_multiply_fusion.2, f32[256]{0:T(256)S(1)} %broadcast_multiply_fusion.7, bf16[2,256,512]{2,1,0:T(8,128)(2,1)S(1)} %copy-done.10), kind=kOutput, calls=%fused_computation.19 | convolution fusion | flops 574488576 | bytes 7080960 | tf_op jit(solution)/shard_map/dot_general | solution.py:59
  177.5 21.6 %all_to_all.62 = f32[1,8,64,256]{3,1,0,2:T(8,128)S(1)} all-to-all(f32[1,8,64,256]{3,1,0,2:T(8,128)S(1)} %copy.37), channel_id=1, replica_groups=mesh['y_lo'=2,'x'=4,'z'=8,'y_hi'=2,'core'=2] {'z','y_hi','core'}, dimensions={2} | all-to-all | bytes 1048576 | tf_op jit(solution)/shard_map/all_to_all | solution.py:72
  199.3 1.1 reshape.525
  (105 shorter events, 8.8 us)
Async XLA Ops:
  0.0 2.2 %copy-start = (bf16[1,2048,512]{2,1,0:T(8,128)(2,1)S(1)}, bf16[1,2048,512]{2,1,0:T(8,128)(2,1)}, u32[]{:S(2)}) copy-start(bf16[1,2048,512]{2,1,0:T(8,128)(2,1)} %param.7) | copy-start | bytes 6291460
  0.0 13.5 %copy-start.6 = (f32[2,512]{1,0:T(2,128)S(1)}, f32[2,512]{1,0:T(2,128)}, u32[]{:S(2)}) copy-start(f32[2,512]{1,0:T(2,128)} %param.10) | copy-start | bytes 12292
  0.0 28.9 %copy-start.7 = (f32[2,512]{1,0:T(2,128)S(1)}, f32[2,512]{1,0:T(2,128)}, u32[]{:S(2)}) copy-start(f32[2,512]{1,0:T(2,128)} %param.11) | copy-start | bytes 12292
  3.5 17.8 %all-to-all-start = ((f32[16,8,128]{2,1,0:T(8,128)}), f32[16,8,128]{2,1,0:T(8,128)S(1)}, u32[]{:S(2)}, u32[]{:S(2)}) async-start(f32[16,8,128]{2,1,0:T(8,128)} %broadcast_in_dim.33), calls=%async_computation | async-start | bytes 131072 | tf_op jit(solution)/shard_map/all_to_all | solution.py:35
  22.1 13.5 %all-to-all-start.1 = ((f32[16,8,128]{2,1,0:T(8,128)}), f32[16,8,128]{2,1,0:T(8,128)S(1)}, u32[]{:S(2)}, u32[]{:S(2)}) async-start(f32[16,8,128]{2,1,0:T(8,128)} %broadcast_in_dim.35), calls=%async_computation.1 | async-start | bytes 131072 | tf_op jit(solution)/shard_map/all_to_all | solution.py:35
  35.8 16.7 %copy-start.4 = (bf16[2,3,512,256]{3,2,1,0:T(8,128)(2,1)S(1)}, bf16[2,3,512,256]{3,2,1,0:T(8,128)(2,1)}, u32[]{:S(2)}) copy-start(bf16[2,3,512,256]{3,2,1,0:T(8,128)(2,1)} %param.8) | copy-start | bytes 4718596
  45.4 11.1 %collective-permute-start.1 = (bf16[1,256,512]{2,1,0:T(8,128)(2,1)S(1)}, bf16[1,256,512]{2,1,0:T(8,128)(2,1)S(1)}, u32[]{:S(2)}, u32[]{:S(2)}) collective-permute-start(bf16[1,256,512]{2,1,0:T(8,128)(2,1)S(1)} %get-tuple-element.23), channel_id=1, source_target_pairs={{1,0},{2,1},{3,2},{4,3},{5,4},{6,5},{7,6},{8,7},{9,8},{10,9},{11,1... | collective-permute-start | bytes 786440 | tf_op jit(solution)/shard_map/ppermute | solution.py:22
  48.9 6.9 %collective-permute-start = (bf16[1,256,512]{2,1,0:T(8,128)(2,1)S(1)}, bf16[1,256,512]{2,1,0:T(8,128)(2,1)S(1)}, u32[]{:S(2)}, u32[]{:S(2)}) collective-permute-start(bf16[1,256,512]{2,1,0:T(8,128)(2,1)S(1)} %get-tuple-element.24), channel_id=1, source_target_pairs={{0,1},{1,2},{2,3},{3,4},{4,5},{5,6},{6,7},{7,8},{8,9},{9,10},{10,1... | collective-permute-start | bytes 786440 | tf_op jit(solution)/shard_map/ppermute | solution.py:21
  57.2 1.4 copy-start.2
  57.2 10.2 %copy-start.8 = (f32[2,256]{1,0:T(2,128)S(1)}, f32[2,256]{1,0:T(2,128)}, u32[]{:S(2)}) copy-start(f32[2,256]{1,0:T(2,128)} %param.12) | copy-start | bytes 6148
  57.2 21.9 %copy-start.9 = (f32[2,256]{1,0:T(2,128)S(1)}, f32[2,256]{1,0:T(2,128)}, u32[]{:S(2)}) copy-start(f32[2,256]{1,0:T(2,128)} %param.13) | copy-start | bytes 6148
  57.3 28.5 %copy-start.10 = (bf16[2,256,512]{2,1,0:T(8,128)(2,1)S(1)}, bf16[2,256,512]{2,1,0:T(8,128)(2,1)}, u32[]{:S(2)}) copy-start(bf16[2,256,512]{2,1,0:T(8,128)(2,1)} %param.9) | copy-start | bytes 1572868
  59.5 15.3 %all-to-all-start.2 = ((f32[16,4,128]{2,1,0:T(4,128)}), f32[16,4,128]{2,1,0:T(4,128)S(1)}, u32[]{:S(2)}, u32[]{:S(2)}) async-start(f32[16,4,128]{2,1,0:T(4,128)} %broadcast_in_dim.37), calls=%async_computation.2 | async-start | bytes 65536 | tf_op jit(solution)/shard_map/all_to_all | solution.py:35
  75.6 10.0 %all-to-all-start.3 = ((f32[16,4,128]{2,1,0:T(4,128)}), f32[16,4,128]{2,1,0:T(4,128)S(1)}, u32[]{:S(2)}, u32[]{:S(2)}) async-start(f32[16,4,128]{2,1,0:T(4,128)} %broadcast_in_dim.39), calls=%async_computation.3 | async-start | bytes 65536 | tf_op jit(solution)/shard_map/all_to_all | solution.py:35
  92.2 1.9 copy-start.1
  126.7 6.2 %copy-start.5 = (bf16[2,3,512,256]{3,2,1,0:T(8,128)(2,1)S(1)}, bf16[2,3,512,256]{3,2,1,0:T(8,128)(2,1)}, u32[]{:S(2)}) copy-start(bf16[2,3,512,256]{3,2,1,0:T(8,128)(2,1)} %param.8) | copy-start | bytes 4718596
  126.8 10.3 %collective-permute-start.2 = (bf16[1,512,512]{2,1,0:T(8,128)(2,1)S(1)}, bf16[1,512,512]{2,1,0:T(8,128)(2,1)S(1)}, u32[]{:S(2)}, u32[]{:S(2)}) collective-permute-start(bf16[1,512,512]{2,1,0:T(8,128)(2,1)S(1)} %get-tuple-element.22), channel_id=1, source_target_pairs={{0,1},{1,2},{2,3},{3,4},{4,5},{5,6},{6,7},{7,8},{8,9},{9,10},{10,1... | collective-permute-start | bytes 1572872 | tf_op jit(solution)/shard_map/ppermute | solution.py:21
  130.9 12.0 %collective-permute-start.3 = (bf16[1,512,512]{2,1,0:T(8,128)(2,1)S(1)}, bf16[1,512,512]{2,1,0:T(8,128)(2,1)S(1)}, u32[]{:S(2)}, u32[]{:S(2)}) collective-permute-start(bf16[1,512,512]{2,1,0:T(8,128)(2,1)S(1)} %get-tuple-element.21), channel_id=1, source_target_pairs={{1,0},{2,1},{3,2},{4,3},{5,4},{6,5},{7,6},{8,7},{9,8},{10,9},{11,1... | collective-permute-start | bytes 1572872 | tf_op jit(solution)/shard_map/ppermute | solution.py:22
  143.7 1.3 copy-start.3

commit v2 on v1

v2 whole, which is shorter than its diff:
```python
import functools

import jax
import jax.numpy as jnp
from jax import lax
from jax.experimental import pallas as pl
from jax.experimental.pallas import tpu as pltpu
from jax.sharding import Mesh, PartitionSpec as P

EPS = 1e-05
HEADS = 8
POOL = 8
ROWS = 2048
CH = 512
MID = 256
TILE = 256
CHUNK = 32

NAMES = ("y_lo", "x", "z", "y_hi", "core")
SIZES = (2, 4, 8, 2, 2)
BATCH = ("y_lo", "x")
SEQ = ("z", "y_hi", "core")
STAGES = (("z", "core"), ("y_lo", "x", "y_hi"))
PEERS = 16
F32 = jnp.float32
BF16 = jnp.bfloat16


def gelu(u):
    return 0.5 * u * (1.0 + lax.erf(u * 0.7071067811865476))


def wide(v):
    return jnp.concatenate([v[j : j + 1] for j in range(v.shape[0])], axis=1)


def norm_terms(layer, got_ref, gain_ref, bias_ref):
    rows = got_ref.shape[1] // 2
    got = got_ref[...]
    means = got[:, :rows]
    mean = jnp.sum(means, axis=0) * (1.0 / PEERS)
    spread = means - mean
    total = jnp.sum(got[:, rows:], axis=0) + (PEERS * ROWS) * jnp.sum(spread * spread, axis=0)
    variance = wide(total) * (1.0 / (PEERS * PEERS * ROWS))
    return wide(mean), gain_ref[layer : layer + 1] * lax.rsqrt(variance + EPS), bias_ref[layer : layer + 1]


def fold(v):
    return jnp.sum(v.reshape(-1, 8, v.shape[-1]), axis=0)


def put_stats(out_ref, mean, squares):
    rows = out_ref.shape[1] // 2
    for j in range(rows):
        for base, v in ((0, mean), (rows, squares)):
            piece = v[:, 128 * j : 128 * (j + 1)].reshape(1, 1, 128)
            out_ref[:, base + j : base + j + 1, :] = jnp.broadcast_to(piece, (PEERS, 1, 128))


def row_slice(i, size):
    return pl.ds(pl.multiple_of(i * size, size), size)


def deviations(refs, mean, channels):
    squares = jnp.zeros((8, channels), F32)
    for ref in refs:

        def step(i, acc, ref=ref):
            d = ref[row_slice(i, 64), :].astype(F32) - mean
            return acc + fold(d * d)

        squares = lax.fori_loop(0, ref.shape[0] // 64, step, squares, unroll=4)
    return jnp.sum(squares, axis=0, keepdims=True)


def input_stats(x_ref, low_ref, high_ref, out_ref):
    low_ref[...] = x_ref[: low_ref.shape[0], :]
    high_ref[...] = x_ref[ROWS - high_ref.shape[0] :, :]

    def step(i, acc):
        return acc + fold(x_ref[row_slice(i, 64), :].astype(F32))

    acc = lax.fori_loop(0, ROWS // 64, step, jnp.zeros((8, CH), F32), unroll=4)
    mean = jnp.sum(acc, axis=0, keepdims=True) * (1.0 / ROWS)
    put_stats(out_ref, mean, deviations((x_ref,), mean, CH))


def conv_kernel(layer, dilation, sources, flag_ref, got_ref, gain_ref, bias_ref, taps_ref, *refs):
    pieces = refs[:sources]
    conv_ref, stats_ref, act_ref = refs[sources:]
    mean, factor, bias = norm_terms(layer, got_ref, gain_ref, bias_ref)
    start = 0
    for k, piece in enumerate(pieces):

        def step(i, carry, piece=piece, start=start, k=k):
            v = piece[row_slice(i, CHUNK), :].astype(F32)
            a = gelu((v - mean) * factor + bias)
            if k == 0:
                a = jnp.where(flag_ref[0] > 0, a, 0.0)
            if k == sources - 1:
                a = jnp.where(flag_ref[1] > 0, a, 0.0)
            act_ref[pl.ds(pl.multiple_of(start + i * CHUNK, CHUNK), CHUNK), :] = a.astype(BF16)
            return carry

        lax.fori_loop(0, piece.shape[0] // CHUNK, step, 0)
        start += piece.shape[0]

    def tile(i, acc):
        base = pl.multiple_of(i * TILE, TILE)
        total = jnp.dot(act_ref[pl.ds(base + dilation, TILE), :], taps_ref[layer, 1], preferred_element_type=F32)
        total += jnp.dot(act_ref[pl.ds(base, TILE), :], taps_ref[layer, 0], preferred_element_type=F32)
        total += jnp.dot(act_ref[pl.ds(base + 2 * dilation, TILE), :], taps_ref[layer, 2], preferred_element_type=F32)
        conv_ref[pl.ds(base, TILE), :] = total
        return acc + fold(total)

    acc = lax.fori_loop(0, ROWS // TILE, tile, jnp.zeros((8, MID), F32))
    mean = jnp.sum(acc, axis=0, keepdims=True) * (1.0 / ROWS)
    put_stats(stats_ref, mean, deviations((conv_ref,), mean, MID))


def gated_tile(conv_ref, i, terms, gated_ref):
    mean, factor, bias = terms
    for c in range(TILE // CHUNK):
        v = conv_ref[pl.ds(pl.multiple_of(i * TILE + c * CHUNK, CHUNK), CHUNK), :]
        gated_ref[c * CHUNK : (c + 1) * CHUNK, :] = gelu((v - mean) * factor + bias).astype(BF16)
    return gated_ref[...]


def point_kernel(
    layer, got_ref, gain_ref, bias_ref, point_ref, conv_ref, x_ref, low_ref, mid_ref, high_ref, stats_ref, pool_ref, gated_ref
):
    terms = norm_terms(layer, got_ref, gain_ref, bias_ref)
    acc = jnp.zeros((8, CH), F32)
    start = 0
    regions = (low_ref, mid_ref, high_ref)
    for region in regions:
        count = region.shape[0] // TILE

        def tile(i, acc, region=region, start=start):
            gated = gated_tile(conv_ref, start + i, terms, gated_ref)
            branch = jnp.dot(gated, point_ref[layer], preferred_element_type=F32)
            total = x_ref[row_slice(start + i, TILE), :].astype(F32) + branch
            region[row_slice(i, TILE), :] = total
            pool_ref[row_slice(start + i, TILE // POOL), :] = jnp.sum(
                total.reshape(TILE // POOL, POOL, CH), axis=1
            )
            return acc + fold(total)

        acc = lax.fori_loop(0, count, tile, acc)
        start += count
    mean = jnp.sum(acc, axis=0, keepdims=True) * (1.0 / ROWS)
    put_stats(stats_ref, mean, deviations(regions, mean, CH))


def pool_kernel(
    layer, got_ref, gain_ref, bias_ref, point_ref, conv_ref, pool_ref, out_ref, gated_ref, sums_ref, flip_ref
):
    terms = norm_terms(layer, got_ref, gain_ref, bias_ref)
    bins = TILE // POOL
    row = lax.broadcasted_iota(jnp.int32, (bins, TILE), 0)
    col = lax.broadcasted_iota(jnp.int32, (bins, TILE), 1)
    pick = jnp.where(col // POOL == row, 1.0, 0.0).astype(BF16)

    def tile(i, carry):
        gated = gated_tile(conv_ref, i, terms, gated_ref)
        sums_ref[row_slice(i, bins), :] = jnp.dot(pick, gated, preferred_element_type=F32)
        return carry

    lax.fori_loop(0, ROWS // TILE, tile, 0)
    sums = sums_ref[...]
    upper = sums.astype(BF16)
    lower = (sums - upper.astype(F32)).astype(BF16)
    branch = jnp.dot(upper, point_ref[layer], preferred_element_type=F32)
    branch += jnp.dot(lower, point_ref[layer], preferred_element_type=F32)
    flipped = ((pool_ref[...] + branch) * (1.0 / POOL)).T
    size = CH // HEADS
    for k in range(ROWS // POOL // 128):
        half = flip_ref.at[k]
        for h in range(HEADS):
            half[pl.ds(h, size, stride=HEADS), :] = flipped[h * size : (h + 1) * size, 128 * k : 128 * (k + 1)]
        out_ref[:, 128 * k : 128 * (k + 1)] = half[...]


VMEM = pl.BlockSpec(memory_space=pltpu.VMEM)
SMEM = pl.BlockSpec(memory_space=pltpu.SMEM)
PARAMS = pltpu.CompilerParams(vmem_limit_bytes=20 * 1024 * 1024)


def call(body, args, outs, scratch=(), scalars=0):
    return pl.pallas_call(
        body,
        out_shape=[jax.ShapeDtypeStruct(s, d) for s, d in outs],
        in_specs=[SMEM] * scalars + [VMEM] * (len(args) - scalars),
        out_specs=[VMEM] * len(outs),
        scratch_shapes=[pltpu.VMEM(s, d) for s, d in scratch],
        compiler_params=PARAMS,
    )(*args)


def reduce_stats(sent):
    got = lax.all_to_all(sent, STAGES[0], 0, 0, tiled=True)
    rows = got.shape[1] // 2
    means = got[:, :rows]
    mean = jnp.mean(means, axis=0)
    spread = means - mean
    squares = jnp.sum(got[:, rows:], axis=0) + ROWS * jnp.sum(spread * spread, axis=0)
    both = jnp.concatenate([mean, squares])
    return lax.all_to_all(jnp.broadcast_to(both[None], sent.shape), STAGES[1], 0, 0, tiled=True)


def halos(low, high):
    up = [(i, i + 1) for i in range(lax.axis_size(SEQ) - 1)]
    down = [(j, i) for i, j in up]
    return lax.ppermute(high, SEQ, up), lax.ppermute(low, SEQ, down)


def per_device(inputs, taps, point, in_gain, in_bias, mid_gain, mid_bias):
    place = lax.axis_index(SEQ)
    flags = jnp.stack([place > 0, place < lax.axis_size(SEQ) - 1]).astype(jnp.int32)
    x = inputs.reshape(ROWS, CH)
    wide_stats = ((PEERS, 8, 128), F32)
    slim_stats = ((PEERS, 4, 128), F32)
    conv_shape = ((ROWS, MID), F32)
    edge = ((512, CH), F32)

    thin = ((256, CH), BF16)
    low, high, stats = call(input_stats, (x,), [thin, thin, wide_stats])
    before, after = halos(low, high)
    got = reduce_stats(stats)
    conv, stats = call(
        functools.partial(conv_kernel, 0, 256, 3),
        (flags, got, in_gain, in_bias, taps, before, x, after),
        [conv_shape, slim_stats],
        [((ROWS + 512, CH), BF16)],
        1,
    )
    got = reduce_stats(stats)
    low, mid, high, stats, pooled = call(
        functools.partial(point_kernel, 0),
        (got, mid_gain, mid_bias, point, conv, x),
        [edge, ((1024, CH), F32), edge, wide_stats, ((ROWS // POOL, CH), F32)],
        [((TILE, MID), BF16)],
    )
    before, after = halos(low, high)
    got = reduce_stats(stats)
    conv, stats = call(
        functools.partial(conv_kernel, 1, 512, 5),
        (flags, got, in_gain, in_bias, taps, before, low, mid, high, after),
        [conv_shape, slim_stats],
        [((ROWS + 1024, CH), BF16)],
        1,
    )
    got = reduce_stats(stats)
    (out,) = call(
        functools.partial(pool_kernel, 1),
        (got, mid_gain, mid_bias, point, conv, pooled),
        [((CH, ROWS // POOL), F32)],
        [((TILE, MID), BF16), ((ROWS // POOL, MID), F32), ((ROWS // POOL // 128, CH, 128), F32)],
    )
    bins = ROWS // POOL
    out = lax.all_to_all(out.reshape(CH // HEADS, HEADS, bins), SEQ, 0, 0, tiled=True)
    peers = lax.axis_size(SEQ)
    out = out.reshape(peers, -1, HEADS, bins).transpose(2, 1, 0, 3)
    return out.reshape(1, HEADS, -1, peers * bins)


def solution(mesh):
    fine = Mesh(mesh.devices.reshape(SIZES), NAMES)
    return jax.shard_map(
        per_device,
        mesh=fine,
        in_specs=(P(BATCH, SEQ, None), P(), P(), P(), P(), P(), P()),
        out_specs=P(BATCH, None, SEQ, None),
        check_vma=False,
    )
```

time: 201 us -> 161 us (0.80)
  waiting for transfers between devices: 39.5 us -> 7.71 us
  blocking collectives: 66.2 us -> 97 us
  other arithmetic: 25.2 us -> 0.38 us
  Pallas kernels: 0 us -> 19.8 us
  matrix products: 18.6 us -> 0 us
  starting transfers between devices: 41.3 us -> 29.8 us
  local copies, waits for them, and re-layouts: 9.16 us -> 5.13 us
    all_to_all x5 -> x7, blocking collectives: 66.2 us -> 97 us  [the longest x3 47.3 us: reduce_stats(): got = lax.all_to_all(sent, STAGES[0], 0, 0, tiled=True)]
    all_to_all x4 -> x2, waiting for transfers between devices: 28.3 us -> 7.69 us  [the longest x1 6.64 us: reduce_stats(): lax.all_to_all(jnp.broadcast_to(both[None], sent.shape), STAGES[1], 0, 0,...]
    convert_element_type x2 -> x1, other arithmetic: 20.4 us -> 0.08 us  [per_device(): jnp.stack([place > 0, place < lax.axis_size(SEQ) - 1]).astype(jnp.int32)]
    pallas_call x0 -> x5, Pallas kernels: none -> 19.8 us  [call(): pl.pallas_call(body, out_shape=[jax.ShapeDtypeStruct(s, d) for s, d in ou...]
    dot_general x8 -> x0, matrix products: 18.6 us -> none  [the longest x2 14.3 us: block(): jnp.dot(gated.reshape(seqs * rows, -1), point, preferred_element_type=jnp...]
    all_to_all x4 -> x2, starting transfers between devices: 28.1 us -> 16.7 us  [the longest x1 9.98 us: reduce_stats(): got = lax.all_to_all(sent, STAGES[0], 0, 0, tiled=True)]
    ppermute x4, waiting for transfers between devices: 11.2 us -> 0.01 us  [halos(): return (lax.ppermute(high, SEQ, up), lax.ppermute(low, SEQ, down))]
    reduce_sum x21 -> x8, other arithmetic: 4.54 us -> 0.21 us  [the longest x4 0.12 us: reduce_stats(): jnp.sum(spread * spread, axis=0)]
  transfers between devices with their start and end apart: 8 -> 6, of which waited for: 7 -> 2; matrix products, arithmetic and copies ran while one was open for 1% -> 1% of each run, Pallas kernels for 0% -> 0%
where the time goes in v2:
time: 161 us; the launch traced here: 160 us
  blocking collectives  97 us (60%)
  starting transfers between devices  29.8 us (19%)
  Pallas kernels  19.8 us (12%)
  waiting for transfers between devices  7.71 us (5%)
  local copies, waits for them, and re-layouts  5.13 us (3%)
    all_to_all x3, blocking collectives, reduce_stats(): got = lax.all_to_all(sent, STAGES[0], 0, 0, tiled=True)  47.3 us
    all_to_all x3, blocking collectives, reduce_stats(): lax.all_to_all(jnp.broadcast_to(both[None], sent.shape), STAGES[1], 0, 0,...  27.9 us
    all_to_all x1, blocking collectives, per_device(): lax.all_to_all(out.reshape(CH // HEADS, HEADS, bins), SEQ, 0, 0, tiled=True)  21.8 us
    pallas_call x5, Pallas kernels, call(): pl.pallas_call(body, out_shape=[jax.ShapeDtypeStruct(s, d) for s, d in ou...  19.8 us
    ppermute x4, starting transfers between devices, halos(): return (lax.ppermute(high, SEQ, up), lax.ppermute(low, SEQ, down))  13 us
    all_to_all x1, starting transfers between devices, reduce_stats(): got = lax.all_to_all(sent, STAGES[0], 0, 0, tiled=True)  9.98 us
    all_to_all x1, starting transfers between devices, reduce_stats(): lax.all_to_all(jnp.broadcast_to(both[None], sent.shape), STAGES[1], 0, 0,...  6.77 us
    all_to_all x1, waiting for transfers between devices, reduce_stats(): lax.all_to_all(jnp.broadcast_to(both[None], sent.shape), STAGES[1], 0, 0,...  6.64 us
  transfers between devices with their start and end apart: 6, of which 2 were waited for; matrix products, arithmetic and copies ran while one was open for 1% of the time, Pallas kernels for 0%

profile of v2, /device:TPU:1, one launch (start us, length us, event | category | flops | bytes accessed | tf_op | source)
XLA Modules:
  0.0 160.0 jit_solution(13916716111758627010)
XLA Ops:
  0.0 1.6 copy-done
  1.6 1.6 shard_map.73
  3.2 10.0 %all-to-all-start = ((f32[16,8,128]{2,1,0:T(8,128)}), f32[16,8,128]{2,1,0:T(8,128)S(1)}, u32[]{:S(2)}, u32[]{:S(2)}) async-start(f32[16,8,128]{2,1,0:T(8,128)} %get-tuple-element.17), calls=%async_computation | async-start | bytes 131072 | tf_op jit(solution)/shard_map/all_to_all | solution.py:201
  13.2 4.8 %collective-permute-start = (bf16[256,512]{1,0:T(8,128)(2,1)S(1)}, bf16[256,512]{1,0:T(8,128)(2,1)S(1)}, u32[]{:S(2)}, u32[]{:S(2)}) collective-permute-start(bf16[256,512]{1,0:T(8,128)(2,1)S(1)} %get-tuple-element.18), channel_id=1, source_target_pairs={{0,1},{1,2},{2,3},{3,4},{4,5},{5,6},{6,7},{7,8},{8,9},{9,10},{10,1... | collective-permute-start | bytes 786440 | tf_op jit(solution)/shard_map/ppermute | solution.py:214
  18.0 1.9 %collective-permute-start.1 = (bf16[256,512]{1,0:T(8,128)(2,1)S(1)}, bf16[256,512]{1,0:T(8,128)(2,1)S(1)}, u32[]{:S(2)}, u32[]{:S(2)}) collective-permute-start(bf16[256,512]{1,0:T(8,128)(2,1)S(1)} %get-tuple-element.19), channel_id=1, source_target_pairs={{1,0},{2,1},{3,2},{4,3},{5,4},{6,5},{7,6},{8,7},{9,8},{10,9},{11,1... | collective-permute-start | bytes 786440 | tf_op jit(solution)/shard_map/ppermute | solution.py:214
  19.9 1.1 all-to-all-done
  21.1 0.6 broadcast_in_dim.8
  21.7 6.8 %all-to-all-start.1 = ((f32[16,8,128]{2,1,0:T(8,128)}), f32[16,8,128]{2,1,0:T(8,128)S(1)}, u32[]{:S(2)}, u32[]{:S(2)}) async-start(f32[16,8,128]{2,1,0:T(8,128)} %broadcast_in_dim.8), calls=%async_computation.1 | async-start | bytes 131072 | tf_op jit(solution)/shard_map/all_to_all | solution.py:208
  28.5 0.0 copy-start.7
  28.5 0.1 add_convert_fusion.flag_ref
  28.6 6.6 %all-to-all-done.1.got_ref = f32[16,8,128]{2,1,0:T(8,128)S(1)} async-done(((f32[16,8,128]{2,1,0:T(8,128)}), f32[16,8,128]{2,1,0:T(8,128)S(1)}, u32[]{:S(2)}, u32[]{:S(2)}) %all-to-all-start.1) | async-done | bytes 65568 | tf_op jit(solution)/shard_map/all_to_all | solution.py:208
  35.2 0.0 collective-permute-done.refs_0_
  35.2 0.0 collective-permute-done.1.refs_2_
  35.2 0.0 copy-start.2
  35.2 1.4 copy-done.2
  36.7 6.3 %shard_map.74 = (f32[2048,256]{1,0:T(8,128)S(1)}, f32[16,4,128]{2,1,0:T(4,128)S(1)}) custom-call(s32[2]{0:T(128)S(1)} %add_convert_fusion.flag_ref, f32[16,8,128]{2,1,0:T(8,128)S(1)} %all-to-all-done.1.got_ref, f32[2,512]{1,0:T(2,128)S(1)} %copy-done.5, f32[2,512]{1,0:T(2,128)S(1)} %copy-done.6, bf16[2,3,512,256]{3,2,1,0:T(8,128)(2,1)S(1)} %copy-done.2, ...), custom_call_target="tpu_custom_call" | custom-call | tf_op jit(solution)/shard_map/pallas_call | solution.py:190
  42.9 15.6 %all_to_all.45 = f32[16,4,128]{2,1,0:T(4,128)S(1)} all-to-all(f32[16,4,128]{2,1,0:T(4,128)S(1)} %get-tuple-element.20), channel_id=1, replica_groups=mesh['y_lo'=2,'x'=4,'z'=8,'y_hi'=2,'core'=2] {'z','core'}, dimensions={0} | all-to-all | bytes 65536 | tf_op jit(solution)/shard_map/all_to_all | solution.py:201
  58.6 9.3 %all_to_all.46.got_ref = f32[16,4,128]{2,1,0:T(4,128)S(1)} all-to-all(f32[16,4,128]{2,1,0:T(4,128)S(1)} %broadcast_in_dim.9), channel_id=1, replica_groups=mesh['y_lo'=2,'x'=4,'z'=8,'y_hi'=2,'core'=2] {'y_lo','x','y_hi'}, dimensions={0} | all-to-all | bytes 65536 | tf_op jit(solution)/shard_map/all_to_all | solution.py:208
  67.9 0.0 copy-start.3
  68.0 3.3 %shard_map.75 = (f32[512,512]{1,0:T(8,128)S(1)}, f32[1024,512]{1,0:T(8,128)S(1)}, f32[512,512]{1,0:T(8,128)S(1)}, f32[16,8,128]{2,1,0:T(8,128)S(1)}, f32[256,512]{1,0:T(8,128)S(1)}) custom-call(f32[16,4,128]{2,1,0:T(4,128)S(1)} %all_to_all.46.got_ref, f32[2,256]{1,0:T(2,128)S(1)} %copy-done.7, f32[2,256]{1,0:T(2,128)S(1)} %copy-done.8, ...), custom_call_target="tpu_custom_call" | custom-call | tf_op jit(solution)/shard_map/pallas_call | solution.py:190
  71.2 4.4 %collective-permute-start.2 = (f32[512,512]{1,0:T(8,128)S(1)}, f32[512,512]{1,0:T(8,128)S(1)}, u32[]{:S(2)}, u32[]{:S(2)}) collective-permute-start(f32[512,512]{1,0:T(8,128)S(1)} %get-tuple-element.23.refs_3_), channel_id=1, source_target_pairs={{0,1},{1,2},{2,3},{3,4},{4,5},{5,6},{6,7},{7,8},{8,9},{9,10},{10,1... | collective-permute-start | bytes 3145736 | tf_op jit(solution)/shard_map/ppermute | solution.py:214
  75.6 1.9 %collective-permute-start.3 = (f32[512,512]{1,0:T(8,128)S(1)}, f32[512,512]{1,0:T(8,128)S(1)}, u32[]{:S(2)}, u32[]{:S(2)}) collective-permute-start(f32[512,512]{1,0:T(8,128)S(1)} %get-tuple-element.24.refs_1_), channel_id=1, source_target_pairs={{1,0},{2,1},{3,2},{4,3},{5,4},{6,5},{7,6},{8,7},{9,8},{10,9},{11,1... | collective-permute-start | bytes 3145736 | tf_op jit(solution)/shard_map/ppermute | solution.py:214
  77.6 17.5 %all_to_all.47 = f32[16,8,128]{2,1,0:T(8,128)S(1)} all-to-all(f32[16,8,128]{2,1,0:T(8,128)S(1)} %get-tuple-element.22), channel_id=1, replica_groups=mesh['y_lo'=2,'x'=4,'z'=8,'y_hi'=2,'core'=2] {'z','core'}, dimensions={0} | all-to-all | bytes 131072 | tf_op jit(solution)/shard_map/all_to_all | solution.py:201
  95.2 9.3 %all_to_all.48.got_ref = f32[16,8,128]{2,1,0:T(8,128)S(1)} all-to-all(f32[16,8,128]{2,1,0:T(8,128)S(1)} %broadcast_in_dim.10), channel_id=1, replica_groups=mesh['y_lo'=2,'x'=4,'z'=8,'y_hi'=2,'core'=2] {'y_lo','x','y_hi'}, dimensions={0} | all-to-all | bytes 131072 | tf_op jit(solution)/shard_map/all_to_all | solution.py:208
  104.5 0.0 collective-permute-done.2.refs_0_
  104.5 6.6 %shard_map.76 = (f32[2048,256]{1,0:T(8,128)S(1)}, f32[16,4,128]{2,1,0:T(4,128)S(1)}) custom-call(s32[2]{0:T(128)S(1)} %add_convert_fusion.flag_ref, f32[16,8,128]{2,1,0:T(8,128)S(1)} %all_to_all.48.got_ref, f32[2,512]{1,0:T(2,128)S(1)} %copy-done.5, f32[2,512]{1,0:T(2,128)S(1)} %copy-done.6, bf16[2,3,512,256]{3,2,1,0:T(8,128)(2,1)S(1)} %copy-done.3, ...), custom_call_target="tpu_custom_call" | custom-call | tf_op jit(solution)/shard_map/pallas_call | solution.py:190
  111.1 14.1 %all_to_all.49 = f32[16,4,128]{2,1,0:T(4,128)S(1)} all-to-all(f32[16,4,128]{2,1,0:T(4,128)S(1)} %get-tuple-element.26), channel_id=1, replica_groups=mesh['y_lo'=2,'x'=4,'z'=8,'y_hi'=2,'core'=2] {'z','core'}, dimensions={0} | all-to-all | bytes 65536 | tf_op jit(solution)/shard_map/all_to_all | solution.py:201
  125.3 9.4 %all_to_all.50.got_ref = f32[16,4,128]{2,1,0:T(4,128)S(1)} all-to-all(f32[16,4,128]{2,1,0:T(4,128)S(1)} %broadcast_in_dim.11), channel_id=1, replica_groups=mesh['y_lo'=2,'x'=4,'z'=8,'y_hi'=2,'core'=2] {'y_lo','x','y_hi'}, dimensions={0} | all-to-all | bytes 65536 | tf_op jit(solution)/shard_map/all_to_all | solution.py:208
  134.6 2.1 %shard_map.77 = f32[512,256]{1,0:T(8,128)S(1)} custom-call(f32[16,4,128]{2,1,0:T(4,128)S(1)} %all_to_all.50.got_ref, f32[2,256]{1,0:T(2,128)S(1)} %copy-done.7, f32[2,256]{1,0:T(2,128)S(1)} %copy-done.8, bf16[2,256,512]{2,1,0:T(8,128)(2,1)S(1)} %copy-done.4, f32[2048,256]{1,0:T(8,128)S(1)} %get-tuple-element.27.conv_ref, ...), custom_call_target="tpu_custom_call" | custom-call | tf_op jit(solution)/shard_map/pallas_call | solution.py:190
  136.7 21.8 %all_to_all.51 = f32[64,8,256]{2,1,0:T(8,128)S(1)} all-to-all(f32[64,8,256]{2,1,0:T(8,128)S(1)} %bitcast.13), channel_id=1, replica_groups=mesh['y_lo'=2,'x'=4,'z'=8,'y_hi'=2,'core'=2] {'z','y_hi','core'}, dimensions={0} | all-to-all | bytes 1048576 | tf_op jit(solution)/shard_map/all_to_all | solution.py:261
  158.6 0.3 copy.10
  158.9 1.1 reshape.31
  (37 shorter events, 0.3 us)
Async XLA Ops:
  0.0 1.6 copy-start
  1.6 33.6 %copy-start.1 = (bf16[1,2048,512]{2,1,0:T(8,128)(2,1)S(1)}, bf16[1,2048,512]{2,1,0:T(8,128)(2,1)}, u32[]{:S(2)}) copy-start(bf16[1,2048,512]{2,1,0:T(8,128)(2,1)} %param.7) | copy-start | bytes 6291460
  1.6 33.6 %copy-start.5 = (f32[2,512]{1,0:T(2,128)S(1)}, f32[2,512]{1,0:T(2,128)}, u32[]{:S(2)}) copy-start(f32[2,512]{1,0:T(2,128)} %gain_ref.6) | copy-start | bytes 12292
  1.6 33.6 %copy-start.6 = (f32[2,512]{1,0:T(2,128)S(1)}, f32[2,512]{1,0:T(2,128)}, u32[]{:S(2)}) copy-start(f32[2,512]{1,0:T(2,128)} %bias_ref.6) | copy-start | bytes 12292
  3.2 17.8 %all-to-all-start = ((f32[16,8,128]{2,1,0:T(8,128)}), f32[16,8,128]{2,1,0:T(8,128)S(1)}, u32[]{:S(2)}, u32[]{:S(2)}) async-start(f32[16,8,128]{2,1,0:T(8,128)} %get-tuple-element.17), calls=%async_computation | async-start | bytes 131072 | tf_op jit(solution)/shard_map/all_to_all | solution.py:201
  13.2 22.0 %collective-permute-start = (bf16[256,512]{1,0:T(8,128)(2,1)S(1)}, bf16[256,512]{1,0:T(8,128)(2,1)S(1)}, u32[]{:S(2)}, u32[]{:S(2)}) collective-permute-start(bf16[256,512]{1,0:T(8,128)(2,1)S(1)} %get-tuple-element.18), channel_id=1, source_target_pairs={{0,1},{1,2},{2,3},{3,4},{4,5},{5,6},{6,7},{7,8},{8,9},{9,10},{10,1... | collective-permute-start | bytes 786440 | tf_op jit(solution)/shard_map/ppermute | solution.py:214
  18.0 17.2 %collective-permute-start.1 = (bf16[256,512]{1,0:T(8,128)(2,1)S(1)}, bf16[256,512]{1,0:T(8,128)(2,1)S(1)}, u32[]{:S(2)}, u32[]{:S(2)}) collective-permute-start(bf16[256,512]{1,0:T(8,128)(2,1)S(1)} %get-tuple-element.19), channel_id=1, source_target_pairs={{1,0},{2,1},{3,2},{4,3},{5,4},{6,5},{7,6},{8,7},{9,8},{10,9},{11,1... | collective-permute-start | bytes 786440 | tf_op jit(solution)/shard_map/ppermute | solution.py:214
  21.7 13.5 %all-to-all-start.1 = ((f32[16,8,128]{2,1,0:T(8,128)}), f32[16,8,128]{2,1,0:T(8,128)S(1)}, u32[]{:S(2)}, u32[]{:S(2)}) async-start(f32[16,8,128]{2,1,0:T(8,128)} %broadcast_in_dim.8), calls=%async_computation.1 | async-start | bytes 131072 | tf_op jit(solution)/shard_map/all_to_all | solution.py:208
  28.5 39.5 %copy-start.7 = (f32[2,256]{1,0:T(2,128)S(1)}, f32[2,256]{1,0:T(2,128)}, u32[]{:S(2)}) copy-start(f32[2,256]{1,0:T(2,128)} %gain_ref.7) | copy-start | bytes 6148
  35.2 1.4 copy-start.2
  36.6 31.3 %copy-start.4 = (bf16[2,256,512]{2,1,0:T(8,128)(2,1)S(1)}, bf16[2,256,512]{2,1,0:T(8,128)(2,1)}, u32[]{:S(2)}) copy-start(bf16[2,256,512]{2,1,0:T(8,128)(2,1)} %point_ref.3) | copy-start | bytes 1572868
  36.7 31.3 %copy-start.8 = (f32[2,256]{1,0:T(2,128)S(1)}, f32[2,256]{1,0:T(2,128)}, u32[]{:S(2)}) copy-start(f32[2,256]{1,0:T(2,128)} %bias_ref.7) | copy-start | bytes 6148
  67.9 36.5 %copy-start.3 = (bf16[2,3,512,256]{3,2,1,0:T(8,128)(2,1)S(1)}, bf16[2,3,512,256]{3,2,1,0:T(8,128)(2,1)}, u32[]{:S(2)}) copy-start(bf16[2,3,512,256]{3,2,1,0:T(8,128)(2,1)} %taps_ref.3) | copy-start | bytes 4718596
  71.2 33.2 %collective-permute-start.2 = (f32[512,512]{1,0:T(8,128)S(1)}, f32[512,512]{1,0:T(8,128)S(1)}, u32[]{:S(2)}, u32[]{:S(2)}) collective-permute-start(f32[512,512]{1,0:T(8,128)S(1)} %get-tuple-element.23.refs_3_), channel_id=1, source_target_pairs={{0,1},{1,2},{2,3},{3,4},{4,5},{5,6},{6,7},{7,8},{8,9},{9,10},{10,1... | collective-permute-start | bytes 3145736 | tf_op jit(solution)/shard_map/ppermute | solution.py:214
  75.6 28.8 %collective-permute-start.3 = (f32[512,512]{1,0:T(8,128)S(1)}, f32[512,512]{1,0:T(8,128)S(1)}, u32[]{:S(2)}, u32[]{:S(2)}) collective-permute-start(f32[512,512]{1,0:T(8,128)S(1)} %get-tuple-element.24.refs_1_), channel_id=1, source_target_pairs={{1,0},{2,1},{3,2},{4,3},{5,4},{6,5},{7,6},{8,7},{9,8},{10,9},{11,1... | collective-permute-start | bytes 3145736 | tf_op jit(solution)/shard_map/ppermute | solution.py:214

commit v3 on v2

v3 whole, which is shorter than its diff:
```python
import functools

import jax
import jax.numpy as jnp
from jax import lax
from jax.experimental import pallas as pl
from jax.experimental.pallas import tpu as pltpu
from jax.sharding import Mesh, PartitionSpec as P

EPS = 1e-05
HEADS = 8
POOL = 8
ROWS = 2048
CH = 512
MID = 256
TILE = 256
CHUNK = 32
NEAR = 256
FAR = 512

NAMES = ("y_lo", "x", "z", "y_hi", "core")
SIZES = (2, 4, 8, 2, 2)
BATCH = ("y_lo", "x")
SEQ = ("z", "y_hi", "core")
ACROSS = ("y_lo", "x", "y_hi")
ALONG = ("z", "core")
PEERS = 16
F32 = jnp.float32
BF16 = jnp.bfloat16


def gelu(u):
    return 0.5 * u * (1.0 + lax.erf(u * 0.7071067811865476))


def wide(v):
    return jnp.concatenate([v[j : j + 1] for j in range(v.shape[0])], axis=1)


def norm_terms(layer, got_ref, gain_ref, bias_ref):
    rows = got_ref.shape[1] // 2
    got = got_ref[...]
    means = got[:, :rows]
    mean = jnp.sum(means, axis=0) * (1.0 / PEERS)
    spread = means - mean
    total = jnp.sum(got[:, rows:], axis=0) + (PEERS * ROWS) * jnp.sum(spread * spread, axis=0)
    variance = wide(total) * (1.0 / (PEERS * PEERS * ROWS))
    return wide(mean), gain_ref[layer : layer + 1] * lax.rsqrt(variance + EPS), bias_ref[layer : layer + 1]


def fold(v):
    return jnp.sum(v.reshape(-1, 8, v.shape[-1]), axis=0)


def put_stats(out_ref, mean, squares):
    rows = out_ref.shape[1] // 2
    for j in range(rows):
        for base, v in ((0, mean), (rows, squares)):
            piece = v[:, 128 * j : 128 * (j + 1)].reshape(1, 1, 128)
            out_ref[:, base + j : base + j + 1, :] = jnp.broadcast_to(piece, (PEERS, 1, 128))


def row_slice(i, size):
    return pl.ds(pl.multiple_of(i * size, size), size)


def deviations(refs, mean, channels):
    squares = jnp.zeros((8, channels), F32)
    for ref in refs:

        def step(i, acc, ref=ref):
            d = ref[row_slice(i, 64), :].astype(F32) - mean
            return acc + fold(d * d)

        squares = lax.fori_loop(0, ref.shape[0] // 64, step, squares, unroll=4)
    return jnp.sum(squares, axis=0, keepdims=True)


def input_stats(place_ref, x_ref, facing_ref, outer_ref, out_ref):
    put_edges(place_ref[0], x_ref, facing_ref, outer_ref)

    def step(i, acc):
        return acc + fold(x_ref[row_slice(i, 64), :].astype(F32))

    acc = lax.fori_loop(0, ROWS // 64, step, jnp.zeros((8, CH), F32), unroll=4)
    mean = jnp.sum(acc, axis=0, keepdims=True) * (1.0 / ROWS)
    put_stats(out_ref, mean, deviations((x_ref,), mean, CH))


def activate(piece, first, count, terms, act_ref, offset, flag=None):
    mean, factor, bias = terms

    def step(i, carry):
        v = piece[pl.ds(pl.multiple_of(first + i * CHUNK, CHUNK), CHUNK), :].astype(F32)
        a = gelu((v - mean) * factor + bias)
        if flag is not None:
            a = jnp.where(flag > 0, a, 0.0)
        act_ref[pl.ds(pl.multiple_of(offset + i * CHUNK, CHUNK), CHUNK), :] = a.astype(BF16)
        return carry

    lax.fori_loop(0, count // CHUNK, step, 0)


def convolve(layer, dilation, act_ref, taps_ref, conv_ref, first, count, acc):
    def tile(i, acc):
        base = pl.multiple_of(first + i * TILE, TILE)
        total = jnp.dot(act_ref[pl.ds(base + dilation, TILE), :], taps_ref[layer, 1], preferred_element_type=F32)
        total += jnp.dot(act_ref[pl.ds(base, TILE), :], taps_ref[layer, 0], preferred_element_type=F32)
        total += jnp.dot(act_ref[pl.ds(base + 2 * dilation, TILE), :], taps_ref[layer, 2], preferred_element_type=F32)
        conv_ref[pl.ds(base, TILE), :] = total
        return acc + fold(total)

    return lax.fori_loop(0, count // TILE, tile, acc)


def conv_stats(acc, center, stats_ref):
    mean = jnp.sum(acc, axis=0, keepdims=True) * (1.0 / ROWS)
    put_stats(stats_ref, mean, deviations((center,), mean, MID))


def conv_kernel(
    layer,
    dilation,
    place_ref,
    got_ref,
    gain_ref,
    bias_ref,
    taps_ref,
    near_ref,
    center_ref,
    cross_ref,
    conv_ref,
    stats_ref,
    act_ref,
):
    terms = norm_terms(layer, got_ref, gain_ref, bias_ref)
    core = place_ref[0]
    activate(near_ref, 0, dilation, terms, act_ref, (1 - core) * (dilation + ROWS))
    activate(center_ref, 0, ROWS, terms, act_ref, dilation)
    activate(cross_ref, 0, dilation, terms, act_ref, core * (dilation + ROWS), place_ref[1])
    acc = convolve(layer, dilation, act_ref, taps_ref, conv_ref, 0, ROWS, jnp.zeros((8, MID), F32))
    conv_stats(acc, conv_ref, stats_ref)


def put_edges(core, rows_ref, facing_ref, outer_ref):
    size = facing_ref.shape[0]
    last = ROWS - size
    facing_ref[...] = rows_ref[pl.ds(pl.multiple_of((1 - core) * last, 256), size), :]
    outer_ref[...] = rows_ref[pl.ds(pl.multiple_of(core * last, 256), size), :]


def gated_tile(conv_ref, i, terms, gated_ref):
    mean, factor, bias = terms
    for c in range(TILE // CHUNK):
        v = conv_ref[pl.ds(pl.multiple_of(i * TILE + c * CHUNK, CHUNK), CHUNK), :]
        gated_ref[c * CHUNK : (c + 1) * CHUNK, :] = gelu((v - mean) * factor + bias).astype(BF16)
    return gated_ref[...]


def point_kernel(
    place_ref,
    got_ref,
    gain_ref,
    bias_ref,
    point_ref,
    conv_ref,
    x_ref,
    stream_ref,
    facing_ref,
    outer_ref,
    stats_ref,
    pool_ref,
    gated_ref,
):
    terms = norm_terms(0, got_ref, gain_ref, bias_ref)

    def tile(i, acc):
        gated = gated_tile(conv_ref, i, terms, gated_ref)
        branch = jnp.dot(gated, point_ref[0], preferred_element_type=F32)
        total = x_ref[row_slice(i, TILE), :].astype(F32) + branch
        stream_ref[row_slice(i, TILE), :] = total
        pool_ref[row_slice(i, TILE // POOL), :] = jnp.sum(total.reshape(TILE // POOL, POOL, CH), axis=1)
        return acc + fold(total)

    acc = lax.fori_loop(0, ROWS // TILE, tile, jnp.zeros((8, CH), F32))
    put_edges(place_ref[0], stream_ref, facing_ref, outer_ref)
    mean = jnp.sum(acc, axis=0, keepdims=True) * (1.0 / ROWS)
    put_stats(stats_ref, mean, deviations((stream_ref,), mean, CH))


def pool_kernel(
    got_ref, gain_ref, bias_ref, point_ref, conv_ref, pool_ref, out_ref, gated_ref, sums_ref, flip_ref
):
    terms = norm_terms(1, got_ref, gain_ref, bias_ref)
    bins = TILE // POOL
    row = lax.broadcasted_iota(jnp.int32, (bins, TILE), 0)
    col = lax.broadcasted_iota(jnp.int32, (bins, TILE), 1)
    pick = jnp.where(col // POOL == row, 1.0, 0.0).astype(BF16)

    def tile(i, carry):
        gated = gated_tile(conv_ref, i, terms, gated_ref)
        sums_ref[row_slice(i, bins), :] = jnp.dot(pick, gated, preferred_element_type=F32)
        return carry

    lax.fori_loop(0, ROWS // TILE, tile, 0)
    sums = sums_ref[...]
    upper = sums.astype(BF16)
    lower = (sums - upper.astype(F32)).astype(BF16)
    branch = jnp.dot(upper, point_ref[1], preferred_element_type=F32)
    branch += jnp.dot(lower, point_ref[1], preferred_element_type=F32)
    flipped = ((pool_ref[...] + branch) * (1.0 / POOL)).T
    size = CH // HEADS
    for k in range(ROWS // POOL // 128):
        half = flip_ref.at[k]
        for h in range(HEADS):
            half[pl.ds(h, size, stride=HEADS), :] = flipped[h * size : (h + 1) * size, 128 * k : 128 * (k + 1)]
        out_ref[:, 128 * k : 128 * (k + 1)] = half[...]


VMEM = pl.BlockSpec(memory_space=pltpu.VMEM)
SMEM = pl.BlockSpec(memory_space=pltpu.SMEM)
PARAMS = pltpu.CompilerParams(vmem_limit_bytes=20 * 1024 * 1024)


def call(body, args, outs, scratch=(), scalars=0):
    return pl.pallas_call(
        body,
        out_shape=[jax.ShapeDtypeStruct(s, d) for s, d in outs],
        in_specs=[SMEM] * scalars + [VMEM] * (len(args) - scalars),
        out_specs=[VMEM] * len(outs),
        scratch_shapes=[pltpu.VMEM(s, d) for s, d in scratch],
        compiler_params=PARAMS,
    )(*args)


def reduce_stats(sent, first, second):
    got = lax.all_to_all(sent, first, 0, 0, tiled=True)
    rows = got.shape[1] // 2
    means = got[:, :rows]
    mean = jnp.mean(means, axis=0)
    spread = means - mean
    squares = jnp.sum(got[:, rows:], axis=0) + ROWS * jnp.sum(spread * spread, axis=0)
    both = jnp.concatenate([mean, squares])
    return lax.all_to_all(jnp.broadcast_to(both[None], sent.shape), second, 0, 0, tiled=True)


def halos(facing, outer):
    peers = lax.axis_size(SEQ)
    near = lax.ppermute(facing, SEQ, [(i, i ^ 1) for i in range(peers)])
    pairs = [(i, i + 1) for i in range(1, peers - 1, 2)]
    return near, lax.ppermute(outer, SEQ, pairs + [(j, i) for i, j in pairs])


def per_device(inputs, taps, point, in_gain, in_bias, mid_gain, mid_bias):
    place = lax.axis_index(SEQ)
    core = lax.axis_index("core")
    joined = jnp.where(core == 0, place > 0, place < lax.axis_size(SEQ) - 1)
    where = jnp.stack([core, joined.astype(core.dtype)]).astype(jnp.int32)
    x = inputs.reshape(ROWS, CH)
    wide_stats = ((PEERS, 8, 128), F32)
    slim_stats = ((PEERS, 4, 128), F32)
    conv_outs = [((ROWS, MID), F32), slim_stats]

    edge = ((NEAR, CH), BF16)
    facing, outer, stats = call(input_stats, (where, x), [edge, edge, wide_stats], scalars=1)
    near, cross = halos(facing, outer)
    got = reduce_stats(stats, ACROSS, ALONG)
    conv, stats = call(
        functools.partial(conv_kernel, 0, NEAR),
        (where, got, in_gain, in_bias, taps, near, x, cross),
        conv_outs,
        [((ROWS + 2 * NEAR, CH), BF16)],
        1,
    )
    got = reduce_stats(stats, ACROSS, ALONG)
    edge = ((FAR, CH), F32)
    stream, facing, outer, stats, pooled = call(
        point_kernel,
        (where, got, mid_gain, mid_bias, point, conv, x),
        [((ROWS, CH), F32), edge, edge, wide_stats, ((ROWS // POOL, CH), F32)],
        [((TILE, MID), BF16)],
        1,
    )
    near, cross = halos(facing, outer)
    got = reduce_stats(stats, ALONG, ACROSS)
    conv, stats = call(
        functools.partial(conv_kernel, 1, FAR),
        (where, got, in_gain, in_bias, taps, near, stream, cross),
        conv_outs,
        [((ROWS + 2 * FAR, CH), BF16)],
        1,
    )
    got = reduce_stats(stats, ACROSS, ALONG)
    (out,) = call(
        pool_kernel,
        (got, mid_gain, mid_bias, point, conv, pooled),
        [((CH, ROWS // POOL), F32)],
        [((TILE, MID), BF16), ((ROWS // POOL, MID), F32), ((ROWS // POOL // 128, CH, 128), F32)],
    )
    bins = ROWS // POOL
    out = lax.all_to_all(out.reshape(CH // HEADS, HEADS, bins), SEQ, 0, 0, tiled=True)
    peers = lax.axis_size(SEQ)
    out = out.reshape(peers, -1, HEADS, bins).transpose(2, 1, 0, 3)
    return out.reshape(1, HEADS, -1, peers * bins)


def solution(mesh):
    fine = Mesh(mesh.devices.reshape(SIZES), NAMES)
    return jax.shard_map(
        per_device,
        mesh=fine,
        in_specs=(P(BATCH, SEQ, None), P(), P(), P(), P(), P(), P()),
        out_specs=P(BATCH, None, SEQ, None),
        check_vma=False,
    )
```

time: 161 us -> 154 us (0.957)
  starting transfers between devices: 29.8 us -> 16.6 us
  blocking collectives: 97 us -> 110 us
  waiting for transfers between devices: 7.71 us -> 0.83 us
    all_to_all x6 -> x7, blocking collectives: 75.2 us -> 90 us  [the longest x4 54.7 us: reduce_stats(): lax.all_to_all(jnp.broadcast_to(both[None], sent.shape), second, 0, 0, ti...]
    all_to_all x2 -> x1, starting transfers between devices: 16.7 us -> 7.58 us  [reduce_stats(): got = lax.all_to_all(sent, first, 0, 0, tiled=True)]
    all_to_all x2 -> x1, waiting for transfers between devices: 7.69 us -> 0.82 us  [reduce_stats(): got = lax.all_to_all(sent, first, 0, 0, tiled=True)]
    ppermute x4, starting transfers between devices: 13 us -> 9.05 us  [the longest x2 7.52 us: halos(): return (near, lax.ppermute(outer, SEQ, pairs + [(j, i) for i, j in pairs]))]
  transfers between devices with their start and end apart: 6 -> 5, of which waited for: 2 -> 1; matrix products, arithmetic and copies ran while one was open for 1% -> 0% of each run, Pallas kernels for 0% -> 0%
where the time goes in v3:
time: 154 us
  blocking collectives  110 us (71%)
  Pallas kernels  20.9 us (14%)
  starting transfers between devices  16.6 us (11%)
  local copies, waits for them, and re-layouts  4.5 us (3%)
    all_to_all x4, blocking collectives, reduce_stats(): lax.all_to_all(jnp.broadcast_to(both[None], sent.shape), second, 0, 0, ti...  54.7 us
    all_to_all x3, blocking collectives, reduce_stats(): got = lax.all_to_all(sent, first, 0, 0, tiled=True)  35.3 us
    pallas_call x5, Pallas kernels, call(): pl.pallas_call(body, out_shape=[jax.ShapeDtypeStruct(s, d) for s, d in ou...  20.9 us
    all_to_all x1, blocking collectives, per_device(): lax.all_to_all(out.reshape(CH // HEADS, HEADS, bins), SEQ, 0, 0, tiled=True)  20.4 us
    all_to_all x1, starting transfers between devices, reduce_stats(): got = lax.all_to_all(sent, first, 0, 0, tiled=True)  7.58 us
    ppermute x2, starting transfers between devices, halos(): return (near, lax.ppermute(outer, SEQ, pairs + [(j, i) for i, j in pairs]))  7.52 us
  transfers between devices with their start and end apart: 5, of which 1 were waited for; matrix products, arithmetic and copies ran while one was open for 0% of the time, Pallas kernels for 0%

profile of v3, /device:TPU:1, one launch (start us, length us, event | category | flops | bytes accessed | tf_op | source)
XLA Modules:
  0.0 153.9 jit_solution(6970670274265166187)
XLA Ops:
  0.0 0.1 pad_add_fusion.place_ref
  0.1 1.6 %copy-done = bf16[1,2048,512]{2,1,0:T(8,128)(2,1)S(1)} copy-done((bf16[1,2048,512]{2,1,0:T(8,128)(2,1)S(1)}, bf16[1,2048,512]{2,1,0:T(8,128)(2,1)}, u32[]{:S(2)}) %copy-start) | copy-done | bytes 2097176
  1.7 2.1 %shard_map.73 = (bf16[256,512]{1,0:T(8,128)(2,1)S(1)}, bf16[256,512]{1,0:T(8,128)(2,1)S(1)}, f32[16,8,128]{2,1,0:T(8,128)}) custom-call(s32[2]{0:T(128)S(1)} %pad_add_fusion.place_ref, bf16[2048,512]{1,0:T(8,128)(2,1)S(1)} %bitcast.10), custom_call_target="tpu_custom_call" | custom-call | tf_op jit(solution)/shard_map/pallas_call | solution.py:226
  3.8 7.6 %all-to-all-start = ((f32[16,8,128]{2,1,0:T(8,128)}), f32[16,8,128]{2,1,0:T(8,128)S(1)}, u32[]{:S(2)}, u32[]{:S(2)}) async-start(f32[16,8,128]{2,1,0:T(8,128)} %get-tuple-element.17), calls=%async_computation | async-start | bytes 131072 | tf_op jit(solution)/shard_map/all_to_all | solution.py:237
  11.4 1.0 collective-permute-start
  12.4 4.9 %collective-permute-start.1 = (bf16[256,512]{1,0:T(8,128)(2,1)S(1)}, bf16[256,512]{1,0:T(8,128)(2,1)S(1)}, u32[]{:S(2)}, u32[]{:S(2)}) collective-permute-start(bf16[256,512]{1,0:T(8,128)(2,1)S(1)} %get-tuple-element.19), channel_id=1, source_target_pairs={{1,2},{3,4},{5,6},{7,8},{9,10},{11,12},{13,14},{15,16},{17,18},{19... | collective-permute-start | bytes 786440 | tf_op jit(solution)/shard_map/ppermute | solution.py:251
  17.3 0.8 all-to-all-done
  18.2 0.0 copy-start.7
  18.2 0.0 copy-start.8
  18.3 18.2 %all_to_all.45.got_ref = f32[16,8,128]{2,1,0:T(8,128)S(1)} all-to-all(f32[16,8,128]{2,1,0:T(8,128)S(1)} %broadcast_in_dim.8), channel_id=1, replica_groups=mesh['y_lo'=2,'x'=4,'z'=8,'y_hi'=2,'core'=2] {'z','core'}, dimensions={0} | all-to-all | bytes 131072 | tf_op jit(solution)/shard_map/all_to_all | solution.py:244
  36.4 0.0 collective-permute-done.near_ref
  36.5 0.0 collective-permute-done.1.cross_ref
  36.5 0.0 copy-start.2
  36.5 1.4 copy-done.2
  37.9 6.2 %shard_map.74 = (f32[2048,256]{1,0:T(8,128)S(1)}, f32[16,4,128]{2,1,0:T(4,128)S(1)}) custom-call(s32[2]{0:T(128)S(1)} %pad_add_fusion.place_ref, f32[16,8,128]{2,1,0:T(8,128)S(1)} %all_to_all.45.got_ref, f32[2,512]{1,0:T(2,128)S(1)} %copy-done.5, f32[2,512]{1,0:T(2,128)S(1)} %copy-done.6, bf16[2,3,512,256]{3,2,1,0:T(8,128)(2,1)S(1)} %copy-done.2, ...), custom_call_target="tpu_custom_call" | custom-call | tf_op jit(solution)/shard_map/pallas_call | solution.py:226
  44.1 9.3 %all_to_all.46 = f32[16,4,128]{2,1,0:T(4,128)S(1)} all-to-all(f32[16,4,128]{2,1,0:T(4,128)S(1)} %get-tuple-element.20), channel_id=1, replica_groups=mesh['y_lo'=2,'x'=4,'z'=8,'y_hi'=2,'core'=2] {'y_lo','x','y_hi'}, dimensions={0} | all-to-all | bytes 65536 | tf_op jit(solution)/shard_map/all_to_all | solution.py:237
  53.5 11.5 %all_to_all.47.got_ref = f32[16,4,128]{2,1,0:T(4,128)S(1)} all-to-all(f32[16,4,128]{2,1,0:T(4,128)S(1)} %broadcast_in_dim.9), channel_id=1, replica_groups=mesh['y_lo'=2,'x'=4,'z'=8,'y_hi'=2,'core'=2] {'z','core'}, dimensions={0} | all-to-all | bytes 65536 | tf_op jit(solution)/shard_map/all_to_all | solution.py:244
  65.0 0.0 copy-start.3
  65.0 3.9 %shard_map.75 = (f32[2048,512]{1,0:T(8,128)S(1)}, f32[512,512]{1,0:T(8,128)S(1)}, f32[512,512]{1,0:T(8,128)S(1)}, f32[16,8,128]{2,1,0:T(8,128)S(1)}, f32[256,512]{1,0:T(8,128)S(1)}) custom-call(s32[2]{0:T(128)S(1)} %pad_add_fusion.place_ref, f32[16,4,128]{2,1,0:T(4,128)S(1)} %all_to_all.47.got_ref, f32[2,256]{1,0:T(2,128)S(1)} %copy-done.7, ...), custom_call_target="tpu_custom_call" | custom-call | tf_op jit(solution)/shard_map/pallas_call | solution.py:226
  69.0 0.5 collective-permute-start.2
  69.4 2.7 %collective-permute-start.3 = (f32[512,512]{1,0:T(8,128)S(1)}, f32[512,512]{1,0:T(8,128)S(1)}, u32[]{:S(2)}, u32[]{:S(2)}) collective-permute-start(f32[512,512]{1,0:T(8,128)S(1)} %get-tuple-element.25), channel_id=1, source_target_pairs={{1,2},{3,4},{5,6},{7,8},{9,10},{11,12},{13,14},{15,16},{17,18},{19... | collective-permute-start | bytes 3145736 | tf_op jit(solution)/shard_map/ppermute | solution.py:251
  72.1 15.5 %all_to_all.48 = f32[16,8,128]{2,1,0:T(8,128)S(1)} all-to-all(f32[16,8,128]{2,1,0:T(8,128)S(1)} %get-tuple-element.22), channel_id=1, replica_groups=mesh['y_lo'=2,'x'=4,'z'=8,'y_hi'=2,'core'=2] {'z','core'}, dimensions={0} | all-to-all | bytes 131072 | tf_op jit(solution)/shard_map/all_to_all | solution.py:237
  87.7 9.7 %all_to_all.49.got_ref = f32[16,8,128]{2,1,0:T(8,128)S(1)} all-to-all(f32[16,8,128]{2,1,0:T(8,128)S(1)} %broadcast_in_dim.10), channel_id=1, replica_groups=mesh['y_lo'=2,'x'=4,'z'=8,'y_hi'=2,'core'=2] {'y_lo','x','y_hi'}, dimensions={0} | all-to-all | bytes 131072 | tf_op jit(solution)/shard_map/all_to_all | solution.py:244
  97.4 0.0 collective-permute-done.2.near_ref
  97.4 0.0 collective-permute-done.3.cross_ref
  97.4 6.5 %shard_map.76 = (f32[2048,256]{1,0:T(8,128)S(1)}, f32[16,4,128]{2,1,0:T(4,128)S(1)}) custom-call(s32[2]{0:T(128)S(1)} %pad_add_fusion.place_ref, f32[16,8,128]{2,1,0:T(8,128)S(1)} %all_to_all.49.got_ref, f32[2,512]{1,0:T(2,128)S(1)} %copy-done.5, f32[2,512]{1,0:T(2,128)S(1)} %copy-done.6, bf16[2,3,512,256]{3,2,1,0:T(8,128)(2,1)S(1)} %copy-done.3, ...), custom_call_target="tpu_custom_call" | custom-call | tf_op jit(solution)/shard_map/pallas_call | solution.py:226
  104.0 10.5 %all_to_all.50 = f32[16,4,128]{2,1,0:T(4,128)S(1)} all-to-all(f32[16,4,128]{2,1,0:T(4,128)S(1)} %get-tuple-element.26), channel_id=1, replica_groups=mesh['y_lo'=2,'x'=4,'z'=8,'y_hi'=2,'core'=2] {'y_lo','x','y_hi'}, dimensions={0} | all-to-all | bytes 65536 | tf_op jit(solution)/shard_map/all_to_all | solution.py:237
  114.5 15.4 %all_to_all.51.got_ref = f32[16,4,128]{2,1,0:T(4,128)S(1)} all-to-all(f32[16,4,128]{2,1,0:T(4,128)S(1)} %broadcast_in_dim.11), channel_id=1, replica_groups=mesh['y_lo'=2,'x'=4,'z'=8,'y_hi'=2,'core'=2] {'z','core'}, dimensions={0} | all-to-all | bytes 65536 | tf_op jit(solution)/shard_map/all_to_all | solution.py:244
  129.9 2.1 %shard_map.77 = f32[512,256]{1,0:T(8,128)S(1)} custom-call(f32[16,4,128]{2,1,0:T(4,128)S(1)} %all_to_all.51.got_ref, f32[2,256]{1,0:T(2,128)S(1)} %copy-done.7, f32[2,256]{1,0:T(2,128)S(1)} %copy-done.8, bf16[2,256,512]{2,1,0:T(8,128)(2,1)S(1)} %copy-done.4, f32[2048,256]{1,0:T(8,128)S(1)} %get-tuple-element.27.conv_ref, ...), custom_call_target="tpu_custom_call" | custom-call | tf_op jit(solution)/shard_map/pallas_call | solution.py:226
  132.0 20.4 %all_to_all.52 = f32[64,8,256]{2,1,0:T(8,128)S(1)} all-to-all(f32[64,8,256]{2,1,0:T(8,128)S(1)} %bitcast.13), channel_id=1, replica_groups=mesh['y_lo'=2,'x'=4,'z'=8,'y_hi'=2,'core'=2] {'z','y_hi','core'}, dimensions={0} | all-to-all | bytes 1048576 | tf_op jit(solution)/shard_map/all_to_all | solution.py:301
  152.4 0.3 copy.10
  152.7 1.1 reshape.31
  (36 shorter events, 0.3 us)
Async XLA Ops:
  0.0 36.5 %copy-start.6 = (f32[2,512]{1,0:T(2,128)S(1)}, f32[2,512]{1,0:T(2,128)}, u32[]{:S(2)}) copy-start(f32[2,512]{1,0:T(2,128)} %bias_ref.6) | copy-start | bytes 12292
  0.0 36.5 %copy-start.5 = (f32[2,512]{1,0:T(2,128)S(1)}, f32[2,512]{1,0:T(2,128)}, u32[]{:S(2)}) copy-start(f32[2,512]{1,0:T(2,128)} %gain_ref.6) | copy-start | bytes 12292
  0.1 1.6 %copy-start = (bf16[1,2048,512]{2,1,0:T(8,128)(2,1)S(1)}, bf16[1,2048,512]{2,1,0:T(8,128)(2,1)}, u32[]{:S(2)}) copy-start(bf16[1,2048,512]{2,1,0:T(8,128)(2,1)} %param.7) | copy-start | bytes 6291460
  1.7 34.8 %copy-start.1 = (bf16[1,2048,512]{2,1,0:T(8,128)(2,1)S(1)}, bf16[1,2048,512]{2,1,0:T(8,128)(2,1)}, u32[]{:S(2)}) copy-start(bf16[1,2048,512]{2,1,0:T(8,128)(2,1)} %param.7) | copy-start | bytes 6291460
  3.8 14.3 %all-to-all-start = ((f32[16,8,128]{2,1,0:T(8,128)}), f32[16,8,128]{2,1,0:T(8,128)S(1)}, u32[]{:S(2)}, u32[]{:S(2)}) async-start(f32[16,8,128]{2,1,0:T(8,128)} %get-tuple-element.17), calls=%async_computation | async-start | bytes 131072 | tf_op jit(solution)/shard_map/all_to_all | solution.py:237
  11.4 25.0 %collective-permute-start = (bf16[256,512]{1,0:T(8,128)(2,1)S(1)}, bf16[256,512]{1,0:T(8,128)(2,1)S(1)}, u32[]{:S(2)}, u32[]{:S(2)}) collective-permute-start(bf16[256,512]{1,0:T(8,128)(2,1)S(1)} %get-tuple-element.18), channel_id=1, source_target_pairs={{0,1},{1,0},{2,3},{3,2},{4,5},{5,4},{6,7},{7,6},{8,9},{9,8},{10,11... | collective-permute-start | bytes 786440 | tf_op jit(solution)/shard_map/ppermute | solution.py:249
  12.4 24.0 %collective-permute-start.1 = (bf16[256,512]{1,0:T(8,128)(2,1)S(1)}, bf16[256,512]{1,0:T(8,128)(2,1)S(1)}, u32[]{:S(2)}, u32[]{:S(2)}) collective-permute-start(bf16[256,512]{1,0:T(8,128)(2,1)S(1)} %get-tuple-element.19), channel_id=1, source_target_pairs={{1,2},{3,4},{5,6},{7,8},{9,10},{11,12},{13,14},{15,16},{17,18},{19... | collective-permute-start | bytes 786440 | tf_op jit(solution)/shard_map/ppermute | solution.py:251
  18.2 46.8 %copy-start.7 = (f32[2,256]{1,0:T(2,128)S(1)}, f32[2,256]{1,0:T(2,128)}, u32[]{:S(2)}) copy-start(f32[2,256]{1,0:T(2,128)} %gain_ref.7) | copy-start | bytes 6148
  18.2 46.8 %copy-start.8 = (f32[2,256]{1,0:T(2,128)S(1)}, f32[2,256]{1,0:T(2,128)}, u32[]{:S(2)}) copy-start(f32[2,256]{1,0:T(2,128)} %bias_ref.7) | copy-start | bytes 6148
  36.5 1.4 copy-start.2
  37.9 27.1 %copy-start.4 = (bf16[2,256,512]{2,1,0:T(8,128)(2,1)S(1)}, bf16[2,256,512]{2,1,0:T(8,128)(2,1)}, u32[]{:S(2)}) copy-start(bf16[2,256,512]{2,1,0:T(8,128)(2,1)} %point_ref.3) | copy-start | bytes 1572868
  65.0 32.4 %copy-start.3 = (bf16[2,3,512,256]{3,2,1,0:T(8,128)(2,1)S(1)}, bf16[2,3,512,256]{3,2,1,0:T(8,128)(2,1)}, u32[]{:S(2)}) copy-start(bf16[2,3,512,256]{3,2,1,0:T(8,128)(2,1)} %taps_ref.3) | copy-start | bytes 4718596
  69.0 28.5 %collective-permute-start.2 = (f32[512,512]{1,0:T(8,128)S(1)}, f32[512,512]{1,0:T(8,128)S(1)}, u32[]{:S(2)}, u32[]{:S(2)}) collective-permute-start(f32[512,512]{1,0:T(8,128)S(1)} %get-tuple-element.23), channel_id=1, source_target_pairs={{0,1},{1,0},{2,3},{3,2},{4,5},{5,4},{6,7},{7,6},{8,9},{9,8},{10,11... | collective-permute-start | bytes 3145736 | tf_op jit(solution)/shard_map/ppermute | solution.py:249
  69.4 28.0 %collective-permute-start.3 = (f32[512,512]{1,0:T(8,128)S(1)}, f32[512,512]{1,0:T(8,128)S(1)}, u32[]{:S(2)}, u32[]{:S(2)}) collective-permute-start(f32[512,512]{1,0:T(8,128)S(1)} %get-tuple-element.25), channel_id=1, source_target_pairs={{1,2},{3,4},{5,6},{7,8},{9,10},{11,12},{13,14},{15,16},{17,18},{19... | collective-permute-start | bytes 3145736 | tf_op jit(solution)/shard_map/ppermute | solution.py:251

commit v4 on v3

v4 whole, which is shorter than its diff:
```python
import functools

import jax
import jax.numpy as jnp
from jax import lax
from jax.experimental import pallas as pl
from jax.experimental.pallas import tpu as pltpu
from jax.sharding import Mesh, PartitionSpec as P

EPS = 1e-05
HEADS = 8
POOL = 8
ROWS = 2048
CH = 512
MID = 256
TILE = 256
CHUNK = 32
NEAR = 256
FAR = 512

NAMES = ("y_lo", "x", "z", "y_hi", "core")
SIZES = (2, 4, 8, 2, 2)
BATCH = ("y_lo", "x")
SEQ = ("z", "y_hi", "core")
ACROSS = ("y_lo", "x", "y_hi")
ALONG = ("z", "core")
PEERS = 16
COUNT = PEERS * PEERS * ROWS
TOP = 60000.0
F32 = jnp.float32
BF16 = jnp.bfloat16


def gelu(u):
    return 0.5 * u * (1.0 + lax.erf(u * 0.7071067811865476))


def wide(v):
    return jnp.concatenate([v[j : j + 1] for j in range(v.shape[0])], axis=1)


def combined(got_ref):
    rows = got_ref.shape[1] // 2
    got = got_ref[...]
    means = got[:, :rows]
    mean = jnp.sum(means, axis=0) * (1.0 / PEERS)
    spread = means - mean
    total = jnp.sum(got[:, rows:], axis=0) + (PEERS * ROWS) * jnp.sum(spread * spread, axis=0)
    return mean, total * (1.0 / COUNT)


def norm_terms(layer, got_ref, gain_ref, bias_ref):
    mean, variance = combined(got_ref)
    factor = gain_ref[layer : layer + 1] * lax.rsqrt(wide(variance) + EPS)
    return wide(mean), factor, bias_ref[layer : layer + 1]


def largest(v):
    return jnp.max(jnp.max(v, axis=0, keepdims=True), axis=1, keepdims=True)


def output_bound(stream_got_ref, gain_ref, bias_ref, point_ref):
    mean, variance = combined(stream_got_ref)
    root = 1.01 * COUNT**0.5
    stream = root * jnp.sqrt(largest(variance + mean * mean))
    gated = root * largest(jnp.abs(gain_ref[1:2])) + 1.01 * largest(jnp.abs(bias_ref[1:2]))
    weights = jnp.sum(jnp.abs(point_ref[1].astype(F32)), axis=0, keepdims=True)
    return stream + gated * largest(weights) + 1e-30


def fold(v):
    return jnp.sum(v.reshape(-1, 8, v.shape[-1]), axis=0)


def put_stats(out_ref, mean, squares):
    rows = out_ref.shape[1] // 2
    for j in range(rows):
        for base, v in ((0, mean), (rows, squares)):
            piece = v[:, 128 * j : 128 * (j + 1)].reshape(1, 1, 128)
            out_ref[:, base + j : base + j + 1, :] = jnp.broadcast_to(piece, (PEERS, 1, 128))


def row_slice(i, size):
    return pl.ds(pl.multiple_of(i * size, size), size)


def deviations(refs, mean, channels):
    squares = jnp.zeros((8, channels), F32)
    for ref in refs:

        def step(i, acc, ref=ref):
            d = ref[row_slice(i, 64), :].astype(F32) - mean
            return acc + fold(d * d)

        squares = lax.fori_loop(0, ref.shape[0] // 64, step, squares, unroll=4)
    return jnp.sum(squares, axis=0, keepdims=True)


def input_stats(place_ref, x_hbm, facing_ref, outer_ref, out_ref, x_ref, sems):
    parts = sems.shape[0]
    size = ROWS // parts
    copies = []
    for p in range(parts):
        rows = pl.ds(p * size, size)
        copies.append(pltpu.make_async_copy(x_hbm.at[rows], x_ref.at[rows], sems.at[p]))
        copies[p].start()
    means, squares = [], jnp.zeros((1, CH), F32)
    for p in range(parts):
        copies[p].wait()
        part = x_ref.at[p * size : (p + 1) * size]

        def step(i, acc, part=part):
            return acc + fold(part[row_slice(i, 64), :].astype(F32))

        acc = lax.fori_loop(0, size // 64, step, jnp.zeros((8, CH), F32), unroll=4)
        means.append(jnp.sum(acc, axis=0, keepdims=True) * (1.0 / size))
        squares += deviations((part,), means[p], CH)
    put_edges(place_ref[0], x_ref, facing_ref, outer_ref)
    mean = sum(means) * (1.0 / parts)
    put_stats(out_ref, mean, squares + size * sum((m - mean) * (m - mean) for m in means))


def activate(piece, first, count, terms, act_ref, offset, flag=None):
    mean, factor, bias = terms

    def step(i, carry):
        v = piece[pl.ds(pl.multiple_of(first + i * CHUNK, CHUNK), CHUNK), :].astype(F32)
        a = gelu((v - mean) * factor + bias)
        if flag is not None:
            a = jnp.where(flag > 0, a, 0.0)
        act_ref[pl.ds(pl.multiple_of(offset + i * CHUNK, CHUNK), CHUNK), :] = a.astype(BF16)
        return carry

    lax.fori_loop(0, count // CHUNK, step, 0)


def conv_stats(acc, center, stats_ref):
    mean = jnp.sum(acc, axis=0, keepdims=True) * (1.0 / ROWS)
    put_stats(stats_ref, mean, deviations((center,), mean, MID))


def conv_kernel(
    layer,
    dilation,
    size,
    place_ref,
    got_ref,
    gain_ref,
    bias_ref,
    taps_hbm,
    near_ref,
    center_ref,
    cross_ref,
    conv_ref,
    stats_ref,
    act_ref,
    taps_ref,
    taps_sem,
):
    copy = pltpu.make_async_copy(taps_hbm.at[layer], taps_ref, taps_sem)
    copy.start()
    terms = norm_terms(layer, got_ref, gain_ref, bias_ref)
    core = place_ref[0]
    activate(near_ref, 0, dilation, terms, act_ref, (1 - core) * (dilation + ROWS))
    activate(cross_ref, 0, dilation, terms, act_ref, core * (dilation + ROWS), place_ref[1])
    copy.wait()
    weights = taps_ref[...].reshape(3 * CH, MID)
    mean, factor, bias = terms
    acc = jnp.zeros((8, MID), F32)
    done = 0
    for end in range(size, ROWS + size, size):
        for r in range(end - size, end, CHUNK):
            v = center_ref[r : r + CHUNK, :].astype(F32)
            act_ref[dilation + r : dilation + r + CHUNK, :] = gelu((v - mean) * factor + bias).astype(BF16)
        ready = ROWS if end == ROWS else end - dilation
        while done + size <= ready:
            rows = [act_ref[done + k * dilation : done + k * dilation + size, :] for k in range(3)]
            total = jnp.dot(jnp.concatenate(rows, axis=1), weights, preferred_element_type=F32)
            conv_ref[done : done + size, :] = total
            acc = acc + fold(total)
            done += size
    conv_stats(acc, conv_ref, stats_ref)


def put_edges(core, rows_ref, facing_ref, outer_ref):
    size = facing_ref.shape[0]
    last = ROWS - size
    facing_ref[...] = rows_ref[pl.ds(pl.multiple_of((1 - core) * last, 256), size), :]
    outer_ref[...] = rows_ref[pl.ds(pl.multiple_of(core * last, 256), size), :]


def gated_tile(conv_ref, i, terms, gated_ref):
    mean, factor, bias = terms
    for r in range(i * TILE, (i + 1) * TILE, CHUNK):
        gated_ref[r : r + CHUNK, :] = gelu((conv_ref[r : r + CHUNK, :] - mean) * factor + bias).astype(BF16)
    return gated_ref[i * TILE : (i + 1) * TILE, :]


def point_kernel(
    place_ref,
    got_ref,
    gain_ref,
    bias_ref,
    point_ref,
    conv_ref,
    x_ref,
    stream_ref,
    facing_ref,
    outer_ref,
    stats_ref,
    pool_ref,
    gated_ref,
):
    terms = norm_terms(0, got_ref, gain_ref, bias_ref)
    acc = jnp.zeros((8, CH), F32)
    bins = TILE // POOL
    for i in range(ROWS // TILE):
        rows = slice(i * TILE, (i + 1) * TILE)
        gated = gated_tile(conv_ref, i, terms, gated_ref)
        total = x_ref[rows, :].astype(F32) + jnp.dot(gated, point_ref[0], preferred_element_type=F32)
        stream_ref[rows, :] = total
        pool_ref[i * bins : (i + 1) * bins, :] = jnp.sum(total.reshape(bins, POOL, CH), axis=1)
        acc = acc + fold(total)
    put_edges(place_ref[0], stream_ref, facing_ref, outer_ref)
    mean = jnp.sum(acc, axis=0, keepdims=True) * (1.0 / ROWS)
    put_stats(stats_ref, mean, deviations((stream_ref,), mean, CH))


def pool_kernel(
    got_ref,
    stream_got_ref,
    gain_ref,
    bias_ref,
    point_ref,
    conv_ref,
    pool_ref,
    out_ref,
    bound_ref,
    gated_ref,
    sums_ref,
    flip_ref,
):
    bound = output_bound(stream_got_ref, gain_ref, bias_ref, point_ref)
    bound_ref[...] = jnp.broadcast_to(bound * (1.0 / TOP), bound_ref.shape)
    scale = (TOP / POOL) / bound
    terms = norm_terms(1, got_ref, gain_ref, bias_ref)
    bins = TILE // POOL
    row = lax.broadcasted_iota(jnp.int32, (bins, TILE), 0)
    col = lax.broadcasted_iota(jnp.int32, (bins, TILE), 1)
    pick = jnp.where(col // POOL == row, 1.0, 0.0).astype(BF16)

    for i in range(ROWS // TILE):
        gated = gated_tile(conv_ref, i, terms, gated_ref)
        sums_ref[i * bins : (i + 1) * bins, :] = jnp.dot(pick, gated, preferred_element_type=F32)
    sums = sums_ref[...]
    upper = sums.astype(BF16)
    lower = (sums - upper.astype(F32)).astype(BF16)
    branch = jnp.dot(upper, point_ref[1], preferred_element_type=F32)
    branch += jnp.dot(lower, point_ref[1], preferred_element_type=F32)
    flipped = ((pool_ref[...] + branch) * scale).T
    size = CH // HEADS
    for k in range(ROWS // POOL // 128):
        half = flip_ref.at[k]
        for h in range(HEADS):
            half[pl.ds(h, size, stride=HEADS), :] = flipped[h * size : (h + 1) * size, 128 * k : 128 * (k + 1)]
        out_ref[:, 128 * k : 128 * (k + 1)] = half[...]


VMEM = pl.BlockSpec(memory_space=pltpu.VMEM)
SMEM = pl.BlockSpec(memory_space=pltpu.SMEM)
HBM = pl.BlockSpec(memory_space=pltpu.HBM)
PARAMS = pltpu.CompilerParams(vmem_limit_bytes=20 * 1024 * 1024)


def call(body, args, outs, scratch=(), scalars=0, far=()):
    specs = [SMEM if i < scalars else HBM if i in far else VMEM for i in range(len(args))]
    return pl.pallas_call(
        body,
        out_shape=[jax.ShapeDtypeStruct(s, d) for s, d in outs],
        in_specs=specs,
        out_specs=[VMEM] * len(outs),
        scratch_shapes=list(scratch),
        compiler_params=PARAMS,
    )(*args)


def reduce_stats(sent, first, second):
    got = lax.all_to_all(sent, first, 0, 0, tiled=True)
    rows = got.shape[1] // 2
    means = got[:, :rows]
    mean = jnp.mean(means, axis=0)
    spread = means - mean
    squares = jnp.sum(got[:, rows:], axis=0) + ROWS * jnp.sum(spread * spread, axis=0)
    both = jnp.concatenate([mean, squares])
    return lax.all_to_all(jnp.broadcast_to(both[None], sent.shape), second, 0, 0, tiled=True)


def halos(facing, outer):
    peers = lax.axis_size(SEQ)
    near = lax.ppermute(facing, SEQ, [(i, i ^ 1) for i in range(peers)])
    pairs = [(i, i + 1) for i in range(1, peers - 1, 2)]
    return near, lax.ppermute(outer, SEQ, pairs + [(j, i) for i, j in pairs])


def per_device(inputs, taps, point, in_gain, in_bias, mid_gain, mid_bias):
    place = lax.axis_index(SEQ)
    core = lax.axis_index("core")
    joined = jnp.where(core == 0, place > 0, place < lax.axis_size(SEQ) - 1)
    where = jnp.stack([core, joined.astype(core.dtype)]).astype(jnp.int32)
    x = inputs.reshape(ROWS, CH)
    wide_stats = ((PEERS, 8, 128), F32)
    slim_stats = ((PEERS, 4, 128), F32)
    conv_outs = [((ROWS, MID), F32), slim_stats]

    edge = ((NEAR, CH), BF16)
    facing, outer, stats = call(
        input_stats,
        (where, x),
        [edge, edge, wide_stats],
        [pltpu.VMEM((ROWS, CH), BF16), pltpu.SemaphoreType.DMA((4,))],
        1,
        (1,),
    )
    near, cross = halos(facing, outer)
    got = reduce_stats(stats, ACROSS, ALONG)
    conv, stats = call(
        functools.partial(conv_kernel, 0, NEAR, 256),
        (where, got, in_gain, in_bias, taps, near, x, cross),
        conv_outs,
        [pltpu.VMEM((ROWS + 2 * NEAR, CH), BF16), pltpu.VMEM((3, CH, MID), BF16), pltpu.SemaphoreType.DMA],
        1,
        (4,),
    )
    got = reduce_stats(stats, ACROSS, ALONG)
    edge = ((FAR, CH), F32)
    stream, facing, outer, stats, pooled = call(
        point_kernel,
        (where, got, mid_gain, mid_bias, point, conv, x),
        [((ROWS, CH), F32), edge, edge, wide_stats, ((ROWS // POOL, CH), F32)],
        [pltpu.VMEM((ROWS, MID), BF16)],
        1,
    )
    near, cross = halos(facing, outer)
    stream_got = reduce_stats(stats, ALONG, ACROSS)
    conv, stats = call(
        functools.partial(conv_kernel, 1, FAR, 512),
        (where, stream_got, in_gain, in_bias, taps, near, stream, cross),
        conv_outs,
        [pltpu.VMEM((ROWS + 2 * FAR, CH), BF16), pltpu.VMEM((3, CH, MID), BF16), pltpu.SemaphoreType.DMA],
        1,
        (4,),
    )
    got = reduce_stats(stats, ACROSS, ALONG)
    out, bound = call(
        pool_kernel,
        (got, stream_got, mid_gain, mid_bias, point, conv, pooled),
        [((CH, ROWS // POOL), F32), ((1, ROWS // POOL), F32)],
        [
            pltpu.VMEM((ROWS, MID), BF16),
            pltpu.VMEM((ROWS // POOL, MID), F32),
            pltpu.VMEM((ROWS // POOL // 128, CH, 128), F32),
        ],
    )
    bins = ROWS // POOL
    out = lax.all_to_all(out.reshape(CH // HEADS, HEADS, bins).astype(jnp.float16), SEQ, 0, 0, tiled=True)
    peers = lax.axis_size(SEQ)
    out = out.astype(F32).reshape(peers, -1, HEADS, bins) * bound.reshape(1, 1, 1, bins)
    return out.transpose(2, 1, 0, 3).reshape(1, HEADS, -1, peers * bins)


def solution(mesh):
    fine = Mesh(mesh.devices.reshape(SIZES), NAMES)
    return jax.shard_map(
        per_device,
        mesh=fine,
        in_specs=(P(BATCH, SEQ, None), P(), P(), P(), P(), P(), P()),
        out_specs=P(BATCH, None, SEQ, None),
        check_vma=False,
    )
```

time: 154 us -> 143 us (0.929)
  Pallas kernels: 20.9 us -> 14 us
  blocking collectives: 110 us -> 106 us
    pallas_call x5, Pallas kernels: 20.9 us -> 14 us  [call(): pl.pallas_call(body, out_shape=[jax.ShapeDtypeStruct(s, d) for s, d in ou...]
    all_to_all x1, blocking collectives: 20.4 us -> 16 us  [per_device(): lax.all_to_all(out.reshape(CH // HEADS, HEADS, bins).astype(jnp.float16),...]
where the time goes in v4:
time: 143 us
  blocking collectives  106 us (74%)
  starting transfers between devices  16.6 us (12%)
  Pallas kernels  14 us (10%)
  local copies, waits for them, and re-layouts  4.19 us (3%)
    all_to_all x4, blocking collectives, reduce_stats(): lax.all_to_all(jnp.broadcast_to(both[None], sent.shape), second, 0, 0, ti...  54.8 us
    all_to_all x3, blocking collectives, reduce_stats(): got = lax.all_to_all(sent, first, 0, 0, tiled=True)  35.2 us
    all_to_all x1, blocking collectives, per_device(): lax.all_to_all(out.reshape(CH // HEADS, HEADS, bins).astype(jnp.float16),...  16 us
    pallas_call x5, Pallas kernels, call(): pl.pallas_call(body, out_shape=[jax.ShapeDtypeStruct(s, d) for s, d in ou...  14 us
    all_to_all x1, starting transfers between devices, reduce_stats(): got = lax.all_to_all(sent, first, 0, 0, tiled=True)  7.6 us
    ppermute x2, starting transfers between devices, halos(): return (near, lax.ppermute(outer, SEQ, pairs + [(j, i) for i, j in pairs]))  7.52 us
    unnamed x18, local copies, waits for them, and re-layouts  3.03 us
  transfers between devices with their start and end apart: 5, of which 1 were waited for; matrix products, arithmetic and copies ran while one was open for 0% of the time, Pallas kernels for 0%

profile of v4, /device:TPU:1, one launch (start us, length us, event | category | flops | bytes accessed | tf_op | source)
XLA Modules:
  0.0 142.7 jit_solution(5074847828631765315)
XLA Ops:
  0.0 0.1 pad_add_fusion.place_ref
  0.1 1.6 %copy-done = bf16[1,2048,512]{2,1,0:T(8,128)(2,1)S(1)} copy-done((bf16[1,2048,512]{2,1,0:T(8,128)(2,1)S(1)}, bf16[1,2048,512]{2,1,0:T(8,128)(2,1)}, u32[]{:S(2)}) %copy-start) | copy-done | bytes 2097176
  1.7 2.4 %shard_map.73 = (bf16[256,512]{1,0:T(8,128)(2,1)S(1)}, bf16[256,512]{1,0:T(8,128)(2,1)S(1)}, f32[16,8,128]{2,1,0:T(8,128)}) custom-call(s32[2]{0:T(128)S(1)} %pad_add_fusion.place_ref, bf16[2048,512]{1,0:T(8,128)(2,1)S(1)} %bitcast.12), custom_call_target="tpu_custom_call" | custom-call | tf_op jit(solution)/shard_map/pallas_call | solution.py:277
  4.1 7.6 %all-to-all-start = ((f32[16,8,128]{2,1,0:T(8,128)}), f32[16,8,128]{2,1,0:T(8,128)S(1)}, u32[]{:S(2)}, u32[]{:S(2)}) async-start(f32[16,8,128]{2,1,0:T(8,128)} %get-tuple-element.19), calls=%async_computation | async-start | bytes 131072 | tf_op jit(solution)/shard_map/all_to_all | solution.py:288
  11.7 1.0 collective-permute-start
  12.8 4.9 %collective-permute-start.1 = (bf16[256,512]{1,0:T(8,128)(2,1)S(1)}, bf16[256,512]{1,0:T(8,128)(2,1)S(1)}, u32[]{:S(2)}, u32[]{:S(2)}) collective-permute-start(bf16[256,512]{1,0:T(8,128)(2,1)S(1)} %get-tuple-element.21), channel_id=1, source_target_pairs={{1,2},{3,4},{5,6},{7,8},{9,10},{11,12},{13,14},{15,16},{17,18},{19... | collective-permute-start | bytes 786440 | tf_op jit(solution)/shard_map/ppermute | solution.py:302
  17.6 0.8 all-to-all-done
  18.5 0.0 copy-start.7
  18.6 0.0 copy-start.8
  18.6 18.2 %all_to_all.45.got_ref = f32[16,8,128]{2,1,0:T(8,128)S(1)} all-to-all(f32[16,8,128]{2,1,0:T(8,128)S(1)} %broadcast_in_dim.8), channel_id=1, replica_groups=mesh['y_lo'=2,'x'=4,'z'=8,'y_hi'=2,'core'=2] {'z','core'}, dimensions={0} | all-to-all | bytes 131072 | tf_op jit(solution)/shard_map/all_to_all | solution.py:295
  36.8 0.0 collective-permute-done.near_ref
  36.8 0.0 collective-permute-done.1.cross_ref
  36.8 0.0 copy-start.2
  36.8 1.4 copy-done.2
  38.2 3.3 %shard_map.74 = (f32[2048,256]{1,0:T(8,128)S(1)}, f32[16,4,128]{2,1,0:T(4,128)S(1)}) custom-call(s32[2]{0:T(128)S(1)} %pad_add_fusion.place_ref, f32[16,8,128]{2,1,0:T(8,128)S(1)} %all_to_all.45.got_ref, f32[2,512]{1,0:T(2,128)S(1)} %copy-done.5, f32[2,512]{1,0:T(2,128)S(1)} %copy-done.6, bf16[2,3,512,256]{3,2,1,0:T(8,128)(2,1)S(1)} %copy-done.2, ...), custom_call_target="tpu_custom_call" | custom-call | tf_op jit(solution)/shard_map/pallas_call | solution.py:277
  41.5 9.3 %all_to_all.46 = f32[16,4,128]{2,1,0:T(4,128)S(1)} all-to-all(f32[16,4,128]{2,1,0:T(4,128)S(1)} %get-tuple-element.22), channel_id=1, replica_groups=mesh['y_lo'=2,'x'=4,'z'=8,'y_hi'=2,'core'=2] {'y_lo','x','y_hi'}, dimensions={0} | all-to-all | bytes 65536 | tf_op jit(solution)/shard_map/all_to_all | solution.py:288
  51.0 11.5 %all_to_all.47.got_ref = f32[16,4,128]{2,1,0:T(4,128)S(1)} all-to-all(f32[16,4,128]{2,1,0:T(4,128)S(1)} %broadcast_in_dim.9), channel_id=1, replica_groups=mesh['y_lo'=2,'x'=4,'z'=8,'y_hi'=2,'core'=2] {'z','core'}, dimensions={0} | all-to-all | bytes 65536 | tf_op jit(solution)/shard_map/all_to_all | solution.py:295
  62.4 0.0 copy-start.3
  62.4 3.2 %shard_map.75 = (f32[2048,512]{1,0:T(8,128)S(1)}, f32[512,512]{1,0:T(8,128)S(1)}, f32[512,512]{1,0:T(8,128)S(1)}, f32[16,8,128]{2,1,0:T(8,128)S(1)}, f32[256,512]{1,0:T(8,128)S(1)}) custom-call(s32[2]{0:T(128)S(1)} %pad_add_fusion.place_ref, f32[16,4,128]{2,1,0:T(4,128)S(1)} %all_to_all.47.got_ref, f32[2,256]{1,0:T(2,128)S(1)} %copy-done.7, ...), custom_call_target="tpu_custom_call" | custom-call | tf_op jit(solution)/shard_map/pallas_call | solution.py:277
  65.7 0.5 collective-permute-start.2
  66.1 2.7 %collective-permute-start.3 = (f32[512,512]{1,0:T(8,128)S(1)}, f32[512,512]{1,0:T(8,128)S(1)}, u32[]{:S(2)}, u32[]{:S(2)}) collective-permute-start(f32[512,512]{1,0:T(8,128)S(1)} %get-tuple-element.27), channel_id=1, source_target_pairs={{1,2},{3,4},{5,6},{7,8},{9,10},{11,12},{13,14},{15,16},{17,18},{19... | collective-permute-start | bytes 3145736 | tf_op jit(solution)/shard_map/ppermute | solution.py:302
  68.8 15.5 %all_to_all.48 = f32[16,8,128]{2,1,0:T(8,128)S(1)} all-to-all(f32[16,8,128]{2,1,0:T(8,128)S(1)} %get-tuple-element.24), channel_id=1, replica_groups=mesh['y_lo'=2,'x'=4,'z'=8,'y_hi'=2,'core'=2] {'z','core'}, dimensions={0} | all-to-all | bytes 131072 | tf_op jit(solution)/shard_map/all_to_all | solution.py:288
  84.4 9.7 %all_to_all.49.got_ref.stream_got_ref = f32[16,8,128]{2,1,0:T(8,128)S(1)} all-to-all(f32[16,8,128]{2,1,0:T(8,128)S(1)} %broadcast_in_dim.10), channel_id=1, replica_groups=mesh['y_lo'=2,'x'=4,'z'=8,'y_hi'=2,'core'=2] {'y_lo','x','y_hi'}, dimensions={0} | all-to-all | bytes 131072 | tf_op jit(solution)/shard_map/all_to_all | solution.py:295
  94.1 0.0 collective-permute-done.2.near_ref
  94.1 3.8 %shard_map.76 = (f32[2048,256]{1,0:T(8,128)S(1)}, f32[16,4,128]{2,1,0:T(4,128)S(1)}) custom-call(s32[2]{0:T(128)S(1)} %pad_add_fusion.place_ref, f32[16,8,128]{2,1,0:T(8,128)S(1)} %all_to_all.49.got_ref.stream_got_ref, f32[2,512]{1,0:T(2,128)S(1)} %copy-done.5, f32[2,512]{1,0:T(2,128)S(1)} %copy-done.6, bf16[2,3,512,256]{3,2,1,0:T(8,128)(2,1)S(1)} %copy-done.3, ...), custom_call_target="tpu_custom_call" | custom-call | tf_op jit(solution)/shard_map/pallas_call | solution.py:277
  98.0 10.5 %all_to_all.50 = f32[16,4,128]{2,1,0:T(4,128)S(1)} all-to-all(f32[16,4,128]{2,1,0:T(4,128)S(1)} %get-tuple-element.28), channel_id=1, replica_groups=mesh['y_lo'=2,'x'=4,'z'=8,'y_hi'=2,'core'=2] {'y_lo','x','y_hi'}, dimensions={0} | all-to-all | bytes 65536 | tf_op jit(solution)/shard_map/all_to_all | solution.py:288
  108.5 15.4 %all_to_all.51.got_ref = f32[16,4,128]{2,1,0:T(4,128)S(1)} all-to-all(f32[16,4,128]{2,1,0:T(4,128)S(1)} %broadcast_in_dim.11), channel_id=1, replica_groups=mesh['y_lo'=2,'x'=4,'z'=8,'y_hi'=2,'core'=2] {'z','core'}, dimensions={0} | all-to-all | bytes 65536 | tf_op jit(solution)/shard_map/all_to_all | solution.py:295
  123.9 1.2 shard_map.77
  125.2 16.0 %all_to_all.52 = f16[64,8,256]{2,1,0:T(8,128)(2,1)S(1)} all-to-all(f16[64,8,256]{2,1,0:T(8,128)(2,1)S(1)} %convert_bitcast_fusion), channel_id=1, replica_groups=mesh['y_lo'=2,'x'=4,'z'=8,'y_hi'=2,'core'=2] {'z','y_hi','core'}, dimensions={0} | all-to-all | bytes 524288 | tf_op jit(solution)/shard_map/all_to_all | solution.py:365
  141.2 0.1 convert.2
  141.2 0.3 fusion
  141.5 1.1 reshape.35
  (38 shorter events, 0.4 us)
Async XLA Ops:
  0.0 36.8 %copy-start.6 = (f32[2,512]{1,0:T(2,128)S(1)}, f32[2,512]{1,0:T(2,128)}, u32[]{:S(2)}) copy-start(f32[2,512]{1,0:T(2,128)} %bias_ref.6) | copy-start | bytes 12292
  0.0 36.8 %copy-start.5 = (f32[2,512]{1,0:T(2,128)S(1)}, f32[2,512]{1,0:T(2,128)}, u32[]{:S(2)}) copy-start(f32[2,512]{1,0:T(2,128)} %gain_ref.6) | copy-start | bytes 12292
  0.1 1.6 %copy-start = (bf16[1,2048,512]{2,1,0:T(8,128)(2,1)S(1)}, bf16[1,2048,512]{2,1,0:T(8,128)(2,1)}, u32[]{:S(2)}) copy-start(bf16[1,2048,512]{2,1,0:T(8,128)(2,1)} %param.7) | copy-start | bytes 6291460
  1.7 35.1 %copy-start.1 = (bf16[1,2048,512]{2,1,0:T(8,128)(2,1)S(1)}, bf16[1,2048,512]{2,1,0:T(8,128)(2,1)}, u32[]{:S(2)}) copy-start(bf16[1,2048,512]{2,1,0:T(8,128)(2,1)} %param.7) | copy-start | bytes 6291460
  4.1 14.3 %all-to-all-start = ((f32[16,8,128]{2,1,0:T(8,128)}), f32[16,8,128]{2,1,0:T(8,128)S(1)}, u32[]{:S(2)}, u32[]{:S(2)}) async-start(f32[16,8,128]{2,1,0:T(8,128)} %get-tuple-element.19), calls=%async_computation | async-start | bytes 131072 | tf_op jit(solution)/shard_map/all_to_all | solution.py:288
  11.7 25.0 %collective-permute-start = (bf16[256,512]{1,0:T(8,128)(2,1)S(1)}, bf16[256,512]{1,0:T(8,128)(2,1)S(1)}, u32[]{:S(2)}, u32[]{:S(2)}) collective-permute-start(bf16[256,512]{1,0:T(8,128)(2,1)S(1)} %get-tuple-element.20), channel_id=1, source_target_pairs={{0,1},{1,0},{2,3},{3,2},{4,5},{5,4},{6,7},{7,6},{8,9},{9,8},{10,11... | collective-permute-start | bytes 786440 | tf_op jit(solution)/shard_map/ppermute | solution.py:300
  12.8 24.0 %collective-permute-start.1 = (bf16[256,512]{1,0:T(8,128)(2,1)S(1)}, bf16[256,512]{1,0:T(8,128)(2,1)S(1)}, u32[]{:S(2)}, u32[]{:S(2)}) collective-permute-start(bf16[256,512]{1,0:T(8,128)(2,1)S(1)} %get-tuple-element.21), channel_id=1, source_target_pairs={{1,2},{3,4},{5,6},{7,8},{9,10},{11,12},{13,14},{15,16},{17,18},{19... | collective-permute-start | bytes 786440 | tf_op jit(solution)/shard_map/ppermute | solution.py:302
  18.5 43.9 %copy-start.7 = (f32[2,256]{1,0:T(2,128)S(1)}, f32[2,256]{1,0:T(2,128)}, u32[]{:S(2)}) copy-start(f32[2,256]{1,0:T(2,128)} %gain_ref.7) | copy-start | bytes 6148
  18.6 43.9 %copy-start.8 = (f32[2,256]{1,0:T(2,128)S(1)}, f32[2,256]{1,0:T(2,128)}, u32[]{:S(2)}) copy-start(f32[2,256]{1,0:T(2,128)} %bias_ref.7) | copy-start | bytes 6148
  36.8 1.4 copy-start.2
  38.2 24.2 %copy-start.4 = (bf16[2,256,512]{2,1,0:T(8,128)(2,1)S(1)}, bf16[2,256,512]{2,1,0:T(8,128)(2,1)}, u32[]{:S(2)}) copy-start(bf16[2,256,512]{2,1,0:T(8,128)(2,1)} %point_ref.3) | copy-start | bytes 1572868
  62.4 31.7 %copy-start.3 = (bf16[2,3,512,256]{3,2,1,0:T(8,128)(2,1)S(1)}, bf16[2,3,512,256]{3,2,1,0:T(8,128)(2,1)}, u32[]{:S(2)}) copy-start(bf16[2,3,512,256]{3,2,1,0:T(8,128)(2,1)} %taps_hbm.3) | copy-start | bytes 4718596
  65.7 28.5 %collective-permute-start.2 = (f32[512,512]{1,0:T(8,128)S(1)}, f32[512,512]{1,0:T(8,128)S(1)}, u32[]{:S(2)}, u32[]{:S(2)}) collective-permute-start(f32[512,512]{1,0:T(8,128)S(1)} %get-tuple-element.25), channel_id=1, source_target_pairs={{0,1},{1,0},{2,3},{3,2},{4,5},{5,4},{6,7},{7,6},{8,9},{9,8},{10,11... | collective-permute-start | bytes 3145736 | tf_op jit(solution)/shard_map/ppermute | solution.py:300
  66.1 28.0 %collective-permute-start.3 = (f32[512,512]{1,0:T(8,128)S(1)}, f32[512,512]{1,0:T(8,128)S(1)}, u32[]{:S(2)}, u32[]{:S(2)}) collective-permute-start(f32[512,512]{1,0:T(8,128)S(1)} %get-tuple-element.27), channel_id=1, source_target_pairs={{1,2},{3,4},{5,6},{7,8},{9,10},{11,12},{13,14},{15,16},{17,18},{19... | collective-permute-start | bytes 3145736 | tf_op jit(solution)/shard_map/ppermute | solution.py:302

commit v5 on v4

--- a/solution.py
+++ b/solution.py
@@ -1,5 +1,3 @@
-import functools
-
 import jax
 import jax.numpy as jnp
 from jax import lax
@@ -96,28 +94,17 @@
     return jnp.sum(squares, axis=0, keepdims=True)
 
 
-def input_stats(place_ref, x_hbm, facing_ref, outer_ref, out_ref, x_ref, sems):
-    parts = sems.shape[0]
-    size = ROWS // parts
-    copies = []
-    for p in range(parts):
-        rows = pl.ds(p * size, size)
-        copies.append(pltpu.make_async_copy(x_hbm.at[rows], x_ref.at[rows], sems.at[p]))
-        copies[p].start()
-    means, squares = [], jnp.zeros((1, CH), F32)
-    for p in range(parts):
-        copies[p].wait()
-        part = x_ref.at[p * size : (p + 1) * size]
-
-        def step(i, acc, part=part):
-            return acc + fold(part[row_slice(i, 64), :].astype(F32))
-
-        acc = lax.fori_loop(0, size // 64, step, jnp.zeros((8, CH), F32), unroll=4)
-        means.append(jnp.sum(acc, axis=0, keepdims=True) * (1.0 / size))
-        squares += deviations((part,), means[p], CH)
+def input_stats(place_ref, x_ref, facing_ref, outer_ref, out_ref):
     put_edges(place_ref[0], x_ref, facing_ref, outer_ref)
-    mean = sum(means) * (1.0 / parts)
-    put_stats(out_ref, mean, squares + size * sum((m - mean) * (m - mean) for m in means))
+    acc = jnp.zeros((8, CH), F32)
+    for r in range(0, ROWS, 64):
+        acc += fold(x_ref[r : r + 64, :].astype(F32))
+    mean = jnp.sum(acc, axis=0, keepdims=True) * (1.0 / ROWS)
+    squares = jnp.zeros((8, CH), F32)
+    for r in range(0, ROWS, 64):
+        d = x_ref[r : r + 64, :].astype(F32) - mean
+        squares += fold(d * d)
+    put_stats(out_ref, mean, jnp.sum(squares, axis=0, keepdims=True))
 
 
 def activate(piece, first, count, terms, act_ref, offset, flag=None):
@@ -139,32 +126,7 @@
     put_stats(stats_ref, mean, deviations((center,), mean, MID))
 
 
-def conv_kernel(
-    layer,
-    dilation,
-    size,
-    place_ref,
-    got_ref,
-    gain_ref,
-    bias_ref,
-    taps_hbm,
-    near_ref,
-    center_ref,
-    cross_ref,
-    conv_ref,
-    stats_ref,
-    act_ref,
-    taps_ref,
-    taps_sem,
-):
-    copy = pltpu.make_async_copy(taps_hbm.at[layer], taps_ref, taps_sem)
-    copy.start()
-    terms = norm_terms(layer, got_ref, gain_ref, bias_ref)
-    core = place_ref[0]
-    activate(near_ref, 0, dilation, terms, act_ref, (1 - core) * (dilation + ROWS))
-    activate(cross_ref, 0, dilation, terms, act_ref, core * (dilation + ROWS), place_ref[1])
-    copy.wait()
-    weights = taps_ref[...].reshape(3 * CH, MID)
+def conv_tiles(dilation, size, terms, center_ref, weights, conv_ref, stats_ref, act_ref):
     mean, factor, bias = terms
     acc = jnp.zeros((8, MID), F32)
     done = 0
@@ -180,6 +142,59 @@
             acc = acc + fold(total)
             done += size
     conv_stats(acc, conv_ref, stats_ref)
+
+
+def first_conv(
+    place_ref,
+    got_ref,
+    gain_ref,
+    bias_ref,
+    taps_ref,
+    near_ref,
+    center_ref,
+    cross_ref,
+    conv_ref,
+    stats_ref,
+    act_ref,
+):
+    terms = norm_terms(0, got_ref, gain_ref, bias_ref)
+    core = place_ref[0]
+    activate(near_ref, core * (FAR - NEAR), NEAR, terms, act_ref, (1 - core) * (NEAR + ROWS))
+    activate(cross_ref, (1 - core) * (FAR - NEAR), NEAR, terms, act_ref, core * (NEAR + ROWS), place_ref[1])
+    weights = taps_ref[0].reshape(3 * CH, MID)
+    conv_tiles(NEAR, 256, terms, center_ref, weights, conv_ref, stats_ref, act_ref)
+
+
+def second_conv(
+    place_ref,
+    got_ref,
+    gain_ref,
+    bias_ref,
+    taps_ref,
+    point_ref,
+    near_ref,
+    near_gated_ref,
+    center_ref,
+    cross_ref,
+    cross_gated_ref,
+    conv_ref,
+    stats_ref,
+    act_ref,
+    near_stream_ref,
+    cross_stream_ref,
+):
+    terms = norm_terms(1, got_ref, gain_ref, bias_ref)
+    core = place_ref[0]
+    for x_ref, gated_ref, stream_ref in (
+        (near_ref, near_gated_ref, near_stream_ref),
+        (cross_ref, cross_gated_ref, cross_stream_ref),
+    ):
+        branch = jnp.dot(gated_ref[...], point_ref[0], preferred_element_type=F32)
+        stream_ref[...] = x_ref[...].astype(F32) + branch
+    activate(near_stream_ref, 0, FAR, terms, act_ref, (1 - core) * (FAR + ROWS))
+    activate(cross_stream_ref, 0, FAR, terms, act_ref, core * (FAR + ROWS), place_ref[1])
+    weights = taps_ref[1].reshape(3 * CH, MID)
+    conv_tiles(FAR, 512, terms, center_ref, weights, conv_ref, stats_ref, act_ref)
 
 
 def put_edges(core, rows_ref, facing_ref, outer_ref):
@@ -221,7 +236,7 @@
         stream_ref[rows, :] = total
         pool_ref[i * bins : (i + 1) * bins, :] = jnp.sum(total.reshape(bins, POOL, CH), axis=1)
         acc = acc + fold(total)
-    put_edges(place_ref[0], stream_ref, facing_ref, outer_ref)
+    put_edges(place_ref[0], gated_ref, facing_ref, outer_ref)
     mean = jnp.sum(acc, axis=0, keepdims=True) * (1.0 / ROWS)
     put_stats(stats_ref, mean, deviations((stream_ref,), mean, CH))
 
@@ -268,23 +283,28 @@
 
 VMEM = pl.BlockSpec(memory_space=pltpu.VMEM)
 SMEM = pl.BlockSpec(memory_space=pltpu.SMEM)
-HBM = pl.BlockSpec(memory_space=pltpu.HBM)
 PARAMS = pltpu.CompilerParams(vmem_limit_bytes=20 * 1024 * 1024)
 
 
-def call(body, args, outs, scratch=(), scalars=0, far=()):
-    specs = [SMEM if i < scalars else HBM if i in far else VMEM for i in range(len(args))]
+def call(body, args, outs, scratch=(), scalars=0):
     return pl.pallas_call(
         body,
         out_shape=[jax.ShapeDtypeStruct(s, d) for s, d in outs],
-        in_specs=specs,
+        in_specs=[SMEM] * scalars + [VMEM] * (len(args) - scalars),
         out_specs=[VMEM] * len(outs),
         scratch_shapes=list(scratch),
         compiler_params=PARAMS,
     )(*args)
 
 
-def reduce_stats(sent, first, second):
+def halos(facing, outer):
+    peers = lax.axis_size(SEQ)
+    near = lax.ppermute(facing, SEQ, [(i, i ^ 1) for i in range(peers)])
+    pairs = [(i, i + 1) for i in range(1, peers - 1, 2)]
+    return near, lax.ppermute(outer, SEQ, pairs + [(j, i) for i, j in pairs])
+
+
+def reduce_stats(sent, first, second, *edges):
     got = lax.all_to_all(sent, first, 0, 0, tiled=True)
     rows = got.shape[1] // 2
     means = got[:, :rows]
@@ -292,14 +312,10 @@
     spread = means - mean
     squares = jnp.sum(got[:, rows:], axis=0) + ROWS * jnp.sum(spread * spread, axis=0)
     both = jnp.concatenate([mean, squares])
-    return lax.all_to_all(jnp.broadcast_to(both[None], sent.shape), second, 0, 0, tiled=True)
-
-
-def halos(facing, outer):
-    peers = lax.axis_size(SEQ)
-    near = lax.ppermute(facing, SEQ, [(i, i ^ 1) for i in range(peers)])
-    pairs = [(i, i + 1) for i in range(1, peers - 1, 2)]
-    return near, lax.ppermute(outer, SEQ, pairs + [(j, i) for i, j in pairs])
+    if edges:
+        both, *edges = lax.optimization_barrier((both, *edges))
+        edges = halos(*edges)
+    return lax.all_to_all(jnp.broadcast_to(both[None], sent.shape), second, 0, 0, tiled=True), *edges
 
 
 def per_device(inputs, taps, point, in_gain, in_bias, mid_gain, mid_bias):
@@ -312,27 +328,23 @@
     slim_stats = ((PEERS, 4, 128), F32)
     conv_outs = [((ROWS, MID), F32), slim_stats]
 
-    edge = ((NEAR, CH), BF16)
+    edge = ((FAR, CH), BF16)
     facing, outer, stats = call(
         input_stats,
         (where, x),
         [edge, edge, wide_stats],
-        [pltpu.VMEM((ROWS, CH), BF16), pltpu.SemaphoreType.DMA((4,))],
-        1,
-        (1,),
-    )
-    near, cross = halos(facing, outer)
-    got = reduce_stats(stats, ACROSS, ALONG)
+        scalars=1,
+    )
+    got, near, cross = reduce_stats(stats, ACROSS, ALONG, facing, outer)
     conv, stats = call(
-        functools.partial(conv_kernel, 0, NEAR, 256),
+        first_conv,
         (where, got, in_gain, in_bias, taps, near, x, cross),
         conv_outs,
-        [pltpu.VMEM((ROWS + 2 * NEAR, CH), BF16), pltpu.VMEM((3, CH, MID), BF16), pltpu.SemaphoreType.DMA],
+        [pltpu.VMEM((ROWS + 2 * NEAR, CH), BF16)],
         1,
-        (4,),
-    )
-    got = reduce_stats(stats, ACROSS, ALONG)
-    edge = ((FAR, CH), F32)
+    )
+    (got,) = reduce_stats(stats, ACROSS, ALONG)
+    edge = ((FAR, MID), BF16)
     stream, facing, outer, stats, pooled = call(
         point_kernel,
         (where, got, mid_gain, mid_bias, point, conv, x),
@@ -340,17 +352,19 @@
         [pltpu.VMEM((ROWS, MID), BF16)],
         1,
     )
-    near, cross = halos(facing, outer)
-    stream_got = reduce_stats(stats, ALONG, ACROSS)
+    stream_got, near_gated, cross_gated = reduce_stats(stats, ACROSS, ALONG, facing, outer)
     conv, stats = call(
-        functools.partial(conv_kernel, 1, FAR, 512),
-        (where, stream_got, in_gain, in_bias, taps, near, stream, cross),
+        second_conv,
+        (where, stream_got, in_gain, in_bias, taps, point, near, near_gated, stream, cross, cross_gated),
         conv_outs,
-        [pltpu.VMEM((ROWS + 2 * FAR, CH), BF16), pltpu.VMEM((3, CH, MID), BF16), pltpu.SemaphoreType.DMA],
+        [
+            pltpu.VMEM((ROWS + 2 * FAR, CH), BF16),
+            pltpu.VMEM((FAR, CH), F32),
+            pltpu.VMEM((FAR, CH), F32),
+        ],
         1,
-        (4,),
-    )
-    got = reduce_stats(stats, ACROSS, ALONG)
+    )
+    (got,) = reduce_stats(stats, ACROSS, ALONG)
     out, bound = call(
         pool_kernel,
         (got, stream_got, mid_gain, mid_bias, point, conv, pooled),

time: 143 us -> 141 us (0.986)
  blocking collectives: 106 us -> 114 us
  starting transfers between devices: 16.6 us -> 8.98 us
    all_to_all x3 -> x4, blocking collectives: 35.2 us -> 43.3 us  [reduce_stats(): got = lax.all_to_all(sent, first, 0, 0, tiled=True)]
    all_to_all x1 -> x0, starting transfers between devices: 7.6 us -> none  [reduce_stats(): got = lax.all_to_all(sent, first, 0, 0, tiled=True)]
    ppermute x2, starting transfers between devices: 7.52 us -> 4.87 us  [halos(): return (near, lax.ppermute(outer, SEQ, pairs + [(j, i) for i, j in pairs]))]
    ppermute x2, starting transfers between devices: 1.53 us -> 4.1 us  [halos(): near = lax.ppermute(facing, SEQ, [(i, i ^ 1) for i in range(peers)])]
    unnamed x18 -> x14, local copies, waits for them, and re-layouts: 3.03 us -> 1.61 us
  transfers between devices with their start and end apart: 5 -> 4, of which waited for: 1 -> 0; matrix products, arithmetic and copies ran while one was open for 0% -> 0% of each run, Pallas kernels for 0% -> 0%
where the time goes in v5:
time: 141 us; the launch traced here: 140 us
  blocking collectives  114 us (81%)
  Pallas kernels  13.3 us (9%)
  starting transfers between devices  8.98 us (6%)
  local copies, waits for them, and re-layouts  2.78 us (2%)
    all_to_all x4, blocking collectives, reduce_stats(): lax.all_to_all(jnp.broadcast_to(both[None], sent.shape), second, 0, 0, ti...  54.7 us
    all_to_all x4, blocking collectives, reduce_stats(): got = lax.all_to_all(sent, first, 0, 0, tiled=True)  43.3 us
    all_to_all x1, blocking collectives, per_device(): lax.all_to_all(out.reshape(CH // HEADS, HEADS, bins).astype(jnp.float16),...  16 us
    pallas_call x5, Pallas kernels, call(): pl.pallas_call(body, out_shape=[jax.ShapeDtypeStruct(s, d) for s, d in ou...  13.3 us
    ppermute x2, starting transfers between devices, halos(): return (near, lax.ppermute(outer, SEQ, pairs + [(j, i) for i, j in pairs]))  4.87 us
    ppermute x2, starting transfers between devices, halos(): near = lax.ppermute(facing, SEQ, [(i, i ^ 1) for i in range(peers)])  4.1 us
  transfers between devices with their start and end apart: 4, of which 0 were waited for; matrix products, arithmetic and copies ran while one was open for 0% of the time, Pallas kernels for 0%

profile of v5, /device:TPU:1, one launch (start us, length us, event | category | flops | bytes accessed | tf_op | source)
XLA Modules:
  0.0 140.1 jit_solution(17999125795051445304)
XLA Ops:
  0.0 0.1 pad_add_fusion.place_ref
  0.1 1.6 %copy-done = bf16[1,2048,512]{2,1,0:T(8,128)(2,1)S(1)} copy-done((bf16[1,2048,512]{2,1,0:T(8,128)(2,1)S(1)}, bf16[1,2048,512]{2,1,0:T(8,128)(2,1)}, u32[]{:S(2)}) %copy-start) | copy-done | bytes 2097176
  1.7 1.5 %shard_map.73 = (bf16[512,512]{1,0:T(8,128)(2,1)S(1)}, bf16[512,512]{1,0:T(8,128)(2,1)S(1)}, f32[16,8,128]{2,1,0:T(8,128)S(1)}) custom-call(s32[2]{0:T(128)S(1)} %pad_add_fusion.place_ref, bf16[2048,512]{1,0:T(8,128)(2,1)S(1)} %bitcast.12), custom_call_target="tpu_custom_call" | custom-call | tf_op jit(solution)/shard_map/pallas_call | solution.py:290
  3.2 14.1 %all_to_all.45 = f32[16,8,128]{2,1,0:T(8,128)S(1)} all-to-all(f32[16,8,128]{2,1,0:T(8,128)S(1)} %get-tuple-element.25), channel_id=1, replica_groups=mesh['y_lo'=2,'x'=4,'z'=8,'y_hi'=2,'core'=2] {'y_lo','x','y_hi'}, dimensions={0} | all-to-all | bytes 131072 | tf_op jit(solution)/shard_map/all_to_all | solution.py:308
  17.4 2.2 %collective-permute-start = (bf16[512,512]{1,0:T(8,128)(2,1)S(1)}, bf16[512,512]{1,0:T(8,128)(2,1)S(1)}, u32[]{:S(2)}, u32[]{:S(2)}) collective-permute-start(bf16[512,512]{1,0:T(8,128)(2,1)S(1)} %get-tuple-element.29), channel_id=1, source_target_pairs={{0,1},{1,0},{2,3},{3,2},{4,5},{5,4},{6,7},{7,6},{8,9},{9,8},{10,11... | collective-permute-start | bytes 1572872 | tf_op jit(solution)/shard_map/ppermute | solution.py:302
  19.6 2.4 %collective-permute-start.1 = (bf16[512,512]{1,0:T(8,128)(2,1)S(1)}, bf16[512,512]{1,0:T(8,128)(2,1)S(1)}, u32[]{:S(2)}, u32[]{:S(2)}) collective-permute-start(bf16[512,512]{1,0:T(8,128)(2,1)S(1)} %get-tuple-element.30), channel_id=1, source_target_pairs={{1,2},{3,4},{5,6},{7,8},{9,10},{11,12},{13,14},{15,16},{17,18},{19... | collective-permute-start | bytes 1572872 | tf_op jit(solution)/shard_map/ppermute | solution.py:304
  22.1 16.6 %all_to_all.46.got_ref = f32[16,8,128]{2,1,0:T(8,128)S(1)} all-to-all(f32[16,8,128]{2,1,0:T(8,128)S(1)} %broadcast_in_dim.8), channel_id=1, replica_groups=mesh['y_lo'=2,'x'=4,'z'=8,'y_hi'=2,'core'=2] {'z','core'}, dimensions={0} | all-to-all | bytes 131072 | tf_op jit(solution)/shard_map/all_to_all | solution.py:318
  38.6 0.0 collective-permute-done.near_ref
  38.6 0.0 collective-permute-done.1.cross_ref
  38.6 0.0 copy-done.4
  38.7 0.0 copy-done.3
  38.7 0.0 copy-done.1
  38.7 3.4 %shard_map.74 = (f32[2048,256]{1,0:T(8,128)S(1)}, f32[16,4,128]{2,1,0:T(4,128)S(1)}) custom-call(s32[2]{0:T(128)S(1)} %pad_add_fusion.place_ref, f32[16,8,128]{2,1,0:T(8,128)S(1)} %all_to_all.46.got_ref, f32[2,512]{1,0:T(2,128)S(1)} %copy-done.3, f32[2,512]{1,0:T(2,128)S(1)} %copy-done.4, bf16[2,3,512,256]{3,2,1,0:T(8,128)(2,1)S(1)} %copy-done.1, ...), custom_call_target="tpu_custom_call" | custom-call | tf_op jit(solution)/shard_map/pallas_call | solution.py:290
  42.0 10.4 %all_to_all.47 = f32[16,4,128]{2,1,0:T(4,128)S(1)} all-to-all(f32[16,4,128]{2,1,0:T(4,128)S(1)} %get-tuple-element.31), channel_id=1, replica_groups=mesh['y_lo'=2,'x'=4,'z'=8,'y_hi'=2,'core'=2] {'y_lo','x','y_hi'}, dimensions={0} | all-to-all | bytes 65536 | tf_op jit(solution)/shard_map/all_to_all | solution.py:308
  52.6 14.5 %all_to_all.48.got_ref = f32[16,4,128]{2,1,0:T(4,128)S(1)} all-to-all(f32[16,4,128]{2,1,0:T(4,128)S(1)} %broadcast_in_dim.9), channel_id=1, replica_groups=mesh['y_lo'=2,'x'=4,'z'=8,'y_hi'=2,'core'=2] {'z','core'}, dimensions={0} | all-to-all | bytes 65536 | tf_op jit(solution)/shard_map/all_to_all | solution.py:318
  67.1 0.0 copy-done.2
  67.1 0.0 copy-done.6
  67.1 3.1 %shard_map.75 = (f32[2048,512]{1,0:T(8,128)S(1)}, bf16[512,256]{1,0:T(8,128)(2,1)S(1)}, bf16[512,256]{1,0:T(8,128)(2,1)S(1)}, f32[16,8,128]{2,1,0:T(8,128)S(1)}, f32[256,512]{1,0:T(8,128)S(1)}) custom-call(s32[2]{0:T(128)S(1)} %pad_add_fusion.place_ref, f32[16,4,128]{2,1,0:T(4,128)S(1)} %all_to_all.48.got_ref, f32[2,256]{1,0:T(2,128)S(1)} %copy-done.5, ...), custom_call_target="tpu_custom_call" | custom-call | tf_op jit(solution)/shard_map/pallas_call | solution.py:290
  70.3 9.4 %all_to_all.49 = f32[16,8,128]{2,1,0:T(8,128)S(1)} all-to-all(f32[16,8,128]{2,1,0:T(8,128)S(1)} %get-tuple-element.33), channel_id=1, replica_groups=mesh['y_lo'=2,'x'=4,'z'=8,'y_hi'=2,'core'=2] {'y_lo','x','y_hi'}, dimensions={0} | all-to-all | bytes 131072 | tf_op jit(solution)/shard_map/all_to_all | solution.py:308
  79.8 1.9 %collective-permute-start.2 = (bf16[512,256]{1,0:T(8,128)(2,1)S(1)}, bf16[512,256]{1,0:T(8,128)(2,1)S(1)}, u32[]{:S(2)}, u32[]{:S(2)}) collective-permute-start(bf16[512,256]{1,0:T(8,128)(2,1)S(1)} %get-tuple-element.37), channel_id=1, source_target_pairs={{0,1},{1,0},{2,3},{3,2},{4,5},{5,4},{6,7},{7,6},{8,9},{9,8},{10,11... | collective-permute-start | bytes 786440 | tf_op jit(solution)/shard_map/ppermute | solution.py:302
  81.7 2.4 %collective-permute-start.3 = (bf16[512,256]{1,0:T(8,128)(2,1)S(1)}, bf16[512,256]{1,0:T(8,128)(2,1)S(1)}, u32[]{:S(2)}, u32[]{:S(2)}) collective-permute-start(bf16[512,256]{1,0:T(8,128)(2,1)S(1)} %get-tuple-element.39), channel_id=1, source_target_pairs={{1,2},{3,4},{5,6},{7,8},{9,10},{11,12},{13,14},{15,16},{17,18},{19... | collective-permute-start | bytes 786440 | tf_op jit(solution)/shard_map/ppermute | solution.py:304
  84.2 12.1 %all_to_all.50.got_ref.stream_got_ref = f32[16,8,128]{2,1,0:T(8,128)S(1)} all-to-all(f32[16,8,128]{2,1,0:T(8,128)S(1)} %broadcast_in_dim.10), channel_id=1, replica_groups=mesh['y_lo'=2,'x'=4,'z'=8,'y_hi'=2,'core'=2] {'z','core'}, dimensions={0} | all-to-all | bytes 131072 | tf_op jit(solution)/shard_map/all_to_all | solution.py:318
  96.3 0.0 collective-permute-done.2.near_gated_ref
  96.3 0.0 collective-permute-done.3.cross_gated_ref
  96.3 4.1 %shard_map.76 = (f32[2048,256]{1,0:T(8,128)S(1)}, f32[16,4,128]{2,1,0:T(4,128)S(1)}) custom-call(s32[2]{0:T(128)S(1)} %pad_add_fusion.place_ref, f32[16,8,128]{2,1,0:T(8,128)S(1)} %all_to_all.50.got_ref.stream_got_ref, f32[2,512]{1,0:T(2,128)S(1)} %copy-done.3, f32[2,512]{1,0:T(2,128)S(1)} %copy-done.4, bf16[2,3,512,256]{3,2,1,0:T(8,128)(2,1)S(1)} %copy-done.1, ...), custom_call_target="tpu_custom_call" | custom-call | tf_op jit(solution)/shard_map/pallas_call | solution.py:290
  100.4 9.3 %all_to_all.51 = f32[16,4,128]{2,1,0:T(4,128)S(1)} all-to-all(f32[16,4,128]{2,1,0:T(4,128)S(1)} %get-tuple-element.40), channel_id=1, replica_groups=mesh['y_lo'=2,'x'=4,'z'=8,'y_hi'=2,'core'=2] {'y_lo','x','y_hi'}, dimensions={0} | all-to-all | bytes 65536 | tf_op jit(solution)/shard_map/all_to_all | solution.py:308
  109.9 11.5 %all_to_all.52.got_ref = f32[16,4,128]{2,1,0:T(4,128)S(1)} all-to-all(f32[16,4,128]{2,1,0:T(4,128)S(1)} %broadcast_in_dim.11), channel_id=1, replica_groups=mesh['y_lo'=2,'x'=4,'z'=8,'y_hi'=2,'core'=2] {'z','core'}, dimensions={0} | all-to-all | bytes 65536 | tf_op jit(solution)/shard_map/all_to_all | solution.py:318
  121.3 1.2 shard_map.77
  122.6 16.0 %all_to_all.53 = f16[64,8,256]{2,1,0:T(8,128)(2,1)S(1)} all-to-all(f16[64,8,256]{2,1,0:T(8,128)(2,1)S(1)} %convert_bitcast_fusion), channel_id=1, replica_groups=mesh['y_lo'=2,'x'=4,'z'=8,'y_hi'=2,'core'=2] {'z','y_hi','core'}, dimensions={0} | all-to-all | bytes 524288 | tf_op jit(solution)/shard_map/all_to_all | solution.py:379
  138.6 0.1 convert.2
  138.6 0.3 fusion
  139.0 1.1 reshape.35
  (33 shorter events, 0.4 us)
Async XLA Ops:
  0.0 38.7 %copy-start.4 = (f32[2,512]{1,0:T(2,128)S(1)}, f32[2,512]{1,0:T(2,128)}, u32[]{:S(2)}) copy-start(f32[2,512]{1,0:T(2,128)} %bias_ref.6) | copy-start | bytes 12292
  0.0 38.7 %copy-start.3 = (f32[2,512]{1,0:T(2,128)S(1)}, f32[2,512]{1,0:T(2,128)}, u32[]{:S(2)}) copy-start(f32[2,512]{1,0:T(2,128)} %gain_ref.6) | copy-start | bytes 12292
  0.1 1.6 %copy-start = (bf16[1,2048,512]{2,1,0:T(8,128)(2,1)S(1)}, bf16[1,2048,512]{2,1,0:T(8,128)(2,1)}, u32[]{:S(2)}) copy-start(bf16[1,2048,512]{2,1,0:T(8,128)(2,1)} %param.7) | copy-start | bytes 6291460
  1.7 37.0 %copy-start.1 = (bf16[2,3,512,256]{3,2,1,0:T(8,128)(2,1)S(1)}, bf16[2,3,512,256]{3,2,1,0:T(8,128)(2,1)}, u32[]{:S(2)}) copy-start(bf16[2,3,512,256]{3,2,1,0:T(8,128)(2,1)} %taps_ref.3) | copy-start | bytes 4718596
  17.4 21.2 %collective-permute-start = (bf16[512,512]{1,0:T(8,128)(2,1)S(1)}, bf16[512,512]{1,0:T(8,128)(2,1)S(1)}, u32[]{:S(2)}, u32[]{:S(2)}) collective-permute-start(bf16[512,512]{1,0:T(8,128)(2,1)S(1)} %get-tuple-element.29), channel_id=1, source_target_pairs={{0,1},{1,0},{2,3},{3,2},{4,5},{5,4},{6,7},{7,6},{8,9},{9,8},{10,11... | collective-permute-start | bytes 1572872 | tf_op jit(solution)/shard_map/ppermute | solution.py:302
  19.6 19.0 %collective-permute-start.1 = (bf16[512,512]{1,0:T(8,128)(2,1)S(1)}, bf16[512,512]{1,0:T(8,128)(2,1)S(1)}, u32[]{:S(2)}, u32[]{:S(2)}) collective-permute-start(bf16[512,512]{1,0:T(8,128)(2,1)S(1)} %get-tuple-element.30), channel_id=1, source_target_pairs={{1,2},{3,4},{5,6},{7,8},{9,10},{11,12},{13,14},{15,16},{17,18},{19... | collective-permute-start | bytes 1572872 | tf_op jit(solution)/shard_map/ppermute | solution.py:304
  38.6 28.5 %copy-start.2 = (bf16[2,256,512]{2,1,0:T(8,128)(2,1)S(1)}, bf16[2,256,512]{2,1,0:T(8,128)(2,1)}, u32[]{:S(2)}) copy-start(bf16[2,256,512]{2,1,0:T(8,128)(2,1)} %point_ref.5) | copy-start | bytes 1572868
  38.6 28.5 %copy-start.5 = (f32[2,256]{1,0:T(2,128)S(1)}, f32[2,256]{1,0:T(2,128)}, u32[]{:S(2)}) copy-start(f32[2,256]{1,0:T(2,128)} %gain_ref.7) | copy-start | bytes 6148
  38.6 28.5 %copy-start.6 = (f32[2,256]{1,0:T(2,128)S(1)}, f32[2,256]{1,0:T(2,128)}, u32[]{:S(2)}) copy-start(f32[2,256]{1,0:T(2,128)} %bias_ref.7) | copy-start | bytes 6148
  79.8 16.5 %collective-permute-start.2 = (bf16[512,256]{1,0:T(8,128)(2,1)S(1)}, bf16[512,256]{1,0:T(8,128)(2,1)S(1)}, u32[]{:S(2)}, u32[]{:S(2)}) collective-permute-start(bf16[512,256]{1,0:T(8,128)(2,1)S(1)} %get-tuple-element.37), channel_id=1, source_target_pairs={{0,1},{1,0},{2,3},{3,2},{4,5},{5,4},{6,7},{7,6},{8,9},{9,8},{10,11... | collective-permute-start | bytes 786440 | tf_op jit(solution)/shard_map/ppermute | solution.py:302
  81.7 14.6 %collective-permute-start.3 = (bf16[512,256]{1,0:T(8,128)(2,1)S(1)}, bf16[512,256]{1,0:T(8,128)(2,1)S(1)}, u32[]{:S(2)}, u32[]{:S(2)}) collective-permute-start(bf16[512,256]{1,0:T(8,128)(2,1)S(1)} %get-tuple-element.39), channel_id=1, source_target_pairs={{1,2},{3,4},{5,6},{7,8},{9,10},{11,12},{13,14},{15,16},{17,18},{19... | collective-permute-start | bytes 786440 | tf_op jit(solution)/shard_map/ppermute | solution.py:304

commit v6 on v5

--- a/solution.py
+++ b/solution.py
@@ -92,6 +92,14 @@
 
         squares = lax.fori_loop(0, ref.shape[0] // 64, step, squares, unroll=4)
     return jnp.sum(squares, axis=0, keepdims=True)
+
+
+def pack_edges(core, gated_ref, x_ref, facing_ref, outer_ref):
+    put_edges(core, gated_ref, facing_ref.at[:, :MID], outer_ref.at[:, :MID])
+    for last, edge_ref in ((1 - core, facing_ref), (core, outer_ref)):
+        rows = pl.ds(pl.multiple_of(NEAR + last * (ROWS - FAR - NEAR), NEAR), NEAR)
+        edge_ref[:NEAR, MID:] = x_ref[rows, :MID]
+        edge_ref[NEAR:, MID:] = x_ref[rows, MID:]
 
 
 def input_stats(place_ref, x_ref, facing_ref, outer_ref, out_ref):
@@ -159,8 +167,8 @@
 ):
     terms = norm_terms(0, got_ref, gain_ref, bias_ref)
     core = place_ref[0]
-    activate(near_ref, core * (FAR - NEAR), NEAR, terms, act_ref, (1 - core) * (NEAR + ROWS))
-    activate(cross_ref, (1 - core) * (FAR - NEAR), NEAR, terms, act_ref, core * (NEAR + ROWS), place_ref[1])
+    activate(near_ref, 0, NEAR, terms, act_ref, (1 - core) * (NEAR + ROWS))
+    activate(cross_ref, 0, NEAR, terms, act_ref, core * (NEAR + ROWS), place_ref[1])
     weights = taps_ref[0].reshape(3 * CH, MID)
     conv_tiles(NEAR, 256, terms, center_ref, weights, conv_ref, stats_ref, act_ref)
 
@@ -173,10 +181,10 @@
     taps_ref,
     point_ref,
     near_ref,
-    near_gated_ref,
+    near_packed_ref,
     center_ref,
     cross_ref,
-    cross_gated_ref,
+    cross_packed_ref,
     conv_ref,
     stats_ref,
     act_ref,
@@ -185,12 +193,16 @@
 ):
     terms = norm_terms(1, got_ref, gain_ref, bias_ref)
     core = place_ref[0]
-    for x_ref, gated_ref, stream_ref in (
-        (near_ref, near_gated_ref, near_stream_ref),
-        (cross_ref, cross_gated_ref, cross_stream_ref),
+    for side, x_ref, packed_ref, stream_ref in (
+        (core, near_ref, near_packed_ref, near_stream_ref),
+        (1 - core, cross_ref, cross_packed_ref, cross_stream_ref),
     ):
-        branch = jnp.dot(gated_ref[...], point_ref[0], preferred_element_type=F32)
-        stream_ref[...] = x_ref[...].astype(F32) + branch
+        stream_ref[...] = jnp.dot(packed_ref[:, :MID], point_ref[0], preferred_element_type=F32)
+        close = pl.ds(pl.multiple_of(side * NEAR, NEAR), NEAR)
+        distant = pl.ds(pl.multiple_of((1 - side) * NEAR, NEAR), NEAR)
+        stream_ref[close, :] += x_ref[...].astype(F32)
+        stream_ref[distant, :MID] += packed_ref[:NEAR, MID:].astype(F32)
+        stream_ref[distant, MID:] += packed_ref[NEAR:, MID:].astype(F32)
     activate(near_stream_ref, 0, FAR, terms, act_ref, (1 - core) * (FAR + ROWS))
     activate(cross_stream_ref, 0, FAR, terms, act_ref, core * (FAR + ROWS), place_ref[1])
     weights = taps_ref[1].reshape(3 * CH, MID)
@@ -236,7 +248,7 @@
         stream_ref[rows, :] = total
         pool_ref[i * bins : (i + 1) * bins, :] = jnp.sum(total.reshape(bins, POOL, CH), axis=1)
         acc = acc + fold(total)
-    put_edges(place_ref[0], gated_ref, facing_ref, outer_ref)
+    pack_edges(place_ref[0], gated_ref, x_ref, facing_ref, outer_ref)
     mean = jnp.sum(acc, axis=0, keepdims=True) * (1.0 / ROWS)
     put_stats(stats_ref, mean, deviations((stream_ref,), mean, CH))
 
@@ -328,14 +340,15 @@
     slim_stats = ((PEERS, 4, 128), F32)
     conv_outs = [((ROWS, MID), F32), slim_stats]
 
-    edge = ((FAR, CH), BF16)
+    edge = ((NEAR, CH), BF16)
     facing, outer, stats = call(
         input_stats,
         (where, x),
         [edge, edge, wide_stats],
         scalars=1,
     )
-    got, near, cross = reduce_stats(stats, ACROSS, ALONG, facing, outer)
+    near, cross = halos(facing, outer)
+    (got,) = reduce_stats(stats, ACROSS, ALONG)
     conv, stats = call(
         first_conv,
         (where, got, in_gain, in_bias, taps, near, x, cross),
@@ -344,7 +357,7 @@
         1,
     )
     (got,) = reduce_stats(stats, ACROSS, ALONG)
-    edge = ((FAR, MID), BF16)
+    edge = ((FAR, CH), BF16)
     stream, facing, outer, stats, pooled = call(
         point_kernel,
         (where, got, mid_gain, mid_bias, point, conv, x),
@@ -352,10 +365,10 @@
         [pltpu.VMEM((ROWS, MID), BF16)],
         1,
     )
-    stream_got, near_gated, cross_gated = reduce_stats(stats, ACROSS, ALONG, facing, outer)
+    stream_got, near_packed, cross_packed = reduce_stats(stats, ACROSS, ALONG, facing, outer)
     conv, stats = call(
         second_conv,
-        (where, stream_got, in_gain, in_bias, taps, point, near, near_gated, stream, cross, cross_gated),
+        (where, stream_got, in_gain, in_bias, taps, point, near, near_packed, stream, cross, cross_packed),
         conv_outs,
         [
             pltpu.VMEM((ROWS + 2 * FAR, CH), BF16),

time: 141 us -> 139 us (0.986)
  blocking collectives: 114 us -> 100 us
  starting transfers between devices: 8.98 us -> 17.8 us
  local copies, waits for them, and re-layouts: 2.78 us -> 4.19 us
    all_to_all x4 -> x3, blocking collectives: 43.3 us -> 28 us  [reduce_stats(): got = lax.all_to_all(sent, first, 0, 0, tiled=True)]
    all_to_all x0 -> x1, starting transfers between devices: none -> 7.58 us  [reduce_stats(): got = lax.all_to_all(sent, first, 0, 0, tiled=True)]
    ppermute x2, starting transfers between devices: 4.87 us -> 7.3 us  [halos(): return (near, lax.ppermute(outer, SEQ, pairs + [(j, i) for i, j in pairs]))]
    all_to_all x4, blocking collectives: 54.7 us -> 56.2 us  [reduce_stats(): lax.all_to_all(jnp.broadcast_to(both[None], sent.shape), second, 0, 0, ti...]
    unnamed x14 -> x18, local copies, waits for them, and re-layouts: 1.61 us -> 3.03 us
  transfers between devices with their start and end apart: 4 -> 5, of which waited for: 0 -> 1; matrix products, arithmetic and copies ran while one was open for 0% -> 0% of each run, Pallas kernels for 0% -> 0%
where the time goes in v6:
time: 139 us; the launch traced here: 138 us
  blocking collectives  100 us (72%)
  starting transfers between devices  17.8 us (13%)
  Pallas kernels  14 us (10%)
  local copies, waits for them, and re-layouts  4.19 us (3%)
    all_to_all x4, blocking collectives, reduce_stats(): lax.all_to_all(jnp.broadcast_to(both[None], sent.shape), second, 0, 0, ti...  56.2 us
    all_to_all x3, blocking collectives, reduce_stats(): got = lax.all_to_all(sent, first, 0, 0, tiled=True)  28 us
    all_to_all x1, blocking collectives, per_device(): lax.all_to_all(out.reshape(CH // HEADS, HEADS, bins).astype(jnp.float16),...  16 us
    pallas_call x5, Pallas kernels, call(): pl.pallas_call(body, out_shape=[jax.ShapeDtypeStruct(s, d) for s, d in ou...  14 us
    all_to_all x1, starting transfers between devices, reduce_stats(): got = lax.all_to_all(sent, first, 0, 0, tiled=True)  7.58 us
    ppermute x2, starting transfers between devices, halos(): return (near, lax.ppermute(outer, SEQ, pairs + [(j, i) for i, j in pairs]))  7.3 us
    unnamed x18, local copies, waits for them, and re-layouts  3.03 us
    ppermute x2, starting transfers between devices, halos(): near = lax.ppermute(facing, SEQ, [(i, i ^ 1) for i in range(peers)])  2.95 us
  transfers between devices with their start and end apart: 5, of which 1 were waited for; matrix products, arithmetic and copies ran while one was open for 0% of the time, Pallas kernels for 0%

profile of v6, /device:TPU:1, one launch (start us, length us, event | category | flops | bytes accessed | tf_op | source)
XLA Modules:
  0.0 138.0 jit_solution(11190578453024270463)
XLA Ops:
  0.0 0.1 pad_add_fusion.place_ref
  0.1 1.6 %copy-done = bf16[1,2048,512]{2,1,0:T(8,128)(2,1)S(1)} copy-done((bf16[1,2048,512]{2,1,0:T(8,128)(2,1)S(1)}, bf16[1,2048,512]{2,1,0:T(8,128)(2,1)}, u32[]{:S(2)}) %copy-start) | copy-done | bytes 2097176
  1.7 2.1 %shard_map.73 = (bf16[256,512]{1,0:T(8,128)(2,1)S(1)}, bf16[256,512]{1,0:T(8,128)(2,1)S(1)}, f32[16,8,128]{2,1,0:T(8,128)}) custom-call(s32[2]{0:T(128)S(1)} %pad_add_fusion.place_ref, bf16[2048,512]{1,0:T(8,128)(2,1)S(1)} %bitcast.12), custom_call_target="tpu_custom_call" | custom-call | tf_op jit(solution)/shard_map/pallas_call | solution.py:302
  3.8 7.6 %all-to-all-start = ((f32[16,8,128]{2,1,0:T(8,128)}), f32[16,8,128]{2,1,0:T(8,128)S(1)}, u32[]{:S(2)}, u32[]{:S(2)}) async-start(f32[16,8,128]{2,1,0:T(8,128)} %get-tuple-element.22), calls=%async_computation | async-start | bytes 131072 | tf_op jit(solution)/shard_map/all_to_all | solution.py:320
  11.4 1.0 collective-permute-start
  12.4 4.9 %collective-permute-start.1 = (bf16[256,512]{1,0:T(8,128)(2,1)S(1)}, bf16[256,512]{1,0:T(8,128)(2,1)S(1)}, u32[]{:S(2)}, u32[]{:S(2)}) collective-permute-start(bf16[256,512]{1,0:T(8,128)(2,1)S(1)} %get-tuple-element.24), channel_id=1, source_target_pairs={{1,2},{3,4},{5,6},{7,8},{9,10},{11,12},{13,14},{15,16},{17,18},{19... | collective-permute-start | bytes 786440 | tf_op jit(solution)/shard_map/ppermute | solution.py:316
  17.3 0.8 all-to-all-done
  18.2 0.0 copy-start.7
  18.2 0.0 copy-start.8
  18.2 18.2 %all_to_all.45.got_ref = f32[16,8,128]{2,1,0:T(8,128)S(1)} all-to-all(f32[16,8,128]{2,1,0:T(8,128)S(1)} %broadcast_in_dim.8), channel_id=1, replica_groups=mesh['y_lo'=2,'x'=4,'z'=8,'y_hi'=2,'core'=2] {'z','core'}, dimensions={0} | all-to-all | bytes 131072 | tf_op jit(solution)/shard_map/all_to_all | solution.py:330
  36.4 0.0 collective-permute-done.near_ref
  36.4 0.0 collective-permute-done.1.cross_ref
  36.5 0.0 copy-start.2
  36.5 1.4 %copy-done.2 = bf16[2,3,512,256]{3,2,1,0:T(8,128)(2,1)S(1)} copy-done((bf16[2,3,512,256]{3,2,1,0:T(8,128)(2,1)S(1)}, bf16[2,3,512,256]{3,2,1,0:T(8,128)(2,1)}, u32[]{:S(2)}) %copy-start.2) | copy-done | bytes 1572888
  37.9 3.3 %shard_map.74 = (f32[2048,256]{1,0:T(8,128)S(1)}, f32[16,4,128]{2,1,0:T(4,128)S(1)}) custom-call(s32[2]{0:T(128)S(1)} %pad_add_fusion.place_ref, f32[16,8,128]{2,1,0:T(8,128)S(1)} %all_to_all.45.got_ref, f32[2,512]{1,0:T(2,128)S(1)} %copy-done.5, f32[2,512]{1,0:T(2,128)S(1)} %copy-done.6, bf16[2,3,512,256]{3,2,1,0:T(8,128)(2,1)S(1)} %copy-done.2, ...), custom_call_target="tpu_custom_call" | custom-call | tf_op jit(solution)/shard_map/pallas_call | solution.py:302
  41.2 9.3 %all_to_all.46 = f32[16,4,128]{2,1,0:T(4,128)S(1)} all-to-all(f32[16,4,128]{2,1,0:T(4,128)S(1)} %get-tuple-element.25), channel_id=1, replica_groups=mesh['y_lo'=2,'x'=4,'z'=8,'y_hi'=2,'core'=2] {'y_lo','x','y_hi'}, dimensions={0} | all-to-all | bytes 65536 | tf_op jit(solution)/shard_map/all_to_all | solution.py:320
  50.6 11.5 %all_to_all.47.got_ref = f32[16,4,128]{2,1,0:T(4,128)S(1)} all-to-all(f32[16,4,128]{2,1,0:T(4,128)S(1)} %broadcast_in_dim.9), channel_id=1, replica_groups=mesh['y_lo'=2,'x'=4,'z'=8,'y_hi'=2,'core'=2] {'z','core'}, dimensions={0} | all-to-all | bytes 65536 | tf_op jit(solution)/shard_map/all_to_all | solution.py:330
  62.1 0.0 copy-start.3
  62.1 3.1 %shard_map.75 = (f32[2048,512]{1,0:T(8,128)S(1)}, bf16[512,512]{1,0:T(8,128)(2,1)S(1)}, bf16[512,512]{1,0:T(8,128)(2,1)S(1)}, f32[16,8,128]{2,1,0:T(8,128)S(1)}, f32[256,512]{1,0:T(8,128)S(1)}) custom-call(s32[2]{0:T(128)S(1)} %pad_add_fusion.place_ref, f32[16,4,128]{2,1,0:T(4,128)S(1)} %all_to_all.47.got_ref, f32[2,256]{1,0:T(2,128)S(1)} %copy-done.7, ...), custom_call_target="tpu_custom_call" | custom-call | tf_op jit(solution)/shard_map/pallas_call | solution.py:302
  65.2 9.4 %all_to_all.48 = f32[16,8,128]{2,1,0:T(8,128)S(1)} all-to-all(f32[16,8,128]{2,1,0:T(8,128)S(1)} %get-tuple-element.27), channel_id=1, replica_groups=mesh['y_lo'=2,'x'=4,'z'=8,'y_hi'=2,'core'=2] {'y_lo','x','y_hi'}, dimensions={0} | all-to-all | bytes 131072 | tf_op jit(solution)/shard_map/all_to_all | solution.py:320
  74.7 1.9 %collective-permute-start.2 = (bf16[512,512]{1,0:T(8,128)(2,1)S(1)}, bf16[512,512]{1,0:T(8,128)(2,1)S(1)}, u32[]{:S(2)}, u32[]{:S(2)}) collective-permute-start(bf16[512,512]{1,0:T(8,128)(2,1)S(1)} %get-tuple-element.31), channel_id=1, source_target_pairs={{0,1},{1,0},{2,3},{3,2},{4,5},{5,4},{6,7},{7,6},{8,9},{9,8},{10,11... | collective-permute-start | bytes 1572872 | tf_op jit(solution)/shard_map/ppermute | solution.py:314
  76.6 2.4 %collective-permute-start.3 = (bf16[512,512]{1,0:T(8,128)(2,1)S(1)}, bf16[512,512]{1,0:T(8,128)(2,1)S(1)}, u32[]{:S(2)}, u32[]{:S(2)}) collective-permute-start(bf16[512,512]{1,0:T(8,128)(2,1)S(1)} %get-tuple-element.33), channel_id=1, source_target_pairs={{1,2},{3,4},{5,6},{7,8},{9,10},{11,12},{13,14},{15,16},{17,18},{19... | collective-permute-start | bytes 1572872 | tf_op jit(solution)/shard_map/ppermute | solution.py:316
  79.1 12.1 %all_to_all.49.got_ref.stream_got_ref = f32[16,8,128]{2,1,0:T(8,128)S(1)} all-to-all(f32[16,8,128]{2,1,0:T(8,128)S(1)} %broadcast_in_dim.10), channel_id=1, replica_groups=mesh['y_lo'=2,'x'=4,'z'=8,'y_hi'=2,'core'=2] {'z','core'}, dimensions={0} | all-to-all | bytes 131072 | tf_op jit(solution)/shard_map/all_to_all | solution.py:330
  91.2 0.0 collective-permute-done.2.near_packed_ref
  91.2 4.3 %shard_map.76 = (f32[2048,256]{1,0:T(8,128)S(1)}, f32[16,4,128]{2,1,0:T(4,128)S(1)}) custom-call(s32[2]{0:T(128)S(1)} %pad_add_fusion.place_ref, f32[16,8,128]{2,1,0:T(8,128)S(1)} %all_to_all.49.got_ref.stream_got_ref, f32[2,512]{1,0:T(2,128)S(1)} %copy-done.5, f32[2,512]{1,0:T(2,128)S(1)} %copy-done.6, bf16[2,3,512,256]{3,2,1,0:T(8,128)(2,1)S(1)} %copy-done.3, ...), custom_call_target="tpu_custom_call" | custom-call | tf_op jit(solution)/shard_map/pallas_call | solution.py:302
  95.5 9.2 %all_to_all.50 = f32[16,4,128]{2,1,0:T(4,128)S(1)} all-to-all(f32[16,4,128]{2,1,0:T(4,128)S(1)} %get-tuple-element.34), channel_id=1, replica_groups=mesh['y_lo'=2,'x'=4,'z'=8,'y_hi'=2,'core'=2] {'y_lo','x','y_hi'}, dimensions={0} | all-to-all | bytes 65536 | tf_op jit(solution)/shard_map/all_to_all | solution.py:320
  104.8 14.4 %all_to_all.51.got_ref = f32[16,4,128]{2,1,0:T(4,128)S(1)} all-to-all(f32[16,4,128]{2,1,0:T(4,128)S(1)} %broadcast_in_dim.11), channel_id=1, replica_groups=mesh['y_lo'=2,'x'=4,'z'=8,'y_hi'=2,'core'=2] {'z','core'}, dimensions={0} | all-to-all | bytes 65536 | tf_op jit(solution)/shard_map/all_to_all | solution.py:330
  119.3 1.2 shard_map.77
  120.5 16.0 %all_to_all.52 = f16[64,8,256]{2,1,0:T(8,128)(2,1)S(1)} all-to-all(f16[64,8,256]{2,1,0:T(8,128)(2,1)S(1)} %convert_bitcast_fusion), channel_id=1, replica_groups=mesh['y_lo'=2,'x'=4,'z'=8,'y_hi'=2,'core'=2] {'z','y_hi','core'}, dimensions={0} | all-to-all | bytes 524288 | tf_op jit(solution)/shard_map/all_to_all | solution.py:392
  136.5 0.1 convert.2
  136.6 0.3 fusion
  136.9 1.1 reshape.35
  (38 shorter events, 0.4 us)
Async XLA Ops:
  0.0 36.4 %copy-start.6 = (f32[2,512]{1,0:T(2,128)S(1)}, f32[2,512]{1,0:T(2,128)}, u32[]{:S(2)}) copy-start(f32[2,512]{1,0:T(2,128)} %bias_ref.6) | copy-start | bytes 12292
  0.0 36.4 %copy-start.5 = (f32[2,512]{1,0:T(2,128)S(1)}, f32[2,512]{1,0:T(2,128)}, u32[]{:S(2)}) copy-start(f32[2,512]{1,0:T(2,128)} %gain_ref.6) | copy-start | bytes 12292
  0.1 1.6 %copy-start = (bf16[1,2048,512]{2,1,0:T(8,128)(2,1)S(1)}, bf16[1,2048,512]{2,1,0:T(8,128)(2,1)}, u32[]{:S(2)}) copy-start(bf16[1,2048,512]{2,1,0:T(8,128)(2,1)} %param.7) | copy-start | bytes 6291460
  1.7 34.8 %copy-start.1 = (bf16[1,2048,512]{2,1,0:T(8,128)(2,1)S(1)}, bf16[1,2048,512]{2,1,0:T(8,128)(2,1)}, u32[]{:S(2)}) copy-start(bf16[1,2048,512]{2,1,0:T(8,128)(2,1)} %param.7) | copy-start | bytes 6291460
  3.8 14.3 %all-to-all-start = ((f32[16,8,128]{2,1,0:T(8,128)}), f32[16,8,128]{2,1,0:T(8,128)S(1)}, u32[]{:S(2)}, u32[]{:S(2)}) async-start(f32[16,8,128]{2,1,0:T(8,128)} %get-tuple-element.22), calls=%async_computation | async-start | bytes 131072 | tf_op jit(solution)/shard_map/all_to_all | solution.py:320
  11.4 25.0 %collective-permute-start = (bf16[256,512]{1,0:T(8,128)(2,1)S(1)}, bf16[256,512]{1,0:T(8,128)(2,1)S(1)}, u32[]{:S(2)}, u32[]{:S(2)}) collective-permute-start(bf16[256,512]{1,0:T(8,128)(2,1)S(1)} %get-tuple-element.23), channel_id=1, source_target_pairs={{0,1},{1,0},{2,3},{3,2},{4,5},{5,4},{6,7},{7,6},{8,9},{9,8},{10,11... | collective-permute-start | bytes 786440 | tf_op jit(solution)/shard_map/ppermute | solution.py:314
  12.4 24.0 %collective-permute-start.1 = (bf16[256,512]{1,0:T(8,128)(2,1)S(1)}, bf16[256,512]{1,0:T(8,128)(2,1)S(1)}, u32[]{:S(2)}, u32[]{:S(2)}) collective-permute-start(bf16[256,512]{1,0:T(8,128)(2,1)S(1)} %get-tuple-element.24), channel_id=1, source_target_pairs={{1,2},{3,4},{5,6},{7,8},{9,10},{11,12},{13,14},{15,16},{17,18},{19... | collective-permute-start | bytes 786440 | tf_op jit(solution)/shard_map/ppermute | solution.py:316
  18.2 43.8 %copy-start.7 = (f32[2,256]{1,0:T(2,128)S(1)}, f32[2,256]{1,0:T(2,128)}, u32[]{:S(2)}) copy-start(f32[2,256]{1,0:T(2,128)} %gain_ref.7) | copy-start | bytes 6148
  18.2 43.8 %copy-start.8 = (f32[2,256]{1,0:T(2,128)S(1)}, f32[2,256]{1,0:T(2,128)}, u32[]{:S(2)}) copy-start(f32[2,256]{1,0:T(2,128)} %bias_ref.7) | copy-start | bytes 6148
  36.5 1.4 %copy-start.2 = (bf16[2,3,512,256]{3,2,1,0:T(8,128)(2,1)S(1)}, bf16[2,3,512,256]{3,2,1,0:T(8,128)(2,1)}, u32[]{:S(2)}) copy-start(bf16[2,3,512,256]{3,2,1,0:T(8,128)(2,1)} %taps_ref.3) | copy-start | bytes 4718596
  37.9 24.2 %copy-start.4 = (bf16[2,256,512]{2,1,0:T(8,128)(2,1)S(1)}, bf16[2,256,512]{2,1,0:T(8,128)(2,1)}, u32[]{:S(2)}) copy-start(bf16[2,256,512]{2,1,0:T(8,128)(2,1)} %point_ref.5) | copy-start | bytes 1572868
  62.1 29.2 %copy-start.3 = (bf16[2,3,512,256]{3,2,1,0:T(8,128)(2,1)S(1)}, bf16[2,3,512,256]{3,2,1,0:T(8,128)(2,1)}, u32[]{:S(2)}) copy-start(bf16[2,3,512,256]{3,2,1,0:T(8,128)(2,1)} %taps_ref.3) | copy-start | bytes 4718596
  74.7 16.5 %collective-permute-start.2 = (bf16[512,512]{1,0:T(8,128)(2,1)S(1)}, bf16[512,512]{1,0:T(8,128)(2,1)S(1)}, u32[]{:S(2)}, u32[]{:S(2)}) collective-permute-start(bf16[512,512]{1,0:T(8,128)(2,1)S(1)} %get-tuple-element.31), channel_id=1, source_target_pairs={{0,1},{1,0},{2,3},{3,2},{4,5},{5,4},{6,7},{7,6},{8,9},{9,8},{10,11... | collective-permute-start | bytes 1572872 | tf_op jit(solution)/shard_map/ppermute | solution.py:314
  76.6 14.6 %collective-permute-start.3 = (bf16[512,512]{1,0:T(8,128)(2,1)S(1)}, bf16[512,512]{1,0:T(8,128)(2,1)S(1)}, u32[]{:S(2)}, u32[]{:S(2)}) collective-permute-start(bf16[512,512]{1,0:T(8,128)(2,1)S(1)} %get-tuple-element.33), channel_id=1, source_target_pairs={{1,2},{3,4},{5,6},{7,8},{9,10},{11,12},{13,14},{15,16},{17,18},{19... | collective-permute-start | bytes 1572872 | tf_op jit(solution)/shard_map/ppermute | solution.py:316

commit v7 on v6

--- a/solution.py
+++ b/solution.py
@@ -102,6 +102,23 @@
         edge_ref[NEAR:, MID:] = x_ref[rows, MID:]
 
 
+def shifted(total, sums):
+    if sums is None:
+        pivot = jnp.sum(fold(total), axis=0, keepdims=True) * (1.0 / total.shape[0])
+        zero = jnp.zeros((8, total.shape[1]), F32)
+        sums = (pivot, zero, zero)
+    pivot, first, second = sums
+    d = total - pivot
+    return pivot, first + fold(d), second + fold(d * d)
+
+
+def put_shifted(stats_ref, sums):
+    pivot, first, second = sums
+    offset = jnp.sum(first, axis=0, keepdims=True) * (1.0 / ROWS)
+    squares = jnp.sum(second, axis=0, keepdims=True) - ROWS * offset * offset
+    put_stats(stats_ref, pivot + offset, jnp.maximum(squares, 0.0))
+
+
 def input_stats(place_ref, x_ref, facing_ref, outer_ref, out_ref):
     put_edges(place_ref[0], x_ref, facing_ref, outer_ref)
     acc = jnp.zeros((8, CH), F32)
@@ -129,14 +146,9 @@
     lax.fori_loop(0, count // CHUNK, step, 0)
 
 
-def conv_stats(acc, center, stats_ref):
-    mean = jnp.sum(acc, axis=0, keepdims=True) * (1.0 / ROWS)
-    put_stats(stats_ref, mean, deviations((center,), mean, MID))
-
-
 def conv_tiles(dilation, size, terms, center_ref, weights, conv_ref, stats_ref, act_ref):
     mean, factor, bias = terms
-    acc = jnp.zeros((8, MID), F32)
+    sums = None
     done = 0
     for end in range(size, ROWS + size, size):
         for r in range(end - size, end, CHUNK):
@@ -147,9 +159,9 @@
             rows = [act_ref[done + k * dilation : done + k * dilation + size, :] for k in range(3)]
             total = jnp.dot(jnp.concatenate(rows, axis=1), weights, preferred_element_type=F32)
             conv_ref[done : done + size, :] = total
-            acc = acc + fold(total)
+            sums = shifted(total, sums)
             done += size
-    conv_stats(acc, conv_ref, stats_ref)
+    put_shifted(stats_ref, sums)
 
 
 def first_conv(

time: 139 us -> 138 us (level)
  no operation moved by 1% of the time
where the time goes in v7:
time: 138 us
  blocking collectives  100 us (72%)
  starting transfers between devices  17.8 us (13%)
  Pallas kernels  13.6 us (10%)
  local copies, waits for them, and re-layouts  4.19 us (3%)
    all_to_all x4, blocking collectives, reduce_stats(): lax.all_to_all(jnp.broadcast_to(both[None], sent.shape), second, 0, 0, ti...  56.2 us
    all_to_all x3, blocking collectives, reduce_stats(): got = lax.all_to_all(sent, first, 0, 0, tiled=True)  28 us
    all_to_all x1, blocking collectives, per_device(): lax.all_to_all(out.reshape(CH // HEADS, HEADS, bins).astype(jnp.float16),...  16 us
    pallas_call x5, Pallas kernels, call(): pl.pallas_call(body, out_shape=[jax.ShapeDtypeStruct(s, d) for s, d in ou...  13.6 us
    all_to_all x1, starting transfers between devices, reduce_stats(): got = lax.all_to_all(sent, first, 0, 0, tiled=True)  7.58 us
    ppermute x2, starting transfers between devices, halos(): return (near, lax.ppermute(outer, SEQ, pairs + [(j, i) for i, j in pairs]))  7.3 us
    unnamed x18, local copies, waits for them, and re-layouts  3.03 us
    ppermute x2, starting transfers between devices, halos(): near = lax.ppermute(facing, SEQ, [(i, i ^ 1) for i in range(peers)])  2.95 us
  transfers between devices with their start and end apart: 5, of which 1 were waited for; matrix products, arithmetic and copies ran while one was open for 0% of the time, Pallas kernels for 0%

profile of v7, /device:TPU:1, one launch (start us, length us, event | category | flops | bytes accessed | tf_op | source)
XLA Modules:
  0.0 137.7 jit_solution(17293695981736808428)
XLA Ops:
  0.0 0.1 pad_add_fusion.place_ref
  0.1 1.6 %copy-done = bf16[1,2048,512]{2,1,0:T(8,128)(2,1)S(1)} copy-done((bf16[1,2048,512]{2,1,0:T(8,128)(2,1)S(1)}, bf16[1,2048,512]{2,1,0:T(8,128)(2,1)}, u32[]{:S(2)}) %copy-start) | copy-done | bytes 2097176
  1.7 2.1 %shard_map.73 = (bf16[256,512]{1,0:T(8,128)(2,1)S(1)}, bf16[256,512]{1,0:T(8,128)(2,1)S(1)}, f32[16,8,128]{2,1,0:T(8,128)}) custom-call(s32[2]{0:T(128)S(1)} %pad_add_fusion.place_ref, bf16[2048,512]{1,0:T(8,128)(2,1)S(1)} %bitcast.12), custom_call_target="tpu_custom_call" | custom-call | tf_op jit(solution)/shard_map/pallas_call | solution.py:314
  3.8 7.6 %all-to-all-start = ((f32[16,8,128]{2,1,0:T(8,128)}), f32[16,8,128]{2,1,0:T(8,128)S(1)}, u32[]{:S(2)}, u32[]{:S(2)}) async-start(f32[16,8,128]{2,1,0:T(8,128)} %get-tuple-element.22), calls=%async_computation | async-start | bytes 131072 | tf_op jit(solution)/shard_map/all_to_all | solution.py:332
  11.4 1.0 collective-permute-start
  12.4 4.9 %collective-permute-start.1 = (bf16[256,512]{1,0:T(8,128)(2,1)S(1)}, bf16[256,512]{1,0:T(8,128)(2,1)S(1)}, u32[]{:S(2)}, u32[]{:S(2)}) collective-permute-start(bf16[256,512]{1,0:T(8,128)(2,1)S(1)} %get-tuple-element.24), channel_id=1, source_target_pairs={{1,2},{3,4},{5,6},{7,8},{9,10},{11,12},{13,14},{15,16},{17,18},{19... | collective-permute-start | bytes 786440 | tf_op jit(solution)/shard_map/ppermute | solution.py:328
  17.3 0.8 all-to-all-done
  18.2 0.0 copy-start.7
  18.2 0.0 copy-start.8
  18.2 18.2 %all_to_all.45.got_ref = f32[16,8,128]{2,1,0:T(8,128)S(1)} all-to-all(f32[16,8,128]{2,1,0:T(8,128)S(1)} %broadcast_in_dim.8), channel_id=1, replica_groups=mesh['y_lo'=2,'x'=4,'z'=8,'y_hi'=2,'core'=2] {'z','core'}, dimensions={0} | all-to-all | bytes 131072 | tf_op jit(solution)/shard_map/all_to_all | solution.py:342
  36.4 0.0 collective-permute-done.near_ref
  36.4 0.0 collective-permute-done.1.cross_ref
  36.5 0.0 copy-start.2
  36.5 1.4 %copy-done.2 = bf16[2,3,512,256]{3,2,1,0:T(8,128)(2,1)S(1)} copy-done((bf16[2,3,512,256]{3,2,1,0:T(8,128)(2,1)S(1)}, bf16[2,3,512,256]{3,2,1,0:T(8,128)(2,1)}, u32[]{:S(2)}) %copy-start.2) | copy-done | bytes 1572888
  37.9 3.1 %shard_map.74 = (f32[2048,256]{1,0:T(8,128)S(1)}, f32[16,4,128]{2,1,0:T(4,128)S(1)}) custom-call(s32[2]{0:T(128)S(1)} %pad_add_fusion.place_ref, f32[16,8,128]{2,1,0:T(8,128)S(1)} %all_to_all.45.got_ref, f32[2,512]{1,0:T(2,128)S(1)} %copy-done.5, f32[2,512]{1,0:T(2,128)S(1)} %copy-done.6, bf16[2,3,512,256]{3,2,1,0:T(8,128)(2,1)S(1)} %copy-done.2, ...), custom_call_target="tpu_custom_call" | custom-call | tf_op jit(solution)/shard_map/pallas_call | solution.py:314
  41.0 9.3 %all_to_all.46 = f32[16,4,128]{2,1,0:T(4,128)S(1)} all-to-all(f32[16,4,128]{2,1,0:T(4,128)S(1)} %get-tuple-element.25), channel_id=1, replica_groups=mesh['y_lo'=2,'x'=4,'z'=8,'y_hi'=2,'core'=2] {'y_lo','x','y_hi'}, dimensions={0} | all-to-all | bytes 65536 | tf_op jit(solution)/shard_map/all_to_all | solution.py:332
  50.4 11.5 %all_to_all.47.got_ref = f32[16,4,128]{2,1,0:T(4,128)S(1)} all-to-all(f32[16,4,128]{2,1,0:T(4,128)S(1)} %broadcast_in_dim.9), channel_id=1, replica_groups=mesh['y_lo'=2,'x'=4,'z'=8,'y_hi'=2,'core'=2] {'z','core'}, dimensions={0} | all-to-all | bytes 65536 | tf_op jit(solution)/shard_map/all_to_all | solution.py:342
  61.9 0.0 copy-start.3
  61.9 3.1 %shard_map.75 = (f32[2048,512]{1,0:T(8,128)S(1)}, bf16[512,512]{1,0:T(8,128)(2,1)S(1)}, bf16[512,512]{1,0:T(8,128)(2,1)S(1)}, f32[16,8,128]{2,1,0:T(8,128)S(1)}, f32[256,512]{1,0:T(8,128)S(1)}) custom-call(s32[2]{0:T(128)S(1)} %pad_add_fusion.place_ref, f32[16,4,128]{2,1,0:T(4,128)S(1)} %all_to_all.47.got_ref, f32[2,256]{1,0:T(2,128)S(1)} %copy-done.7, ...), custom_call_target="tpu_custom_call" | custom-call | tf_op jit(solution)/shard_map/pallas_call | solution.py:314
  65.1 9.4 %all_to_all.48 = f32[16,8,128]{2,1,0:T(8,128)S(1)} all-to-all(f32[16,8,128]{2,1,0:T(8,128)S(1)} %get-tuple-element.27), channel_id=1, replica_groups=mesh['y_lo'=2,'x'=4,'z'=8,'y_hi'=2,'core'=2] {'y_lo','x','y_hi'}, dimensions={0} | all-to-all | bytes 131072 | tf_op jit(solution)/shard_map/all_to_all | solution.py:332
  74.6 1.9 %collective-permute-start.2 = (bf16[512,512]{1,0:T(8,128)(2,1)S(1)}, bf16[512,512]{1,0:T(8,128)(2,1)S(1)}, u32[]{:S(2)}, u32[]{:S(2)}) collective-permute-start(bf16[512,512]{1,0:T(8,128)(2,1)S(1)} %get-tuple-element.31), channel_id=1, source_target_pairs={{0,1},{1,0},{2,3},{3,2},{4,5},{5,4},{6,7},{7,6},{8,9},{9,8},{10,11... | collective-permute-start | bytes 1572872 | tf_op jit(solution)/shard_map/ppermute | solution.py:326
  76.5 2.4 %collective-permute-start.3 = (bf16[512,512]{1,0:T(8,128)(2,1)S(1)}, bf16[512,512]{1,0:T(8,128)(2,1)S(1)}, u32[]{:S(2)}, u32[]{:S(2)}) collective-permute-start(bf16[512,512]{1,0:T(8,128)(2,1)S(1)} %get-tuple-element.33), channel_id=1, source_target_pairs={{1,2},{3,4},{5,6},{7,8},{9,10},{11,12},{13,14},{15,16},{17,18},{19... | collective-permute-start | bytes 1572872 | tf_op jit(solution)/shard_map/ppermute | solution.py:328
  78.9 12.1 %all_to_all.49.got_ref.stream_got_ref = f32[16,8,128]{2,1,0:T(8,128)S(1)} all-to-all(f32[16,8,128]{2,1,0:T(8,128)S(1)} %broadcast_in_dim.10), channel_id=1, replica_groups=mesh['y_lo'=2,'x'=4,'z'=8,'y_hi'=2,'core'=2] {'z','core'}, dimensions={0} | all-to-all | bytes 131072 | tf_op jit(solution)/shard_map/all_to_all | solution.py:342
  91.1 0.0 collective-permute-done.2.near_packed_ref
  91.1 4.1 %shard_map.76 = (f32[2048,256]{1,0:T(8,128)S(1)}, f32[16,4,128]{2,1,0:T(4,128)S(1)}) custom-call(s32[2]{0:T(128)S(1)} %pad_add_fusion.place_ref, f32[16,8,128]{2,1,0:T(8,128)S(1)} %all_to_all.49.got_ref.stream_got_ref, f32[2,512]{1,0:T(2,128)S(1)} %copy-done.5, f32[2,512]{1,0:T(2,128)S(1)} %copy-done.6, bf16[2,3,512,256]{3,2,1,0:T(8,128)(2,1)S(1)} %copy-done.3, ...), custom_call_target="tpu_custom_call" | custom-call | tf_op jit(solution)/shard_map/pallas_call | solution.py:314
  95.1 9.2 %all_to_all.50 = f32[16,4,128]{2,1,0:T(4,128)S(1)} all-to-all(f32[16,4,128]{2,1,0:T(4,128)S(1)} %get-tuple-element.34), channel_id=1, replica_groups=mesh['y_lo'=2,'x'=4,'z'=8,'y_hi'=2,'core'=2] {'y_lo','x','y_hi'}, dimensions={0} | all-to-all | bytes 65536 | tf_op jit(solution)/shard_map/all_to_all | solution.py:332
  104.5 14.4 %all_to_all.51.got_ref = f32[16,4,128]{2,1,0:T(4,128)S(1)} all-to-all(f32[16,4,128]{2,1,0:T(4,128)S(1)} %broadcast_in_dim.11), channel_id=1, replica_groups=mesh['y_lo'=2,'x'=4,'z'=8,'y_hi'=2,'core'=2] {'z','core'}, dimensions={0} | all-to-all | bytes 65536 | tf_op jit(solution)/shard_map/all_to_all | solution.py:342
  118.9 1.2 shard_map.77
  120.1 16.0 %all_to_all.52 = f16[64,8,256]{2,1,0:T(8,128)(2,1)S(1)} all-to-all(f16[64,8,256]{2,1,0:T(8,128)(2,1)S(1)} %convert_bitcast_fusion), channel_id=1, replica_groups=mesh['y_lo'=2,'x'=4,'z'=8,'y_hi'=2,'core'=2] {'z','y_hi','core'}, dimensions={0} | all-to-all | bytes 524288 | tf_op jit(solution)/shard_map/all_to_all | solution.py:404
  136.1 0.1 convert.2
  136.2 0.3 fusion
  136.5 1.1 reshape.35
  (38 shorter events, 0.4 us)
Async XLA Ops:
  0.0 36.4 %copy-start.6 = (f32[2,512]{1,0:T(2,128)S(1)}, f32[2,512]{1,0:T(2,128)}, u32[]{:S(2)}) copy-start(f32[2,512]{1,0:T(2,128)} %bias_ref.6) | copy-start | bytes 12292
  0.0 36.4 %copy-start.5 = (f32[2,512]{1,0:T(2,128)S(1)}, f32[2,512]{1,0:T(2,128)}, u32[]{:S(2)}) copy-start(f32[2,512]{1,0:T(2,128)} %gain_ref.6) | copy-start | bytes 12292
  0.1 1.6 %copy-start = (bf16[1,2048,512]{2,1,0:T(8,128)(2,1)S(1)}, bf16[1,2048,512]{2,1,0:T(8,128)(2,1)}, u32[]{:S(2)}) copy-start(bf16[1,2048,512]{2,1,0:T(8,128)(2,1)} %param.7) | copy-start | bytes 6291460
  1.7 34.8 %copy-start.1 = (bf16[1,2048,512]{2,1,0:T(8,128)(2,1)S(1)}, bf16[1,2048,512]{2,1,0:T(8,128)(2,1)}, u32[]{:S(2)}) copy-start(bf16[1,2048,512]{2,1,0:T(8,128)(2,1)} %param.7) | copy-start | bytes 6291460
  3.8 14.3 %all-to-all-start = ((f32[16,8,128]{2,1,0:T(8,128)}), f32[16,8,128]{2,1,0:T(8,128)S(1)}, u32[]{:S(2)}, u32[]{:S(2)}) async-start(f32[16,8,128]{2,1,0:T(8,128)} %get-tuple-element.22), calls=%async_computation | async-start | bytes 131072 | tf_op jit(solution)/shard_map/all_to_all | solution.py:332
  11.4 25.0 %collective-permute-start = (bf16[256,512]{1,0:T(8,128)(2,1)S(1)}, bf16[256,512]{1,0:T(8,128)(2,1)S(1)}, u32[]{:S(2)}, u32[]{:S(2)}) collective-permute-start(bf16[256,512]{1,0:T(8,128)(2,1)S(1)} %get-tuple-element.23), channel_id=1, source_target_pairs={{0,1},{1,0},{2,3},{3,2},{4,5},{5,4},{6,7},{7,6},{8,9},{9,8},{10,11... | collective-permute-start | bytes 786440 | tf_op jit(solution)/shard_map/ppermute | solution.py:326
  12.4 24.0 %collective-permute-start.1 = (bf16[256,512]{1,0:T(8,128)(2,1)S(1)}, bf16[256,512]{1,0:T(8,128)(2,1)S(1)}, u32[]{:S(2)}, u32[]{:S(2)}) collective-permute-start(bf16[256,512]{1,0:T(8,128)(2,1)S(1)} %get-tuple-element.24), channel_id=1, source_target_pairs={{1,2},{3,4},{5,6},{7,8},{9,10},{11,12},{13,14},{15,16},{17,18},{19... | collective-permute-start | bytes 786440 | tf_op jit(solution)/shard_map/ppermute | solution.py:328
  18.2 43.7 %copy-start.7 = (f32[2,256]{1,0:T(2,128)S(1)}, f32[2,256]{1,0:T(2,128)}, u32[]{:S(2)}) copy-start(f32[2,256]{1,0:T(2,128)} %gain_ref.7) | copy-start | bytes 6148
  18.2 43.7 %copy-start.8 = (f32[2,256]{1,0:T(2,128)S(1)}, f32[2,256]{1,0:T(2,128)}, u32[]{:S(2)}) copy-start(f32[2,256]{1,0:T(2,128)} %bias_ref.7) | copy-start | bytes 6148
  36.5 1.4 %copy-start.2 = (bf16[2,3,512,256]{3,2,1,0:T(8,128)(2,1)S(1)}, bf16[2,3,512,256]{3,2,1,0:T(8,128)(2,1)}, u32[]{:S(2)}) copy-start(bf16[2,3,512,256]{3,2,1,0:T(8,128)(2,1)} %taps_ref.3) | copy-start | bytes 4718596
  37.9 24.0 %copy-start.4 = (bf16[2,256,512]{2,1,0:T(8,128)(2,1)S(1)}, bf16[2,256,512]{2,1,0:T(8,128)(2,1)}, u32[]{:S(2)}) copy-start(bf16[2,256,512]{2,1,0:T(8,128)(2,1)} %point_ref.5) | copy-start | bytes 1572868
  61.9 29.2 %copy-start.3 = (bf16[2,3,512,256]{3,2,1,0:T(8,128)(2,1)S(1)}, bf16[2,3,512,256]{3,2,1,0:T(8,128)(2,1)}, u32[]{:S(2)}) copy-start(bf16[2,3,512,256]{3,2,1,0:T(8,128)(2,1)} %taps_ref.3) | copy-start | bytes 4718596
  74.6 16.5 %collective-permute-start.2 = (bf16[512,512]{1,0:T(8,128)(2,1)S(1)}, bf16[512,512]{1,0:T(8,128)(2,1)S(1)}, u32[]{:S(2)}, u32[]{:S(2)}) collective-permute-start(bf16[512,512]{1,0:T(8,128)(2,1)S(1)} %get-tuple-element.31), channel_id=1, source_target_pairs={{0,1},{1,0},{2,3},{3,2},{4,5},{5,4},{6,7},{7,6},{8,9},{9,8},{10,11... | collective-permute-start | bytes 1572872 | tf_op jit(solution)/shard_map/ppermute | solution.py:326
  76.5 14.6 %collective-permute-start.3 = (bf16[512,512]{1,0:T(8,128)(2,1)S(1)}, bf16[512,512]{1,0:T(8,128)(2,1)S(1)}, u32[]{:S(2)}, u32[]{:S(2)}) collective-permute-start(bf16[512,512]{1,0:T(8,128)(2,1)S(1)} %get-tuple-element.33), channel_id=1, source_target_pairs={{1,2},{3,4},{5,6},{7,8},{9,10},{11,12},{13,14},{15,16},{17,18},{19... | collective-permute-start | bytes 1572872 | tf_op jit(solution)/shard_map/ppermute | solution.py:328

commit v8 on v7

--- a/solution.py
+++ b/solution.py
@@ -389,7 +389,7 @@
         ],
         1,
     )
-    (got,) = reduce_stats(stats, ACROSS, ALONG)
+    (got,) = reduce_stats(stats, ALONG, ACROSS)
     out, bound = call(
         pool_kernel,
         (got, stream_got, mid_gain, mid_bias, point, conv, pooled),

time: 138 us -> 138 us (level)
    all_to_all x4, blocking collectives: 56.2 us -> 51.6 us  [reduce_stats(): lax.all_to_all(jnp.broadcast_to(both[None], sent.shape), second, 0, 0, ti...]
    all_to_all x3, blocking collectives: 28 us -> 31.1 us  [reduce_stats(): got = lax.all_to_all(sent, first, 0, 0, tiled=True)]
    all_to_all x1, blocking collectives: 16 us -> 17.4 us  [per_device(): lax.all_to_all(out.reshape(CH // HEADS, HEADS, bins).astype(jnp.float16),...]
where the time goes in v8:
time: 138 us
  blocking collectives  100 us (72%)
  starting transfers between devices  17.8 us (13%)
  Pallas kernels  13.6 us (10%)
  local copies, waits for them, and re-layouts  4.19 us (3%)
    all_to_all x4, blocking collectives, reduce_stats(): lax.all_to_all(jnp.broadcast_to(both[None], sent.shape), second, 0, 0, ti...  51.6 us
    all_to_all x3, blocking collectives, reduce_stats(): got = lax.all_to_all(sent, first, 0, 0, tiled=True)  31.1 us
    all_to_all x1, blocking collectives, per_device(): lax.all_to_all(out.reshape(CH // HEADS, HEADS, bins).astype(jnp.float16),...  17.4 us
    pallas_call x5, Pallas kernels, call(): pl.pallas_call(body, out_shape=[jax.ShapeDtypeStruct(s, d) for s, d in ou...  13.6 us
    all_to_all x1, starting transfers between devices, reduce_stats(): got = lax.all_to_all(sent, first, 0, 0, tiled=True)  7.58 us
    ppermute x2, starting transfers between devices, halos(): return (near, lax.ppermute(outer, SEQ, pairs + [(j, i) for i, j in pairs]))  7.3 us
    unnamed x18, local copies, waits for them, and re-layouts  3.03 us
    ppermute x2, starting transfers between devices, halos(): near = lax.ppermute(facing, SEQ, [(i, i ^ 1) for i in range(peers)])  2.95 us
  transfers between devices with their start and end apart: 5, of which 1 were waited for; matrix products, arithmetic and copies ran while one was open for 0% of the time, Pallas kernels for 0%

profile of v8, /device:TPU:1, one launch (start us, length us, event | category | flops | bytes accessed | tf_op | source)
XLA Modules:
  0.0 137.7 jit_solution(2877622216553038769)
XLA Ops:
  0.0 0.1 pad_add_fusion.place_ref
  0.1 1.6 %copy-done = bf16[1,2048,512]{2,1,0:T(8,128)(2,1)S(1)} copy-done((bf16[1,2048,512]{2,1,0:T(8,128)(2,1)S(1)}, bf16[1,2048,512]{2,1,0:T(8,128)(2,1)}, u32[]{:S(2)}) %copy-start) | copy-done | bytes 2097176
  1.7 2.1 %shard_map.73 = (bf16[256,512]{1,0:T(8,128)(2,1)S(1)}, bf16[256,512]{1,0:T(8,128)(2,1)S(1)}, f32[16,8,128]{2,1,0:T(8,128)}) custom-call(s32[2]{0:T(128)S(1)} %pad_add_fusion.place_ref, bf16[2048,512]{1,0:T(8,128)(2,1)S(1)} %bitcast.12), custom_call_target="tpu_custom_call" | custom-call | tf_op jit(solution)/shard_map/pallas_call | solution.py:314
  3.8 7.6 %all-to-all-start = ((f32[16,8,128]{2,1,0:T(8,128)}), f32[16,8,128]{2,1,0:T(8,128)S(1)}, u32[]{:S(2)}, u32[]{:S(2)}) async-start(f32[16,8,128]{2,1,0:T(8,128)} %get-tuple-element.22), calls=%async_computation | async-start | bytes 131072 | tf_op jit(solution)/shard_map/all_to_all | solution.py:332
  11.4 1.0 collective-permute-start
  12.4 4.9 %collective-permute-start.1 = (bf16[256,512]{1,0:T(8,128)(2,1)S(1)}, bf16[256,512]{1,0:T(8,128)(2,1)S(1)}, u32[]{:S(2)}, u32[]{:S(2)}) collective-permute-start(bf16[256,512]{1,0:T(8,128)(2,1)S(1)} %get-tuple-element.24), channel_id=1, source_target_pairs={{1,2},{3,4},{5,6},{7,8},{9,10},{11,12},{13,14},{15,16},{17,18},{19... | collective-permute-start | bytes 786440 | tf_op jit(solution)/shard_map/ppermute | solution.py:328
  17.3 0.8 all-to-all-done
  18.2 0.0 copy-start.7
  18.2 0.0 copy-start.8
  18.2 18.2 %all_to_all.45.got_ref = f32[16,8,128]{2,1,0:T(8,128)S(1)} all-to-all(f32[16,8,128]{2,1,0:T(8,128)S(1)} %broadcast_in_dim.8), channel_id=1, replica_groups=mesh['y_lo'=2,'x'=4,'z'=8,'y_hi'=2,'core'=2] {'z','core'}, dimensions={0} | all-to-all | bytes 131072 | tf_op jit(solution)/shard_map/all_to_all | solution.py:342
  36.4 0.0 collective-permute-done.near_ref
  36.4 0.0 collective-permute-done.1.cross_ref
  36.5 0.0 copy-start.2
  36.5 1.4 %copy-done.2 = bf16[2,3,512,256]{3,2,1,0:T(8,128)(2,1)S(1)} copy-done((bf16[2,3,512,256]{3,2,1,0:T(8,128)(2,1)S(1)}, bf16[2,3,512,256]{3,2,1,0:T(8,128)(2,1)}, u32[]{:S(2)}) %copy-start.2) | copy-done | bytes 1572888
  37.9 3.1 %shard_map.74 = (f32[2048,256]{1,0:T(8,128)S(1)}, f32[16,4,128]{2,1,0:T(4,128)S(1)}) custom-call(s32[2]{0:T(128)S(1)} %pad_add_fusion.place_ref, f32[16,8,128]{2,1,0:T(8,128)S(1)} %all_to_all.45.got_ref, f32[2,512]{1,0:T(2,128)S(1)} %copy-done.5, f32[2,512]{1,0:T(2,128)S(1)} %copy-done.6, bf16[2,3,512,256]{3,2,1,0:T(8,128)(2,1)S(1)} %copy-done.2, ...), custom_call_target="tpu_custom_call" | custom-call | tf_op jit(solution)/shard_map/pallas_call | solution.py:314
  41.0 9.3 %all_to_all.46 = f32[16,4,128]{2,1,0:T(4,128)S(1)} all-to-all(f32[16,4,128]{2,1,0:T(4,128)S(1)} %get-tuple-element.25), channel_id=1, replica_groups=mesh['y_lo'=2,'x'=4,'z'=8,'y_hi'=2,'core'=2] {'y_lo','x','y_hi'}, dimensions={0} | all-to-all | bytes 65536 | tf_op jit(solution)/shard_map/all_to_all | solution.py:332
  50.4 11.5 %all_to_all.47.got_ref = f32[16,4,128]{2,1,0:T(4,128)S(1)} all-to-all(f32[16,4,128]{2,1,0:T(4,128)S(1)} %broadcast_in_dim.9), channel_id=1, replica_groups=mesh['y_lo'=2,'x'=4,'z'=8,'y_hi'=2,'core'=2] {'z','core'}, dimensions={0} | all-to-all | bytes 65536 | tf_op jit(solution)/shard_map/all_to_all | solution.py:342
  61.9 0.0 copy-start.3
  61.9 3.1 %shard_map.75 = (f32[2048,512]{1,0:T(8,128)S(1)}, bf16[512,512]{1,0:T(8,128)(2,1)S(1)}, bf16[512,512]{1,0:T(8,128)(2,1)S(1)}, f32[16,8,128]{2,1,0:T(8,128)S(1)}, f32[256,512]{1,0:T(8,128)S(1)}) custom-call(s32[2]{0:T(128)S(1)} %pad_add_fusion.place_ref, f32[16,4,128]{2,1,0:T(4,128)S(1)} %all_to_all.47.got_ref, f32[2,256]{1,0:T(2,128)S(1)} %copy-done.7, ...), custom_call_target="tpu_custom_call" | custom-call | tf_op jit(solution)/shard_map/pallas_call | solution.py:314
  65.1 9.4 %all_to_all.48 = f32[16,8,128]{2,1,0:T(8,128)S(1)} all-to-all(f32[16,8,128]{2,1,0:T(8,128)S(1)} %get-tuple-element.27), channel_id=1, replica_groups=mesh['y_lo'=2,'x'=4,'z'=8,'y_hi'=2,'core'=2] {'y_lo','x','y_hi'}, dimensions={0} | all-to-all | bytes 131072 | tf_op jit(solution)/shard_map/all_to_all | solution.py:332
  74.6 1.9 %collective-permute-start.2 = (bf16[512,512]{1,0:T(8,128)(2,1)S(1)}, bf16[512,512]{1,0:T(8,128)(2,1)S(1)}, u32[]{:S(2)}, u32[]{:S(2)}) collective-permute-start(bf16[512,512]{1,0:T(8,128)(2,1)S(1)} %get-tuple-element.31), channel_id=1, source_target_pairs={{0,1},{1,0},{2,3},{3,2},{4,5},{5,4},{6,7},{7,6},{8,9},{9,8},{10,11... | collective-permute-start | bytes 1572872 | tf_op jit(solution)/shard_map/ppermute | solution.py:326
  76.5 2.4 %collective-permute-start.3 = (bf16[512,512]{1,0:T(8,128)(2,1)S(1)}, bf16[512,512]{1,0:T(8,128)(2,1)S(1)}, u32[]{:S(2)}, u32[]{:S(2)}) collective-permute-start(bf16[512,512]{1,0:T(8,128)(2,1)S(1)} %get-tuple-element.33), channel_id=1, source_target_pairs={{1,2},{3,4},{5,6},{7,8},{9,10},{11,12},{13,14},{15,16},{17,18},{19... | collective-permute-start | bytes 1572872 | tf_op jit(solution)/shard_map/ppermute | solution.py:328
  78.9 12.1 %all_to_all.49.got_ref.stream_got_ref = f32[16,8,128]{2,1,0:T(8,128)S(1)} all-to-all(f32[16,8,128]{2,1,0:T(8,128)S(1)} %broadcast_in_dim.10), channel_id=1, replica_groups=mesh['y_lo'=2,'x'=4,'z'=8,'y_hi'=2,'core'=2] {'z','core'}, dimensions={0} | all-to-all | bytes 131072 | tf_op jit(solution)/shard_map/all_to_all | solution.py:342
  91.1 0.0 collective-permute-done.2.near_packed_ref
  91.1 4.1 %shard_map.76 = (f32[2048,256]{1,0:T(8,128)S(1)}, f32[16,4,128]{2,1,0:T(4,128)S(1)}) custom-call(s32[2]{0:T(128)S(1)} %pad_add_fusion.place_ref, f32[16,8,128]{2,1,0:T(8,128)S(1)} %all_to_all.49.got_ref.stream_got_ref, f32[2,512]{1,0:T(2,128)S(1)} %copy-done.5, f32[2,512]{1,0:T(2,128)S(1)} %copy-done.6, bf16[2,3,512,256]{3,2,1,0:T(8,128)(2,1)S(1)} %copy-done.3, ...), custom_call_target="tpu_custom_call" | custom-call | tf_op jit(solution)/shard_map/pallas_call | solution.py:314
  95.1 12.4 %all_to_all.50 = f32[16,4,128]{2,1,0:T(4,128)S(1)} all-to-all(f32[16,4,128]{2,1,0:T(4,128)S(1)} %get-tuple-element.34), channel_id=1, replica_groups=mesh['y_lo'=2,'x'=4,'z'=8,'y_hi'=2,'core'=2] {'z','core'}, dimensions={0} | all-to-all | bytes 65536 | tf_op jit(solution)/shard_map/all_to_all | solution.py:332
  107.6 9.9 %all_to_all.51.got_ref = f32[16,4,128]{2,1,0:T(4,128)S(1)} all-to-all(f32[16,4,128]{2,1,0:T(4,128)S(1)} %broadcast_in_dim.11), channel_id=1, replica_groups=mesh['y_lo'=2,'x'=4,'z'=8,'y_hi'=2,'core'=2] {'y_lo','x','y_hi'}, dimensions={0} | all-to-all | bytes 65536 | tf_op jit(solution)/shard_map/all_to_all | solution.py:342
  117.5 1.2 shard_map.77
  118.7 17.4 %all_to_all.52 = f16[64,8,256]{2,1,0:T(8,128)(2,1)S(1)} all-to-all(f16[64,8,256]{2,1,0:T(8,128)(2,1)S(1)} %convert_bitcast_fusion), channel_id=1, replica_groups=mesh['y_lo'=2,'x'=4,'z'=8,'y_hi'=2,'core'=2] {'z','y_hi','core'}, dimensions={0} | all-to-all | bytes 524288 | tf_op jit(solution)/shard_map/all_to_all | solution.py:404
  136.1 0.1 convert.2
  136.2 0.3 fusion
  136.5 1.1 reshape.35
  (38 shorter events, 0.4 us)
Async XLA Ops:
  0.0 36.4 %copy-start.6 = (f32[2,512]{1,0:T(2,128)S(1)}, f32[2,512]{1,0:T(2,128)}, u32[]{:S(2)}) copy-start(f32[2,512]{1,0:T(2,128)} %bias_ref.6) | copy-start | bytes 12292
  0.0 36.4 %copy-start.5 = (f32[2,512]{1,0:T(2,128)S(1)}, f32[2,512]{1,0:T(2,128)}, u32[]{:S(2)}) copy-start(f32[2,512]{1,0:T(2,128)} %gain_ref.6) | copy-start | bytes 12292
  0.1 1.6 %copy-start = (bf16[1,2048,512]{2,1,0:T(8,128)(2,1)S(1)}, bf16[1,2048,512]{2,1,0:T(8,128)(2,1)}, u32[]{:S(2)}) copy-start(bf16[1,2048,512]{2,1,0:T(8,128)(2,1)} %param.7) | copy-start | bytes 6291460
  1.7 34.8 %copy-start.1 = (bf16[1,2048,512]{2,1,0:T(8,128)(2,1)S(1)}, bf16[1,2048,512]{2,1,0:T(8,128)(2,1)}, u32[]{:S(2)}) copy-start(bf16[1,2048,512]{2,1,0:T(8,128)(2,1)} %param.7) | copy-start | bytes 6291460
  3.8 14.3 %all-to-all-start = ((f32[16,8,128]{2,1,0:T(8,128)}), f32[16,8,128]{2,1,0:T(8,128)S(1)}, u32[]{:S(2)}, u32[]{:S(2)}) async-start(f32[16,8,128]{2,1,0:T(8,128)} %get-tuple-element.22), calls=%async_computation | async-start | bytes 131072 | tf_op jit(solution)/shard_map/all_to_all | solution.py:332
  11.4 25.0 %collective-permute-start = (bf16[256,512]{1,0:T(8,128)(2,1)S(1)}, bf16[256,512]{1,0:T(8,128)(2,1)S(1)}, u32[]{:S(2)}, u32[]{:S(2)}) collective-permute-start(bf16[256,512]{1,0:T(8,128)(2,1)S(1)} %get-tuple-element.23), channel_id=1, source_target_pairs={{0,1},{1,0},{2,3},{3,2},{4,5},{5,4},{6,7},{7,6},{8,9},{9,8},{10,11... | collective-permute-start | bytes 786440 | tf_op jit(solution)/shard_map/ppermute | solution.py:326
  12.4 24.0 %collective-permute-start.1 = (bf16[256,512]{1,0:T(8,128)(2,1)S(1)}, bf16[256,512]{1,0:T(8,128)(2,1)S(1)}, u32[]{:S(2)}, u32[]{:S(2)}) collective-permute-start(bf16[256,512]{1,0:T(8,128)(2,1)S(1)} %get-tuple-element.24), channel_id=1, source_target_pairs={{1,2},{3,4},{5,6},{7,8},{9,10},{11,12},{13,14},{15,16},{17,18},{19... | collective-permute-start | bytes 786440 | tf_op jit(solution)/shard_map/ppermute | solution.py:328
  18.2 43.7 %copy-start.7 = (f32[2,256]{1,0:T(2,128)S(1)}, f32[2,256]{1,0:T(2,128)}, u32[]{:S(2)}) copy-start(f32[2,256]{1,0:T(2,128)} %gain_ref.7) | copy-start | bytes 6148
  18.2 43.7 %copy-start.8 = (f32[2,256]{1,0:T(2,128)S(1)}, f32[2,256]{1,0:T(2,128)}, u32[]{:S(2)}) copy-start(f32[2,256]{1,0:T(2,128)} %bias_ref.7) | copy-start | bytes 6148
  36.5 1.4 %copy-start.2 = (bf16[2,3,512,256]{3,2,1,0:T(8,128)(2,1)S(1)}, bf16[2,3,512,256]{3,2,1,0:T(8,128)(2,1)}, u32[]{:S(2)}) copy-start(bf16[2,3,512,256]{3,2,1,0:T(8,128)(2,1)} %taps_ref.3) | copy-start | bytes 4718596
  37.9 24.0 %copy-start.4 = (bf16[2,256,512]{2,1,0:T(8,128)(2,1)S(1)}, bf16[2,256,512]{2,1,0:T(8,128)(2,1)}, u32[]{:S(2)}) copy-start(bf16[2,256,512]{2,1,0:T(8,128)(2,1)} %point_ref.5) | copy-start | bytes 1572868
  61.9 29.2 %copy-start.3 = (bf16[2,3,512,256]{3,2,1,0:T(8,128)(2,1)S(1)}, bf16[2,3,512,256]{3,2,1,0:T(8,128)(2,1)}, u32[]{:S(2)}) copy-start(bf16[2,3,512,256]{3,2,1,0:T(8,128)(2,1)} %taps_ref.3) | copy-start | bytes 4718596
  74.6 16.5 %collective-permute-start.2 = (bf16[512,512]{1,0:T(8,128)(2,1)S(1)}, bf16[512,512]{1,0:T(8,128)(2,1)S(1)}, u32[]{:S(2)}, u32[]{:S(2)}) collective-permute-start(bf16[512,512]{1,0:T(8,128)(2,1)S(1)} %get-tuple-element.31), channel_id=1, source_target_pairs={{0,1},{1,0},{2,3},{3,2},{4,5},{5,4},{6,7},{7,6},{8,9},{9,8},{10,11... | collective-permute-start | bytes 1572872 | tf_op jit(solution)/shard_map/ppermute | solution.py:326
  76.5 14.6 %collective-permute-start.3 = (bf16[512,512]{1,0:T(8,128)(2,1)S(1)}, bf16[512,512]{1,0:T(8,128)(2,1)S(1)}, u32[]{:S(2)}, u32[]{:S(2)}) collective-permute-start(bf16[512,512]{1,0:T(8,128)(2,1)S(1)} %get-tuple-element.33), channel_id=1, source_target_pairs={{1,2},{3,4},{5,6},{7,8},{9,10},{11,12},{13,14},{15,16},{17,18},{19... | collective-permute-start | bytes 1572872 | tf_op jit(solution)/shard_map/ppermute | solution.py:328
